TPU v7x, 32 devices: a whole 2x2x4 slice. The times are simulated.
32 devices in a mesh: seq: 8 (over z, x), fsdp: 4 (over y, core).
Axes of the slice: x: 2, y: 2, z: 4, core: 2. Of those that a mesh axis runs over, the one named last changes fastest.
Arguments:
- hidden: bfloat16 [4, 1024, 1024], P('fsdp', 'seq'), may hold values from -6 to 6
- cluster_lengths: int32 [4, 8], P('fsdp'), may hold values from 1 to 1024, as said below
- norm_gain: bfloat16 [1024], P('fsdp'), may hold values from 0.5 to 1.5
- in_weight: bfloat16 [1024, 4096], P('fsdp'), may hold values from -0.1875 to 0.1875
- conv_weight: bfloat16 [2048, 4], P('fsdp'), may hold values from -3 to 3
- conv_bias: bfloat16 [2048], P('fsdp'), may hold values from -0.5 to 0.5
- xproj_weight: bfloat16 [2048, 96], P('fsdp'), may hold values from -0.125 to 0.125
- dt_weight: bfloat16 [2048, 64], P('fsdp'), may hold values from -0.75 to 0.75
- dt_bias: bfloat16 [2048], P('fsdp'), may hold values from -1 to 0.5
- a_log: bfloat16 [2048, 16], P('fsdp'), may hold values from -3.5 to 0.5
- skip: bfloat16 [2048], P('fsdp'), may hold values from 0.5 to 1.5
- out_weight: bfloat16 [2048, 1024], P('fsdp'), may hold values from -0.125 to 0.125
- cotangent: bfloat16 [4, 1024, 1024], P('fsdp', 'seq'), may hold values from -6 to 6
Outputs:
- output: bfloat16 [4, 1024, 1024], P('fsdp', 'seq')
- grad_hidden: float32 [4, 1024, 1024], P('fsdp', 'seq')
- grad_norm_gain: float32 [1024], P(('seq', 'fsdp'))
- grad_in_weight: float32 [1024, 4096], P(('seq', 'fsdp'))
- grad_conv_weight: float32 [2048, 4], P(('seq', 'fsdp'))
- grad_conv_bias: float32 [2048], P(('seq', 'fsdp'))
- grad_xproj_weight: float32 [2048, 96], P(('seq', 'fsdp'))
- grad_dt_weight: float32 [2048, 64], P(('seq', 'fsdp'))
- grad_dt_bias: float32 [2048], P(('seq', 'fsdp'))
- grad_a_log: float32 [2048, 16], P(('seq', 'fsdp'))
- grad_skip: float32 [2048], P(('seq', 'fsdp'))
- grad_out_weight: float32 [2048, 1024], P(('seq', 'fsdp'))
Inputs may be any that keep to these rules, and one draw needn't show every extreme that they name: `cluster_lengths`: each row gives the 8 cluster lengths of one stream in order, summing to 1024; in every row one cluster, neither the first nor the last, starts within the first 128 tokens and ends within the last 128 tokens.
All inputs are finite; a program needn't handle non-finite values.
Results may differ from a plain program's by a relative error of at most 0.012.
Values may be sent and summed in bfloat16 or wider, within the bound.
A program may use at most 192 MiB of HBM per device.

v0:
```python
from functools import partial

import jax
import jax.numpy as jnp
from jax import lax
from jax.sharding import PartitionSpec as P

BLOCK = 64


EPS = 1e-05


def shifted(value, axis, steps):
    count = lax.axis_size(axis)
    first, last = (max(0, -steps), min(count, count - steps))
    return lax.ppermute(value, axis, [(source, source + steps) for source in range(first, last)])


def prefix(x, axis, join, neutral):
    place = lax.axis_index(axis)
    gathered = jax.tree.map(
        lambda a, kind: lax.all_gather(a.astype(kind), axis), x, (jnp.bfloat16, jnp.bfloat16)
    )
    state = jax.tree.map(lambda a, e: jnp.zeros_like(a) + jnp.asarray(e, a.dtype), x, neutral)

    def prefix_one(hop, state):
        return join(
            state,
            jax.tree.map(
                lambda a, own: lax.dynamic_index_in_dim(a, hop, 0, False).astype(own.dtype),
                gathered,
                x,
            ),
        )

    return lax.fori_loop(0, place, prefix_one, state)


def carried_in(part, axis, combine, identity):
    count = lax.axis_size(axis)
    place = lax.axis_index(axis)
    ahead = count - 1 - place
    gathered = jax.tree.map(lambda a: lax.all_gather(a, axis), part)
    state = jax.tree.map(lambda a, e: jnp.zeros_like(a) + jnp.asarray(e, a.dtype), part, identity)

    def carried_one(hop, state):
        source = count - 1 - hop
        return combine(
            state, jax.tree.map(lambda a: lax.dynamic_index_in_dim(a, source, 0, False), gathered)
        )

    return lax.fori_loop(0, ahead, carried_one, state)


def combine_pairs(earlier, later):
    return (earlier[0] * later[0], later[0] * earlier[1] + later[1])


def to_blocks(arrays):
    return tuple(
        (member.reshape((member.shape[0] // BLOCK, BLOCK) + member.shape[1:]) for member in arrays)
    )


def local_scan(start_state, step_sizes, b_proj, c_proj, inputs, decay_rates, keep_mask):

    def local_block_fn(carried, block_items):
        size_block, b_block, c_block, input_block, keep_block = block_items
        outputs = []
        for offset in range(BLOCK):
            factor = jnp.exp(size_block[offset][None, :] * decay_rates) * keep_block[offset]
            carried = (
                factor * carried
                + b_block[offset][:, None] * (size_block[offset] * input_block[offset])[None, :]
            )
            outputs.append(jnp.sum(c_block[offset][:, None] * carried, axis=0))
        return (carried, jnp.stack(outputs))

    final_state, scanned = lax.scan(
        jax.checkpoint(local_block_fn),
        start_state,
        to_blocks((step_sizes, b_proj, c_proj, inputs, keep_mask)),
    )
    return (scanned.reshape(step_sizes.shape), final_state)


def end_state(step_sizes, b_proj, inputs, decay_rates, keep_mask):

    def end_block_fn(carry_pair, block_items):
        decay_prod, carried = carry_pair
        size_block, b_block, input_block, keep_block = block_items
        for offset in range(BLOCK):
            factor = jnp.exp(size_block[offset][None, :] * decay_rates) * keep_block[offset]
            decay_prod = decay_prod * factor
            carried = (
                factor * carried
                + b_block[offset][:, None] * (size_block[offset] * input_block[offset])[None, :]
            )
        return ((decay_prod, carried), None)

    init_pair = (jnp.ones_like(decay_rates), jnp.zeros_like(decay_rates))
    final_pair, _ = lax.scan(
        end_block_fn, init_pair, to_blocks((step_sizes, b_proj, inputs, keep_mask))
    )
    return final_pair


def adjoint_end(step_sizes, c_proj, grad_y, decay_rates, keep_mask):

    def adjoint_block_fn(adjoint, block_items):
        size_block, c_block, grad_block, keep_block = block_items
        for offset in reversed(range(BLOCK)):
            adjoint = adjoint + c_block[offset][:, None] * grad_block[offset][None, :]
            adjoint = (
                jnp.exp(size_block[offset][None, :] * decay_rates) * keep_block[offset] * adjoint
            )
        return (adjoint, None)

    adjoint, _ = lax.scan(
        adjoint_block_fn,
        jnp.zeros_like(decay_rates),
        to_blocks((step_sizes, c_proj, grad_y, keep_mask)),
        reverse=True,
    )
    return adjoint


def per_device(
    hidden,
    cluster_lengths,
    norm_gain,
    in_weight,
    conv_weight,
    conv_bias,
    xproj_weight,
    dt_weight,
    dt_bias,
    a_log,
    skip,
    out_weight,
    cotangent,
):
    (
        gain_full,
        w_in,
        conv_full,
        conv_bias_full,
        w_xproj,
        w_dt,
        dt_bias_full,
        log_rates,
        skip_full,
        w_out,
    ) = (
        lax.all_gather(norm_gain, "fsdp", axis=0, tiled=True),
        lax.all_gather(in_weight, "fsdp", axis=0, tiled=True),
        lax.all_gather(conv_weight, "fsdp", axis=0, tiled=True),
        lax.all_gather(conv_bias, "fsdp", axis=0, tiled=True),
        lax.all_gather(xproj_weight, "fsdp", axis=0, tiled=True),
        lax.all_gather(dt_weight, "fsdp", axis=0, tiled=True),
        lax.all_gather(dt_bias, "fsdp", axis=0, tiled=True),
        lax.all_gather(a_log, "fsdp", axis=0, tiled=True),
        lax.all_gather(skip, "fsdp", axis=0, tiled=True),
        lax.all_gather(out_weight, "fsdp", axis=0, tiled=True),
    )
    tok_rows = hidden.shape[1]
    inner_width = w_out.shape[0]
    dt_rank = w_dt.shape[1]
    state_size = log_rates.shape[1]
    conv_taps = conv_full.shape[1]
    rim_rows = conv_taps - 1
    stream_f = hidden[0].astype(jnp.float32)
    gain_f = gain_full.astype(jnp.float32)
    inv_rms = lax.rsqrt(jnp.mean(stream_f * stream_f, axis=-1, keepdims=True) + EPS)
    scaled = stream_f * inv_rms
    normed = (scaled * gain_f).astype(jnp.bfloat16)
    projected = jnp.dot(normed, w_in, preferred_element_type=jnp.float32)
    x_branch = projected[:, :inner_width].astype(jnp.bfloat16)
    gate_pre = projected[:, inner_width:]
    left_rim = shifted(x_branch[tok_rows - rim_rows :], "seq", 1)
    padded = jnp.concatenate([left_rim, x_branch], axis=0).astype(jnp.float32)
    offsets = jnp.cumsum(cluster_lengths[0])[:-1]
    first_row = lax.axis_index("seq") * tok_rows
    positions = first_row - rim_rows + jnp.arange(tok_rows + rim_rows, dtype=jnp.int32)
    pad_ids = jnp.sum((positions[:, None] >= offsets[None, :]).astype(jnp.int32), axis=1)
    own_ids = pad_ids[rim_rows:]
    starts = jnp.any(positions[rim_rows:, None] == offsets[None, :], axis=1)
    keep_mask = 1.0 - starts.astype(jnp.float32)
    tap_masks = [
        (pad_ids[tap_index : tap_index + tok_rows] == own_ids).astype(jnp.float32)[:, None]
        for tap_index in range(conv_taps)
    ]
    conv_f = conv_full.astype(jnp.float32)
    pre_act = jnp.zeros((tok_rows, inner_width), jnp.float32) + conv_bias_full.astype(jnp.float32)
    for tap_index in range(conv_taps):
        pre_act = (
            pre_act
            + conv_f[:, tap_index] * padded[tap_index : tap_index + tok_rows] * tap_masks[tap_index]
        )
    inputs = jax.nn.silu(pre_act).astype(jnp.bfloat16)
    inputs_f = inputs.astype(jnp.float32)
    x_dbl = jnp.dot(inputs, w_xproj, preferred_element_type=jnp.float32)
    dt_low = x_dbl[:, :dt_rank].astype(jnp.bfloat16)
    b_proj = x_dbl[:, dt_rank : dt_rank + state_size]
    c_proj = x_dbl[:, dt_rank + state_size :]
    dt_pre = jnp.einsum(
        "tr,dr->td", dt_low, w_dt, preferred_element_type=jnp.float32
    ) + dt_bias_full.astype(jnp.float32)
    step_sizes = jax.nn.softplus(dt_pre)
    decay_rates = -jnp.exp(log_rates.astype(jnp.float32).T)
    decay_prod, local_end = end_state(step_sizes, b_proj, inputs_f, decay_rates, keep_mask)
    start_state = prefix(
        (decay_prod, local_end),
        "seq",
        combine_pairs,
        (jnp.ones_like(decay_prod), jnp.zeros_like(local_end)),
    )[1]
    (scanned, final_state), pullback = jax.vjp(
        partial(local_scan, keep_mask=keep_mask),
        start_state,
        step_sizes,
        b_proj,
        c_proj,
        inputs_f,
        decay_rates,
    )
    skip_f = skip_full.astype(jnp.float32)
    mixed = scanned + skip_f * inputs_f
    gate_act = jax.nn.silu(gate_pre)
    gated = (mixed * gate_act).astype(jnp.bfloat16)
    output = (stream_f + jnp.dot(gated, w_out, preferred_element_type=jnp.float32)).astype(
        jnp.bfloat16
    )
    upstream = cotangent[0]
    grad_gated = jnp.einsum("te,de->td", upstream, w_out, preferred_element_type=jnp.float32)
    grad_w_out = jnp.einsum("td,te->de", gated, upstream, preferred_element_type=jnp.float32)
    gate_sig = jax.nn.sigmoid(gate_pre)
    grad_y = grad_gated * gate_act
    grad_gate = grad_gated * mixed * gate_sig * (1.0 + gate_pre * (1.0 - gate_sig))
    grad_skip = jnp.sum(grad_y * inputs_f, axis=0)
    adjoint_local = adjoint_end(step_sizes, c_proj, grad_y, decay_rates, keep_mask)
    future = carried_in(
        (decay_prod, adjoint_local),
        "seq",
        combine_pairs,
        (jnp.ones_like(decay_prod), jnp.zeros_like(adjoint_local)),
    )[1]
    _, grad_steps, grad_b, grad_c, grad_scan_in, grad_rates = pullback((grad_y, future))
    grad_inputs = grad_scan_in + grad_y * skip_f
    grad_pre_dt = grad_steps * jax.nn.sigmoid(dt_pre)
    grad_dt_bias = jnp.sum(grad_pre_dt, axis=0)
    grad_pre_low = grad_pre_dt.astype(jnp.bfloat16)
    grad_w_dt = jnp.einsum("td,tr->dr", grad_pre_low, dt_low, preferred_element_type=jnp.float32)
    grad_dt_low = jnp.dot(grad_pre_low, w_dt, preferred_element_type=jnp.float32)
    grad_x_dbl = jnp.concatenate([grad_dt_low, grad_b, grad_c], axis=1).astype(jnp.bfloat16)
    grad_w_xproj = jnp.einsum("td,tk->dk", inputs, grad_x_dbl, preferred_element_type=jnp.float32)
    grad_inputs = grad_inputs + jnp.einsum(
        "tk,dk->td", grad_x_dbl, w_xproj, preferred_element_type=jnp.float32
    )
    grad_log_rates = (grad_rates * decay_rates).T
    act_sig = jax.nn.sigmoid(pre_act)
    grad_act = grad_inputs * act_sig * (1.0 + pre_act * (1.0 - act_sig))
    grad_conv_bias = jnp.sum(grad_act, axis=0)
    grad_padded = jnp.zeros((tok_rows + rim_rows, inner_width), jnp.float32)
    conv_columns = []
    for tap_index in range(conv_taps):
        masked = grad_act * tap_masks[tap_index]
        conv_columns.append(jnp.sum(masked * padded[tap_index : tap_index + tok_rows], axis=0))
        grad_padded = grad_padded.at[tap_index : tap_index + tok_rows].add(
            masked * conv_f[:, tap_index]
        )
    grad_conv = jnp.stack(conv_columns, axis=1)
    returned = shifted(grad_padded[:rim_rows], "seq", -1)
    grad_x_branch = grad_padded[rim_rows:] + jnp.pad(returned, ((tok_rows - rim_rows, 0), (0, 0)))
    grad_projected = jnp.concatenate([grad_x_branch, grad_gate], axis=1).astype(jnp.bfloat16)
    grad_w_in = jnp.einsum("td,tf->df", normed, grad_projected, preferred_element_type=jnp.float32)
    grad_normed = jnp.einsum("tf,df->td", grad_projected, w_in, preferred_element_type=jnp.float32)
    grad_gain = jnp.sum(grad_normed * scaled, axis=0)
    grad_scaled = grad_normed * gain_f
    grad_stream = inv_rms * grad_scaled - stream_f * inv_rms * inv_rms * inv_rms * jnp.mean(
        grad_scaled * stream_f, axis=-1, keepdims=True
    )
    grad_hidden = (upstream.astype(jnp.float32) + grad_stream)[None]
    reduced = (
        lax.psum_scatter(grad_gain, ("seq", "fsdp"), scatter_dimension=0, tiled=True),
        lax.psum_scatter(grad_w_in, ("seq", "fsdp"), scatter_dimension=0, tiled=True),
        lax.psum_scatter(grad_conv, ("seq", "fsdp"), scatter_dimension=0, tiled=True),
        lax.psum_scatter(grad_conv_bias, ("seq", "fsdp"), scatter_dimension=0, tiled=True),
        lax.psum_scatter(grad_w_xproj, ("seq", "fsdp"), scatter_dimension=0, tiled=True),
        lax.psum_scatter(grad_w_dt, ("seq", "fsdp"), scatter_dimension=0, tiled=True),
        lax.psum_scatter(grad_dt_bias, ("seq", "fsdp"), scatter_dimension=0, tiled=True),
        lax.psum_scatter(grad_log_rates, ("seq", "fsdp"), scatter_dimension=0, tiled=True),
        lax.psum_scatter(grad_skip, ("seq", "fsdp"), scatter_dimension=0, tiled=True),
        lax.psum_scatter(grad_w_out, ("seq", "fsdp"), scatter_dimension=0, tiled=True),
    )
    return (
        output[None],
        grad_hidden,
        reduced[0],
        reduced[1],
        reduced[2],
        reduced[3],
        reduced[4],
        reduced[5],
        reduced[6],
        reduced[7],
        reduced[8],
        reduced[9],
    )


def solution(mesh):
    return jax.shard_map(
        per_device,
        mesh=mesh,
        in_specs=(
            P("fsdp", "seq", None),
            P("fsdp", None),
            P("fsdp"),
            P("fsdp", None),
            P("fsdp", None),
            P("fsdp"),
            P("fsdp", None),
            P("fsdp", None),
            P("fsdp"),
            P("fsdp", None),
            P("fsdp"),
            P("fsdp", None),
            P("fsdp", "seq", None),
        ),
        out_specs=(
            P("fsdp", "seq", None),
            P("fsdp", "seq", None),
            P(("seq", "fsdp")),
            P(("seq", "fsdp"), None),
            P(("seq", "fsdp"), None),
            P(("seq", "fsdp")),
            P(("seq", "fsdp"), None),
            P(("seq", "fsdp"), None),
            P(("seq", "fsdp")),
            P(("seq", "fsdp"), None),
            P(("seq", "fsdp")),
            P(("seq", "fsdp"), None),
        ),
        check_vma=False,
    )
```

profile of v0, /device:TPU:0, one launch (start us, length us, event | category | flops | bytes accessed | tf_op | source)
XLA Modules:
  0.0 2319.7 jit_solution(9456551699575863396)
XLA Ops:
  8.8 6.0 all-gather.5
  15.1 5.5 all_gather.55
  20.5 5.2 all_gather.61
  26.1 9.4 all_gather.58
  35.8 37.4 %all-gather.13.cloned.1.call-done = bf16[1024,4096]{1,0:T(8,128)(2,1)} async-done(((bf16[256,4096]{1,0:T(8,128)(2,1)}), bf16[1024,4096]{1,0:T(8,128)(2,1)}) %all-gather.13.cloned.1.call-update) | async-done | bytes 8388624 | tf_op jit(solution)/shard_map/all_gather | solution.py:157
  73.1 6.1 fusion.394
  82.8 7.4 all_gather.59
  90.3 5.2 all-gather.4
  95.5 5.2 all-gather.6
  101.3 5.5 all-gather.7
  110.8 6.9 multiply_reduce_fusion.320
  121.2 294.1 %while.100 = (s32[]{:T(128)}, f32[16,2048]{1,0:T(8,128)}, f32[16,2048]{1,0:T(8,128)}, f32[2,64,2048]{2,1,0:T(8,128)S(1)}, f32[16,2048]{1,0:T(8,128)S(1)}, /*inde...) while((s32[]{:T(128)}, f32[16,2048]{1,0:T(8,128)}, ...), condition=%wide.region_5.6_spmd.clone, body=%wide.region_4.5_spmd.clone.sunk | while | flops 16973888 | bytes 7749200 | solution.py:103
  184.1 41.1 %multiply_add_fusion.309 = f32[16,2048]{1,0:T(8,128)} fusion(f32[16,2048]{1,0:T(8,128)S(1)} %get-tuple-element.5657, f32[16,2048]{1,0:T(8,128)S(1)} %get-tuple-element.5658, f32[16,2048]{1,0:T(8,128)S(1)} %get-tuple-element.5659, f32[16,2048]{1,0:T(8,128)S(1)} %get-tuple-element.5660, f32[16,2048]{1,0:T(8,128)S(1)} %get-tuple-element.5661, ...), kind=kLoop, calls=%fused_computation.569.clone.1 | loop fusion | flops 10125312 | bytes 2183401 | tf_op jit(solution)/shard_map/while/body/eval_jaxpr/add | solution.py:97
  225.2 42.6 %multiply_multiply_fusion.68 = f32[16,2048]{1,0:T(8,128)} fusion(f32[16,2048]{1,0:T(8,128)} %get-tuple-element.7057, f32[16,2048]{1,0:T(8,128)S(1)} %get-tuple-element.7133, f32[]{:T(128)} %bitcast.3505, f32[2048]{0:T(1024)S(1)} %bitcast.4930, f32[]{:T(128)} %bitcast.3507, f32[2048]{0:T(1024)S(1)} %bitcast.4911, f32[]{:T(128)} %bitcast.3509, ...), kind=kLoop, calls=%fused_computation.571.clone.1 | loop fusion | flops 6324224 | bytes 917761 | tf_op jit(solution)/shard_map/while/body/eval_jaxpr/mul | solution.py:95
  330.6 41.2 %multiply_add_fusion.309 = f32[16,2048]{1,0:T(8,128)} fusion(f32[16,2048]{1,0:T(8,128)S(1)} %get-tuple-element.5657, f32[16,2048]{1,0:T(8,128)S(1)} %get-tuple-element.5658, f32[16,2048]{1,0:T(8,128)S(1)} %get-tuple-element.5659, f32[16,2048]{1,0:T(8,128)S(1)} %get-tuple-element.5660, f32[16,2048]{1,0:T(8,128)S(1)} %get-tuple-element.5661, ...), kind=kLoop, calls=%fused_computation.569.clone.1 | loop fusion | flops 10125312 | bytes 2183401 | tf_op jit(solution)/shard_map/while/body/eval_jaxpr/add | solution.py:97
  371.8 43.5 %multiply_multiply_fusion.68 = f32[16,2048]{1,0:T(8,128)} fusion(f32[16,2048]{1,0:T(8,128)} %get-tuple-element.7057, f32[16,2048]{1,0:T(8,128)S(1)} %get-tuple-element.7133, f32[]{:T(128)} %bitcast.3505, f32[2048]{0:T(1024)S(1)} %bitcast.4930, f32[]{:T(128)} %bitcast.3507, f32[2048]{0:T(1024)S(1)} %bitcast.4911, f32[]{:T(128)} %bitcast.3509, ...), kind=kLoop, calls=%fused_computation.571.clone.1 | loop fusion | flops 6324224 | bytes 917761 | tf_op jit(solution)/shard_map/while/body/eval_jaxpr/mul | solution.py:95
  418.2 129.1 %while.101 = (s32[]{:T(128)}, f32[16,2048]{1,0:T(8,128)}, f32[2,64,2048]{2,1,0:T(8,128)S(1)}, f32[16,2048]{1,0:T(8,128)S(1)}, f32[2,64]{1,0:T(2,128)}, /*index=5...) while((s32[]{:T(128)}, f32[16,2048]{1,0:T(8,128)}, ...), condition=%wide.region_75.76_spmd.clone, body=%wide.region_74.75_spmd.clone.sunk | while | flops 10518595 | bytes 5258631 | solution.py:120
  442.0 40.5 %add_multiply_fusion.2 = f32[16,2048]{1,0:T(8,128)} fusion(f32[16,2048]{1,0:T(8,128)S(1)} %get-tuple-element.5809, f32[16,2048]{1,0:T(8,128)S(1)} %get-tuple-element.5810, f32[16,2048]{1,0:T(8,128)S(1)} %get-tuple-element.5811, f32[16,2048]{1,0:T(8,128)S(1)} %get-tuple-element.5812, f32[16,2048]{1,0:T(8,128)S(1)} %get-tuple-element.5813, ...), kind=kLoop, calls=%fused_computation.917.clone.1 | loop fusion | flops 10158080 | bytes 2183405 | tf_op jit(solution)/shard_map/while/body/eval_jaxpr/mul | solution.py:116
  506.7 40.5 %add_multiply_fusion.2 = f32[16,2048]{1,0:T(8,128)} fusion(f32[16,2048]{1,0:T(8,128)S(1)} %get-tuple-element.5809, f32[16,2048]{1,0:T(8,128)S(1)} %get-tuple-element.5810, f32[16,2048]{1,0:T(8,128)S(1)} %get-tuple-element.5811, f32[16,2048]{1,0:T(8,128)S(1)} %get-tuple-element.5812, f32[16,2048]{1,0:T(8,128)S(1)} %get-tuple-element.5813, ...), kind=kLoop, calls=%fused_computation.917.clone.1 | loop fusion | flops 10158080 | bytes 2183405 | tf_op jit(solution)/shard_map/while/body/eval_jaxpr/mul | solution.py:116
  547.3 31.7 %all-gather = bf16[128,2048]{1,0:T(8,128)(2,1)S(1)} all-gather(bf16[16,2048]{1,0:T(8,128)(2,1)S(1)} %convert_element_type.110), channel_id=2, replica_groups=mesh['seq'=8,'fsdp'=4] {'seq'}, dimensions={0}, use_global_device_ids=true | all-gather | bytes 589824 | tf_op jit(solution)/shard_map/all_gather | solution.py:23
  579.9 31.2 %all-gather.1 = bf16[128,2048]{1,0:T(8,128)(2,1)S(1)} all-gather(bf16[16,2048]{1,0:T(8,128)(2,1)S(1)} %convert_element_type.111), channel_id=3, replica_groups=mesh['seq'=8,'fsdp'=4] {'seq'}, dimensions={0}, use_global_device_ids=true | all-gather | bytes 589824 | tf_op jit(solution)/shard_map/all_gather | solution.py:23
  612.5 171.4 %while.98 = (s32[]{:T(128)}, f32[16,2048]{1,0:T(8,128)S(1)}, f32[2,64,2048]{2,1,0:T(8,128)}, f32[2,16,2048]{2,1,0:T(8,128)}, f32[2,64,2048]{2,1,0:T(8,128)S(1)},...) while((s32[]{:T(128)}, f32[16,2048]{1,0:T(8,128)S(1)}, ...), condition=%wide.region_73.74_spmd, body=%wide.region_8.73_spmd.sunk | while | flops 19923008 | bytes 19564316 | solution.py:80
  625.7 43.6 %multiply_reduce_fusion.379 = (f32[2048]{0:T(1024)S(1)}, f32[16,2048]{1,0:T(8,128)S(1)}, f32[16,2048]{1,0:T(8,128)S(1)}, f32[16,2048]{1,0:T(8,128)S(1)}, f32[16,...) fusion(f32[16]{0:T(128)} %get-tuple-element.5101, ...), kind=kLoop, calls=%fused_computation.4.clone.1 | loop fusion | flops 10221568 | bytes 5353656 | tf_op jit(solution)/shard_map/jvp()/while/body/eval_jaxpr/reduce_sum | solution.py:77
  711.4 43.6 %multiply_reduce_fusion.379 = (f32[2048]{0:T(1024)S(1)}, f32[16,2048]{1,0:T(8,128)S(1)}, f32[16,2048]{1,0:T(8,128)S(1)}, f32[16,2048]{1,0:T(8,128)S(1)}, f32[16,...) fusion(f32[16]{0:T(128)} %get-tuple-element.5101, ...), kind=kLoop, calls=%fused_computation.4.clone.1 | loop fusion | flops 10221568 | bytes 5353656 | tf_op jit(solution)/shard_map/jvp()/while/body/eval_jaxpr/reduce_sum | solution.py:77
  784.6 11.9 while.99
  800.0 633.1 %while.102 = (s32[]{:T(128)}, f32[16,2048]{1,0:T(8,128)}, f32[16,2048]{1,0:T(8,128)}, f32[2,64,2048]{2,1,0:T(8,128)}, bf16[2,64,16]{2,1,0:T(8,128)(2,1)}, /*inde...) while((s32[]{:T(128)}, f32[16,2048]{1,0:T(8,128)}, ...), condition=%wide.region_335.336_spmd.clone, body=%wide.region_78.335_spmd.clone.sunk | while | flops 100626432 | bytes 113702328 | solution.py:80
  831.5 43.5 %multiply_reduce_fusion.397 = (f32[16]{0:T(128)S(1)}, f32[16,2048]{1,0:T(8,128)S(1)}, f32[16,2048]{1,0:T(8,128)S(1)}, f32[16,2048]{1,0:T(8,128)S(1)}, f32[16,204...) fusion(f32[2048]{0:T(1024)S(1)} %bitcast.4719, ...), kind=kLoop, calls=%fused_computation.1249.clone.1 | loop fusion | flops 10387440 | bytes 5501180 | tf_op jit(solution)/shard_map/transpose(jvp())/while/body/eval_jaxpr/checkpoint/reduce_sum | solution.py:77
  957.9 4.4 multiply_reduce_fusion.420
  971.2 4.5 multiply_reduce_fusion.423
  975.8 4.5 multiply_reduce_fusion.424
  984.6 4.5 multiply_reduce_fusion.426
  1074.1 46.8 %select_add_fusion.3 = f32[16,2048]{1,0:T(8,128)} fusion(f32[16,2048]{1,0:T(8,128)} %get-tuple-element.7712, f32[16,2048]{1,0:T(8,128)} %get-tuple-element.6536, f32[16,2048]{1,0:T(8,128)} %get-tuple-element.6537, f32[16,2048]{1,0:T(8,128)} %get-tuple-element.6538, f32[2048]{0:T(1024)} %bitcast.4097, f32[2048]{0:T(1024)} %bitcast.4099, ...), kind=kLoop, calls=%fused_computation.1186.clone.1 | loop fusion | flops 12353536 | bytes 17178932 | tf_op jit(solution)/shard_map/transpose(jvp())/while/body/eval_jaxpr/add_any | solution.py:80
  1134.6 43.5 %multiply_reduce_fusion.397 = (f32[16]{0:T(128)S(1)}, f32[16,2048]{1,0:T(8,128)S(1)}, f32[16,2048]{1,0:T(8,128)S(1)}, f32[16,2048]{1,0:T(8,128)S(1)}, f32[16,204...) fusion(f32[2048]{0:T(1024)S(1)} %bitcast.4719, ...), kind=kLoop, calls=%fused_computation.1249.clone.1 | loop fusion | flops 10387440 | bytes 5501180 | tf_op jit(solution)/shard_map/transpose(jvp())/while/body/eval_jaxpr/checkpoint/reduce_sum | solution.py:77
  1274.3 4.5 multiply_reduce_fusion.423
  1278.8 4.5 multiply_reduce_fusion.424
  1287.6 4.5 multiply_reduce_fusion.426
  1377.2 46.8 %select_add_fusion.3 = f32[16,2048]{1,0:T(8,128)} fusion(f32[16,2048]{1,0:T(8,128)} %get-tuple-element.7712, f32[16,2048]{1,0:T(8,128)} %get-tuple-element.6536, f32[16,2048]{1,0:T(8,128)} %get-tuple-element.6537, f32[16,2048]{1,0:T(8,128)} %get-tuple-element.6538, f32[2048]{0:T(1024)} %bitcast.4097, f32[2048]{0:T(1024)} %bitcast.4099, ...), kind=kLoop, calls=%fused_computation.1186.clone.1 | loop fusion | flops 12353536 | bytes 17178932 | tf_op jit(solution)/shard_map/transpose(jvp())/while/body/eval_jaxpr/add_any | solution.py:80
  1456.1 4.5 fusion.350
  1465.3 4.5 collective-permute-done.1
  1470.8 8.2 fusion.339
  1482.8 6.4 fusion.347
  1489.3 37.4 %all-reduce.326 = (f32[1024]{0:T(1024)S(1)}, f32[2048]{0:T(1024)S(1)}, f32[2048]{0:T(1024)S(1)}, f32[2048]{0:T(1024)S(1)}) all-reduce(f32[1024]{0:T(1024)S(1)} %get-tuple-element.1300, f32[2048]{0:T(1024)S(1)} %copy-done.95, f32[2048]{0:T(1024)S(1)} %copy-done.89, ...), channel_id=6, replica_groups=mesh['seq'=8,'fsdp'=4] {'seq','fsdp'}, use_global_device_ids=true, to_apply=%region_338.339.clone | all-reduce | flops 7168 | bytes 57344
  1530.0 53.1 %reduce-scatter.19.cloned.1.call-done = f32[64,4]{1,0:T(8,128)} async-done(((f32[2048,4]{1,0:T(8,128)}), f32[64,4]{1,0:T(8,128)}) %reduce-scatter.19.cloned.1.call-update) | async-done | bytes 1040
  1584.5 131.5 %reduce-scatter.21.cloned.1.call-done = f32[64,16]{1,0:T(8,128)} async-done(((f32[2048,16]{1,0:T(8,128)}), f32[64,16]{1,0:T(8,128)}) %reduce-scatter.21.cloned.1.call-update) | async-done | bytes 4112
  1717.5 132.1 %reduce-scatter.15.cloned.1.call-done = f32[64,64]{1,0:T(8,128)} async-done(((f32[2048,64]{1,0:T(8,128)}), f32[64,64]{1,0:T(8,128)}) %reduce-scatter.15.cloned.1.call-update) | async-done | bytes 16400 | tf_op jit(solution)/shard_map/reduce_scatter | solution.py:291
  1849.6 133.6 %reduce-scatter.13.cloned.1.call-done = f32[64,96]{1,0:T(8,128)} async-done(((f32[2048,96]{1,0:T(8,128)}), f32[64,96]{1,0:T(8,128)}) %reduce-scatter.13.cloned.1.call-update) | async-done | bytes 24592 | tf_op jit(solution)/shard_map/reduce_scatter | solution.py:290
  1983.2 147.8 %reduce-scatter.17.cloned.1.call-done = f32[64,1024]{1,0:T(8,128)} async-done(((f32[2048,1024]{1,0:T(8,128)}), f32[64,1024]{1,0:T(8,128)}) %reduce-scatter.17.cloned.1.call-update) | async-done | bytes 262160 | tf_op jit(solution)/shard_map/reduce_scatter | solution.py:295
  2131.0 181.7 %reduce-scatter.11.cloned.1.call-done = f32[32,4096]{1,0:T(8,128)} async-done(((f32[1024,4096]{1,0:T(8,128)}), f32[32,4096]{1,0:T(8,128)}) %reduce-scatter.11.cloned.1.call-update) | async-done | bytes 524304 | tf_op jit(solution)/shard_map/reduce_scatter | solution.py:287
  (1073 shorter events, 722.0 us)
Async XLA Ops:
  7.2 65.9 %all-gather.13.cloned.1.call-start = ((), (), s32[]{:S(2)}) async-start(), calls=%async_computation.6 | async-start | bytes 10485760 | tf_op jit(solution)/shard_map/all_gather | solution.py:157
  8.0 102.8 %all-gather.15.cloned.1.call-start = ((), (), s32[]{:S(2)}) async-start(), calls=%async_computation.7 | async-start | bytes 5242880 | tf_op jit(solution)/shard_map/all_gather | solution.py:165
  8.7 775.2 %all-gather.17.cloned.1.call-start = ((), (), s32[]{:S(2)}) async-start(), calls=%async_computation.12 | async-start | bytes 1179648 | tf_op jit(solution)/shard_map/all_gather | solution.py:44
  79.3 28.1 %collective-permute-start = (bf16[3,2048]{1,0:T(4,128)(2,1)S(1)}, bf16[3,2048]{1,0:T(4,128)(2,1)S(1)}, u32[]{:S(2)}, u32[]{:S(2)}) collective-permute-start(bf16[3,2048]{1,0:T(4,128)(2,1)S(1)} %slice.8943), channel_id=1, source_target_pairs={{0,4},{4,8},{8,12},{12,16},{16,20},{20,24},{24,28},{1,5},{5,9},{9,... | collective-permute-start | bytes 36872 | tf_op jit(solution)/shard_map/ppermute | solution.py:17
  415.3 368.6 %all-gather.19.cloned.1.call-start = ((), (), s32[]{:S(2)}) async-start(), calls=%async_computation.13 | async-start | bytes 1179648 | tf_op jit(solution)/shard_map/all_gather | solution.py:44
  611.1 972.0 %reduce-scatter.19.cloned.1.call-start = ((), (), s32[]{:S(2)}) async-start(), calls=%async_computation.14 | async-start | bytes 1081344
  875.1 153.5 %copy-start.15 = (f32[16,2048]{1,0:T(8,128)}, f32[16,2048]{1,0:T(8,128)S(1)}, u32[]{:S(2)}) copy-start(f32[16,2048]{1,0:T(8,128)S(1)} %get-tuple-element.6365) | copy-start | bytes 393220 | tf_op jit(solution)/shard_map/transpose(jvp())/while
  875.1 157.1 %copy-start.13 = (f32[16,2048]{1,0:T(8,128)}, f32[16,2048]{1,0:T(8,128)S(1)}, u32[]{:S(2)}) copy-start(f32[16,2048]{1,0:T(8,128)S(1)} %get-tuple-element.6375) | copy-start | bytes 393220 | tf_op jit(solution)/shard_map/transpose(jvp())/while
  875.1 160.7 %copy-start.5 = (f32[16,2048]{1,0:T(8,128)}, f32[16,2048]{1,0:T(8,128)S(1)}, u32[]{:S(2)}) copy-start(f32[16,2048]{1,0:T(8,128)S(1)} %get-tuple-element.6415) | copy-start | bytes 393220 | tf_op jit(solution)/shard_map/transpose(jvp())/while
  875.1 164.2 %copy-start.9 = (f32[16,2048]{1,0:T(8,128)}, f32[16,2048]{1,0:T(8,128)S(1)}, u32[]{:S(2)}) copy-start(f32[16,2048]{1,0:T(8,128)S(1)} %get-tuple-element.6395) | copy-start | bytes 393220 | tf_op jit(solution)/shard_map/transpose(jvp())/while
  875.1 174.7 %copy-start = (f32[16,2048]{1,0:T(8,128)}, f32[16,2048]{1,0:T(8,128)S(1)}, u32[]{:S(2)}) copy-start(f32[16,2048]{1,0:T(8,128)S(1)} %get-tuple-element.6445) | copy-start | bytes 393220 | tf_op jit(solution)/shard_map/transpose(jvp())/while
  875.1 174.7 %copy-start.1 = (f32[16,2048]{1,0:T(8,128)}, f32[16,2048]{1,0:T(8,128)S(1)}, u32[]{:S(2)}) copy-start(f32[16,2048]{1,0:T(8,128)S(1)} %get-tuple-element.6440) | copy-start | bytes 393220 | tf_op jit(solution)/shard_map/transpose(jvp())/while
  875.2 178.1 %copy-start.4 = (f32[16,2048]{1,0:T(8,128)}, f32[16,2048]{1,0:T(8,128)S(1)}, u32[]{:S(2)}) copy-start(f32[16,2048]{1,0:T(8,128)S(1)} %get-tuple-element.6420) | copy-start | bytes 393220 | tf_op jit(solution)/shard_map/transpose(jvp())/while
  875.2 185.2 %copy-start.7 = (f32[16,2048]{1,0:T(8,128)}, f32[16,2048]{1,0:T(8,128)S(1)}, u32[]{:S(2)}) copy-start(f32[16,2048]{1,0:T(8,128)S(1)} %get-tuple-element.6405) | copy-start | bytes 393220 | tf_op jit(solution)/shard_map/transpose(jvp())/while
  875.2 185.2 %copy-start.8 = (f32[16,2048]{1,0:T(8,128)}, f32[16,2048]{1,0:T(8,128)S(1)}, u32[]{:S(2)}) copy-start(f32[16,2048]{1,0:T(8,128)S(1)} %get-tuple-element.6400) | copy-start | bytes 393220 | tf_op jit(solution)/shard_map/transpose(jvp())/while
  875.2 188.5 %copy-start.10 = (f32[16,2048]{1,0:T(8,128)}, f32[16,2048]{1,0:T(8,128)S(1)}, u32[]{:S(2)}) copy-start(f32[16,2048]{1,0:T(8,128)S(1)} %get-tuple-element.6390) | copy-start | bytes 393220 | tf_op jit(solution)/shard_map/transpose(jvp())/while
  875.2 188.5 %copy-start.11 = (f32[16,2048]{1,0:T(8,128)}, f32[16,2048]{1,0:T(8,128)S(1)}, u32[]{:S(2)}) copy-start(f32[16,2048]{1,0:T(8,128)S(1)} %get-tuple-element.6385) | copy-start | bytes 393220 | tf_op jit(solution)/shard_map/transpose(jvp())/while
  875.2 195.5 %copy-start.12 = (f32[16,2048]{1,0:T(8,128)}, f32[16,2048]{1,0:T(8,128)S(1)}, u32[]{:S(2)}) copy-start(f32[16,2048]{1,0:T(8,128)S(1)} %get-tuple-element.6380) | copy-start | bytes 393220 | tf_op jit(solution)/shard_map/transpose(jvp())/while
  878.8 191.9 %copy-start.16 = (f32[16,2048]{1,0:T(8,128)}, f32[16,2048]{1,0:T(8,128)S(1)}, u32[]{:S(2)}) copy-start(f32[16,2048]{1,0:T(8,128)S(1)} %get-tuple-element.6502) | copy-start | bytes 393220 | tf_op jit(solution)/shard_map/transpose(jvp())/while
  882.5 188.2 %copy-start.19 = (f32[16,2048]{1,0:T(8,128)}, f32[16,2048]{1,0:T(8,128)S(1)}, u32[]{:S(2)}) copy-start(f32[16,2048]{1,0:T(8,128)S(1)} %get-tuple-element.6503) | copy-start | bytes 393220 | tf_op jit(solution)/shard_map/transpose(jvp())/while
  886.3 177.4 %copy-start.20 = (f32[16,2048]{1,0:T(8,128)}, f32[16,2048]{1,0:T(8,128)S(1)}, u32[]{:S(2)}) copy-start(f32[16,2048]{1,0:T(8,128)S(1)} %get-tuple-element.6504) | copy-start | bytes 393220 | tf_op jit(solution)/shard_map/transpose(jvp())/while
  890.1 170.2 %copy-start.21 = (f32[16,2048]{1,0:T(8,128)}, f32[16,2048]{1,0:T(8,128)S(1)}, u32[]{:S(2)}) copy-start(f32[16,2048]{1,0:T(8,128)S(1)} %get-tuple-element.6505) | copy-start | bytes 393220 | tf_op jit(solution)/shard_map/transpose(jvp())/while
  894.0 159.3 %copy-start.22 = (f32[16,2048]{1,0:T(8,128)}, f32[16,2048]{1,0:T(8,128)S(1)}, u32[]{:S(2)}) copy-start(f32[16,2048]{1,0:T(8,128)S(1)} %get-tuple-element.6506) | copy-start | bytes 393220 | tf_op jit(solution)/shard_map/transpose(jvp())/while
  897.7 152.1 %copy-start.23 = (f32[16,2048]{1,0:T(8,128)}, f32[16,2048]{1,0:T(8,128)S(1)}, u32[]{:S(2)}) copy-start(f32[16,2048]{1,0:T(8,128)S(1)} %get-tuple-element.6507) | copy-start | bytes 393220 | tf_op jit(solution)/shard_map/transpose(jvp())/while
  1178.2 153.5 %copy-start.15 = (f32[16,2048]{1,0:T(8,128)}, f32[16,2048]{1,0:T(8,128)S(1)}, u32[]{:S(2)}) copy-start(f32[16,2048]{1,0:T(8,128)S(1)} %get-tuple-element.6365) | copy-start | bytes 393220 | tf_op jit(solution)/shard_map/transpose(jvp())/while
  1178.2 157.1 %copy-start.13 = (f32[16,2048]{1,0:T(8,128)}, f32[16,2048]{1,0:T(8,128)S(1)}, u32[]{:S(2)}) copy-start(f32[16,2048]{1,0:T(8,128)S(1)} %get-tuple-element.6375) | copy-start | bytes 393220 | tf_op jit(solution)/shard_map/transpose(jvp())/while
  1178.2 160.7 %copy-start.5 = (f32[16,2048]{1,0:T(8,128)}, f32[16,2048]{1,0:T(8,128)S(1)}, u32[]{:S(2)}) copy-start(f32[16,2048]{1,0:T(8,128)S(1)} %get-tuple-element.6415) | copy-start | bytes 393220 | tf_op jit(solution)/shard_map/transpose(jvp())/while
  1178.2 164.2 %copy-start.9 = (f32[16,2048]{1,0:T(8,128)}, f32[16,2048]{1,0:T(8,128)S(1)}, u32[]{:S(2)}) copy-start(f32[16,2048]{1,0:T(8,128)S(1)} %get-tuple-element.6395) | copy-start | bytes 393220 | tf_op jit(solution)/shard_map/transpose(jvp())/while
  1178.2 174.7 %copy-start = (f32[16,2048]{1,0:T(8,128)}, f32[16,2048]{1,0:T(8,128)S(1)}, u32[]{:S(2)}) copy-start(f32[16,2048]{1,0:T(8,128)S(1)} %get-tuple-element.6445) | copy-start | bytes 393220 | tf_op jit(solution)/shard_map/transpose(jvp())/while
  1178.2 174.7 %copy-start.1 = (f32[16,2048]{1,0:T(8,128)}, f32[16,2048]{1,0:T(8,128)S(1)}, u32[]{:S(2)}) copy-start(f32[16,2048]{1,0:T(8,128)S(1)} %get-tuple-element.6440) | copy-start | bytes 393220 | tf_op jit(solution)/shard_map/transpose(jvp())/while
  1178.2 178.1 %copy-start.4 = (f32[16,2048]{1,0:T(8,128)}, f32[16,2048]{1,0:T(8,128)S(1)}, u32[]{:S(2)}) copy-start(f32[16,2048]{1,0:T(8,128)S(1)} %get-tuple-element.6420) | copy-start | bytes 393220 | tf_op jit(solution)/shard_map/transpose(jvp())/while
  1178.2 185.2 %copy-start.7 = (f32[16,2048]{1,0:T(8,128)}, f32[16,2048]{1,0:T(8,128)S(1)}, u32[]{:S(2)}) copy-start(f32[16,2048]{1,0:T(8,128)S(1)} %get-tuple-element.6405) | copy-start | bytes 393220 | tf_op jit(solution)/shard_map/transpose(jvp())/while
  1178.3 185.2 %copy-start.8 = (f32[16,2048]{1,0:T(8,128)}, f32[16,2048]{1,0:T(8,128)S(1)}, u32[]{:S(2)}) copy-start(f32[16,2048]{1,0:T(8,128)S(1)} %get-tuple-element.6400) | copy-start | bytes 393220 | tf_op jit(solution)/shard_map/transpose(jvp())/while
  1178.3 188.5 %copy-start.10 = (f32[16,2048]{1,0:T(8,128)}, f32[16,2048]{1,0:T(8,128)S(1)}, u32[]{:S(2)}) copy-start(f32[16,2048]{1,0:T(8,128)S(1)} %get-tuple-element.6390) | copy-start | bytes 393220 | tf_op jit(solution)/shard_map/transpose(jvp())/while
  1178.3 188.5 %copy-start.11 = (f32[16,2048]{1,0:T(8,128)}, f32[16,2048]{1,0:T(8,128)S(1)}, u32[]{:S(2)}) copy-start(f32[16,2048]{1,0:T(8,128)S(1)} %get-tuple-element.6385) | copy-start | bytes 393220 | tf_op jit(solution)/shard_map/transpose(jvp())/while
  1178.3 195.5 %copy-start.12 = (f32[16,2048]{1,0:T(8,128)}, f32[16,2048]{1,0:T(8,128)S(1)}, u32[]{:S(2)}) copy-start(f32[16,2048]{1,0:T(8,128)S(1)} %get-tuple-element.6380) | copy-start | bytes 393220 | tf_op jit(solution)/shard_map/transpose(jvp())/while
  1181.9 191.9 %copy-start.16 = (f32[16,2048]{1,0:T(8,128)}, f32[16,2048]{1,0:T(8,128)S(1)}, u32[]{:S(2)}) copy-start(f32[16,2048]{1,0:T(8,128)S(1)} %get-tuple-element.6502) | copy-start | bytes 393220 | tf_op jit(solution)/shard_map/transpose(jvp())/while
  1185.6 188.2 %copy-start.19 = (f32[16,2048]{1,0:T(8,128)}, f32[16,2048]{1,0:T(8,128)S(1)}, u32[]{:S(2)}) copy-start(f32[16,2048]{1,0:T(8,128)S(1)} %get-tuple-element.6503) | copy-start | bytes 393220 | tf_op jit(solution)/shard_map/transpose(jvp())/while
  1189.4 177.4 %copy-start.20 = (f32[16,2048]{1,0:T(8,128)}, f32[16,2048]{1,0:T(8,128)S(1)}, u32[]{:S(2)}) copy-start(f32[16,2048]{1,0:T(8,128)S(1)} %get-tuple-element.6504) | copy-start | bytes 393220 | tf_op jit(solution)/shard_map/transpose(jvp())/while
  1193.2 170.2 %copy-start.21 = (f32[16,2048]{1,0:T(8,128)}, f32[16,2048]{1,0:T(8,128)S(1)}, u32[]{:S(2)}) copy-start(f32[16,2048]{1,0:T(8,128)S(1)} %get-tuple-element.6505) | copy-start | bytes 393220 | tf_op jit(solution)/shard_map/transpose(jvp())/while
  1197.1 159.3 %copy-start.22 = (f32[16,2048]{1,0:T(8,128)}, f32[16,2048]{1,0:T(8,128)S(1)}, u32[]{:S(2)}) copy-start(f32[16,2048]{1,0:T(8,128)S(1)} %get-tuple-element.6506) | copy-start | bytes 393220 | tf_op jit(solution)/shard_map/transpose(jvp())/while
  1200.8 152.1 %copy-start.23 = (f32[16,2048]{1,0:T(8,128)}, f32[16,2048]{1,0:T(8,128)S(1)}, u32[]{:S(2)}) copy-start(f32[16,2048]{1,0:T(8,128)S(1)} %get-tuple-element.6507) | copy-start | bytes 393220 | tf_op jit(solution)/shard_map/transpose(jvp())/while
  1451.7 264.3 %reduce-scatter.21.cloned.1.call-start = ((), (), s32[]{:S(2)}) async-start(), calls=%async_computation.15 | async-start | bytes 1081344
  1453.2 396.4 %reduce-scatter.15.cloned.1.call-start = ((), (), s32[]{:S(2)}) async-start(), calls=%async_computation.10 | async-start | bytes 1081344 | tf_op jit(solution)/shard_map/reduce_scatter | solution.py:291
  1454.6 528.6 %reduce-scatter.13.cloned.1.call-start = ((), (), s32[]{:S(2)}) async-start(), calls=%async_computation.9 | async-start | bytes 1081344 | tf_op jit(solution)/shard_map/reduce_scatter | solution.py:290
  1456.0 675.0 %reduce-scatter.17.cloned.1.call-start = ((), (), s32[]{:S(2)}) async-start(), calls=%async_computation.11 | async-start | bytes 8650752 | tf_op jit(solution)/shard_map/reduce_scatter | solution.py:295
  1460.6 852.0 %reduce-scatter.11.cloned.1.call-start = ((), (), s32[]{:S(2)}) async-start(), calls=%async_computation.8 | async-start | bytes 17301504 | tf_op jit(solution)/shard_map/reduce_scatter | solution.py:287
  1463.9 5.9 collective-permute-start.1
  (144 other events, 6583.2 us)
Sparse Core Ops, SparseCore 0:
  9.6 63.4 all-gather.12
  74.7 36.0 all-gather.14
  415.4 39.3 all-gather.16
  611.3 39.9 all-gather.18
  1451.9 131.2 reduce-scatter.18
  1585.3 130.7 reduce-scatter.20
  1718.9 130.6 reduce-scatter.14
  1852.5 130.6 reduce-scatter.12
  1986.1 144.8 reduce-scatter.16
  2133.7 178.9 reduce-scatter.10
where the time goes:
time: 2340 us; the launch traced here: 2320 us
  other arithmetic  1110 us (47%)
  waiting for transfers between devices  826 us (35%)
  blocking collectives  150 us (6%)
  local copies, waits for them, and re-layouts  144 us (6%)
  matrix products  42.6 us (2%)
  loops' own time  30.4 us (1%)
    reduce_sum x44, other arithmetic, local_block_fn(): outputs.append(jnp.sum(c_block[offset][:, None] * carried, axis=0))  239 us
    reduce_sum x58, other arithmetic, local_block_fn(): size_block[offset][None, :] * decay_rates  225 us
    unnamed x12, waiting for transfers between devices  186 us
    reduce_scatter x1, waiting for transfers between devices, per_device(): lax.psum_scatter(grad_w_in, ('seq', 'fsdp'), scatter_dimension=0, tiled=T...  182 us
    reduce_scatter x1, waiting for transfers between devices, per_device(): lax.psum_scatter(grad_w_out, ('seq', 'fsdp'), scatter_dimension=0, tiled=...  148 us
    reduce_scatter x1, waiting for transfers between devices, per_device(): lax.psum_scatter(grad_w_xproj, ('seq', 'fsdp'), scatter_dimension=0, tile...  134 us
    reduce_scatter x1, waiting for transfers between devices, per_device(): lax.psum_scatter(grad_w_dt, ('seq', 'fsdp'), scatter_dimension=0, tiled=T...  132 us
    add_any x2, other arithmetic, local_scan(): lax.scan(jax.checkpoint(local_block_fn), start_state, to_blocks((step_siz...  93.6 us
  transfers between devices with their start and end apart: 12, of which 9 were waited for; matrix products, arithmetic and copies ran while one was open for 15% of the time, Pallas kernels for 0%

commit v1 on v0

v1 whole, which is shorter than its diff:
```python
import functools
import math

import jax
import jax.numpy as jnp
from jax import lax
from jax.experimental import pallas as pl
from jax.experimental.pallas import tpu as pltpu
from jax.sharding import PartitionSpec as P

EPS = 1e-05
V = 8
LN = 128
HG = 4
TAIL = 16
LOG2E = 1.0 / math.log(2.0)
RESET = 1e30
F32 = jnp.float32
TOP, BOT = slice(0, V), slice(V, 2 * V)
BF16 = jnp.bfloat16
MESH = pl.DeviceIdType.MESH


class Dims:
    def __init__(self, S, F, tok, D, DI, N, R, K):
        self.S, self.F, self.tok, self.D, self.DI = S, F, tok, D, DI
        self.N, self.R, self.K = N, R, K
        self.H = V // F
        self.Q = tok // self.H
        self.T = F * tok
        self.TE = (self.Q + HG) * V
        self.NAT = F * (tok + TAIL)
        self.CL = DI // F
        self.NB = self.CL // LN


def dot(a, b, ca=1, cb=0):
    return lax.dot_general(a, b, (((ca,), (cb,)), ((), ())), preferred_element_type=F32)


def sigmoid(v):
    return 1.0 / (1.0 + jnp.exp(-v))


def exchange(d, items, cid):
    S, F = d.S, d.F
    n = len(items)
    greet = sorted({(ds % S, df % F) for it in items for ds, df, _, _ in it["sends"]} - {(0, 0)})
    total = sum(len(it["sends"]) for it in items)

    def kern(*refs):
        ins, outs, (ssem, rsem) = refs[:n], refs[n : 2 * n], refs[2 * n :]
        ms, mf = lax.axis_index("seq"), lax.axis_index("fsdp")
        bar = pltpu.get_barrier_semaphore()
        for ds, df in greet:
            to = {"seq": lax.rem(ms + (S - ds), S), "fsdp": lax.rem(mf + (F - df), F)}
            pl.semaphore_signal(bar, inc=1, device_id=to, device_id_type=MESH)
        pl.semaphore_wait(bar, len(greet))
        copies = []
        for it, src, dst in zip(items, ins, outs):
            for ds, df, take, put in it["sends"]:
                ps, pf = lax.rem(ms + ds % S, S), lax.rem(mf + df, F)
                i = len(copies)
                a, b = take(src, ms, mf, ps, pf), put(dst, ms, mf)
                if ds % S == 0 and df % F == 0:
                    c = pltpu.make_async_copy(a, b, rsem.at[i])
                else:
                    c = pltpu.make_async_remote_copy(
                        a, b, ssem.at[i], rsem.at[i], {"seq": ps, "fsdp": pf}, device_id_type=MESH
                    )
                c.start()
                copies.append(c)
        for c in copies:
            c.wait()

    return pl.pallas_call(
        kern,
        out_shape=[jax.ShapeDtypeStruct(it["shape"], it["src"].dtype) for it in items],
        in_specs=[pl.BlockSpec(memory_space=pl.ANY)] * n,
        out_specs=[pl.BlockSpec(memory_space=pl.ANY)] * n,
        scratch_shapes=[pltpu.SemaphoreType.DMA((total,)), pltpu.SemaphoreType.DMA((total,))],
        compiler_params=pltpu.CompilerParams(collective_id=cid, has_side_effects=True),
    )(*[it["src"] for it in items])


def gather_f(d, x):
    return dict(
        src=x,
        shape=(d.F,) + x.shape,
        sends=[(0, k, lambda r, ms, mf, ps, pf: r, lambda r, ms, mf: r.at[mf]) for k in range(d.F)],
    )


def swap_f(d, x):
    return dict(
        src=x,
        shape=x.shape,
        sends=[
            (0, k, lambda r, ms, mf, ps, pf: r.at[pf], lambda r, ms, mf: r.at[mf])
            for k in range(d.F)
        ],
    )


def swap_s(d, x):
    return dict(
        src=x,
        shape=x.shape,
        sends=[
            (k, 0, lambda r, ms, mf, ps, pf: r.at[ps], lambda r, ms, mf: r.at[ms])
            for k in range(d.S)
        ],
    )


def kernel(body, args, outs, scratch=()):
    return pl.pallas_call(
        body,
        out_shape=[jax.ShapeDtypeStruct(s, t) for s, t in outs],
        in_specs=[pl.BlockSpec(memory_space=pltpu.VMEM)] * len(args),
        out_specs=[pl.BlockSpec(memory_space=pltpu.VMEM)] * len(outs),
        scratch_shapes=list(scratch),
        compiler_params=pltpu.CompilerParams(vmem_limit_bytes=60 * 1024 * 1024),
    )(*args)


def lane(j):
    return slice(j * LN, (j + 1) * LN)


def natural_of(d, row, halo):
    q = lax.div(row, V) - halo
    v = lax.rem(row, V)
    f = lax.div(v, d.H)
    p = lax.rem(v, d.H) * d.Q + q
    return jnp.where(p >= 0, f * d.tok + p, d.T + f * TAIL + TAIL + p)


def to_scan(d, halo):
    rows, cols = (d.TE, d.NAT) if halo else (d.T, d.T)
    want = natural_of(d, lax.broadcasted_iota(jnp.int32, (rows, 1), 0), halo)
    have = lax.broadcasted_iota(jnp.int32, (rows, cols), 1)
    return jnp.where(have == want, 1.0, 0.0).astype(BF16)


def from_scan(d, halo):
    rows, cols = (d.NAT, d.TE) if halo else (d.T, d.T)
    want = natural_of(d, lax.broadcasted_iota(jnp.int32, (1, cols), 1), halo)
    have = lax.broadcasted_iota(jnp.int32, (rows, cols), 0)
    return jnp.where(have == want, 1.0, 0.0).astype(BF16)


def front(d, hid, gain, w, cp, xp, lens, normed, xb, gate, pre, inp, rel, xd, scan_s):
    CL = d.CL

    def rms(i, _):
        rows = pl.ds(pl.multiple_of(i * 64, 64), 64)
        h = hid[rows, :].astype(F32)
        inv = lax.rsqrt(jnp.mean(h * h, axis=-1, keepdims=True) + EPS)
        normed[rows, :] = (h * inv * gain[...]).astype(BF16)
        return 0

    lax.fori_loop(0, d.NAT // 64, rms, 0)
    perm = to_scan(d, HG)
    for c in range(0, d.D, 256):
        scan_s[:, c : c + 256] = dot(perm, normed[:, c : c + 256]).astype(BF16)
    for c in range(0, CL, 256):
        xb[:, c : c + 256] = dot(scan_s[...], w[0, :, c : c + 256]).astype(BF16).astype(F32)
        gate[:, c : c + 256] = dot(scan_s[HG * V :, :], w[1, :, c : c + 256])
    sub = lax.broadcasted_iota(jnp.int32, (V, LN), 0)
    stream = lax.div(sub, d.H)
    offs, run = [], jnp.zeros((V, LN), jnp.int32)
    for j in range(lens.shape[1] - 1):
        for f in range(d.F):
            run = run + jnp.where(stream == f, lens[f, j : j + 1, :], 0)
        offs.append(run)
    rel[0 : HG * V, :] = jnp.zeros((HG * V, LN), F32)
    rel[HG * V + d.T :, :] = jnp.zeros((HG * V, LN), F32)
    base = lax.axis_index("seq") * d.tok + lax.rem(sub, d.H) * d.Q

    def mark(q, _):
        pos = base + q
        last = jnp.zeros((V, LN), jnp.int32)
        for o in offs:
            last = jnp.maximum(last, jnp.where(o <= pos, o, 0))
        rel[pl.ds(pl.multiple_of((q + HG) * V, V), V), :] = jnp.where(
            pos == 0, 0.5, (pos - last).astype(F32)
        )
        return 0

    lax.fori_loop(0, d.Q, mark, 0)

    def conv(i, _):
        r0 = pl.multiple_of(i * 64, 64)
        rows = pl.ds(r0, 64)
        age = rel[pl.ds(pl.multiple_of(r0 + HG * V, V), 64), :]
        for j in range(d.NB):
            acc = jnp.zeros((64, LN), F32) + cp[4:5, lane(j)]
            for k in range(d.K):
                back = d.K - 1 - k
                xs = xb[pl.ds(pl.multiple_of(r0 + (HG - back) * V, V), 64), lane(j)]
                acc = acc + jnp.where(age >= back, xs * cp[k : k + 1, lane(j)], 0.0)
            pre[rows, lane(j)] = acc
            inp[rows, lane(j)] = (acc * sigmoid(acc)).astype(BF16)
        return 0

    lax.fori_loop(0, d.T // 64, conv, 0)
    xd[...] = dot(inp[...], xp[...])


def steps_and_local(
    d, xdp, wdt, cp, gate, inp, rel, cot, ow, dec2,
    lows, dtpre, dtd, u, bcb, gg, gy, cots, ends, e_out, sd_out,
):
    CL, T, R, N = d.CL, d.T, d.R, d.N
    xd = xdp[0]
    for f in range(1, d.F):
        xd = xd + xdp[f]
    low = xd[:, :R].astype(BF16)
    lows[...] = low
    bc = xd[:, R : R + 2 * N]
    hi = bc.astype(BF16)
    rest = (bc - hi.astype(F32)).astype(BF16)
    both = jnp.concatenate([hi, rest], axis=1)
    for n in range(0, 2 * N, 4):
        row = lax.rem(lax.broadcasted_iota(jnp.int32, (4 * N, 4 * LN), 0), 2 * N)
        col = lax.div(lax.broadcasted_iota(jnp.int32, (4 * N, 4 * LN), 1), LN) + n
        spread = jnp.where(row == col, 1.0, 0.0).astype(BF16)
        bcb[:, n * LN : (n + 4) * LN] = dot(both, spread).astype(bcb.dtype)
    perm = to_scan(d, 0)
    for c in range(0, d.D, 256):
        cots[:, c : c + 256] = dot(perm, cot[:, c : c + 256]).astype(BF16)
    for c in range(0, CL, 256):
        dtpre[:, c : c + 256] = dot(low, wdt[c : c + 256, :], 1, 1)
        gg[:, c : c + 256] = dot(cots[...], ow[c : c + 256, :], 1, 1)

    def steps(i, _):
        rows = pl.ds(pl.multiple_of(i * 64, 64), 64)
        age = rel[pl.ds(pl.multiple_of(i * 64 + HG * V, V), 64), :]
        for j in range(d.NB):
            z = dtpre[rows, lane(j)] + cp[5:6, lane(j)]
            dt = jnp.maximum(z, 0.0) + jnp.log1p(jnp.exp(-jnp.abs(z)))
            dtpre[rows, lane(j)] = z
            dtd[rows, lane(j)] = jnp.where(age == 0.0, RESET, dt)
            u[rows, lane(j)] = dt * inp[rows, lane(j)].astype(F32)
            g = gate[rows, lane(j)]
            gy[rows, lane(j)] = gg[rows, lane(j)] * (g * sigmoid(g))
        return 0

    lax.fori_loop(0, T // 64, steps, 0)
    half = N // 2
    for j in range(d.NB):
        for n0 in range(0, N, half):
            dn = [
                jnp.broadcast_to(dec2[n : n + 1, lane(j)], (V, LN)) for n in range(n0, n0 + half)
            ]

            def local(q, carry, n0=n0, j=j, dn=dn):
                hs, gs = list(carry[0]), list(carry[1])
                up = pl.ds(pl.multiple_of(q * 2 * V, 2 * V), 2 * V)
                down = pl.ds(pl.multiple_of((d.Q - 2 - 2 * q) * V, 2 * V), 2 * V)
                a_dt, a_u = dtd[up, lane(j)], u[up, lane(j)]
                b_dt, b_gy = dtd[down, lane(j)], gy[down, lane(j)]
                for i in range(half):
                    b = bcb[up, lane(n0 + i)].astype(F32)
                    c = bcb[down, lane(N + n0 + i)].astype(F32)
                    for t in (TOP, BOT):
                        hs[i] = jnp.exp2(a_dt[t] * dn[i]) * hs[i] + a_u[t] * b[t]
                    for t in (BOT, TOP):
                        gs[i] = jnp.exp2(b_dt[t] * dn[i]) * (gs[i] + b_gy[t] * c[t])
                return tuple(hs), tuple(gs)

            zero = tuple(jnp.zeros((V, LN), F32) for _ in range(half))
            hs, gs = lax.fori_loop(0, d.Q // 2, local, (zero, zero))
            for i in range(half):
                ends[0, (n0 + i) * V : (n0 + i + 1) * V, lane(j)] = hs[i]
                ends[1, (n0 + i) * V : (n0 + i + 1) * V, lane(j)] = gs[i]
        def add(q, s, j=j):
            return s + dtd[pl.ds(pl.multiple_of(q * V, V), V), lane(j)]

        own = lax.fori_loop(0, d.Q, add, jnp.zeros((V, LN), F32))
        hidx = lax.rem(lax.broadcasted_iota(jnp.int32, (V, LN), 0), d.H)
        whole, t = own, 1
        while t < d.H:
            low_half = lax.rem(lax.div(hidx, t), 2) == 0
            whole = whole + jnp.where(low_half, pltpu.roll(whole, V - t, 0), pltpu.roll(whole, t, 0))
            t *= 2
        sd_out[0:V, lane(j)] = own
        sd_out[V : 2 * V, lane(j)] = whole
        for n in range(0, N, 2):
            fw, bw = [], []
            for m in (n, n + 1):
                fac = jnp.exp2(own * dec2[m : m + 1, lane(j)])
                e = ends[0, m * V : (m + 1) * V, lane(j)]
                g = ends[1, m * V : (m + 1) * V, lane(j)]
                x, y = e, g
                for t in range(1, d.H):
                    x = jnp.where(hidx == t, fac * pltpu.roll(x, 1, 0) + e, x)
                    y = jnp.where(hidx == d.H - 1 - t, fac * pltpu.roll(y, V - 1, 0) + g, y)
                fw.append(x)
                bw.append(y)
            e_out[0, n * V : (n + 2) * V, lane(j)] = jnp.concatenate(fw, axis=0).astype(BF16)
            e_out[1, n * V : (n + 2) * V, lane(j)] = jnp.concatenate(bw, axis=0).astype(BF16)


def scan_both(
    d, epieces, sdall, ends, sd, dec2, dtpre, dtd, u, inp, bcb, gg, gy, gate, cp, cots, ow, normed, wdt, lows,
    outp, gow, giwg, gpl, gsc, gx, gdec, gwdt, gskip,
    m_s, y_s, start, x_s, gated, ggate, gated_n, ggate_n,
):
    CL, T, N, Q, NB = d.CL, d.T, d.N, d.Q, d.NB
    ms = lax.axis_index("seq")
    hidx = lax.rem(lax.broadcasted_iota(jnp.int32, (V, LN), 0), d.H)
    for j in range(NB):
        own = sd[0:V, lane(j)]
        for n0 in range(0, N, 2):
            dn = [jnp.broadcast_to(dec2[n0 + i : n0 + i + 1, lane(j)], (V, LN)) for i in (0, 1)]
            band = pl.ds(n0 * V, 2 * V)

            def join(p, acc, j=j, dn=dn, band=band):
                tot = sdall[p, :, lane(j)]
                e = epieces[p, band, lane(j)].astype(F32)
                return tuple(jnp.exp2(tot * dn[i]) * acc[i] + e[i * V : (i + 1) * V] for i in (0, 1))

            zero = (jnp.zeros((V, LN), F32),) * 2
            fw = lax.fori_loop(0, ms, join, zero)
            bw = lax.fori_loop(
                0, d.S - 1 - ms, lambda i, acc: join(d.S - 1 - i, acc), zero
            )
            for i in (0, 1):
                n = n0 + i
                rows = slice(n * V, (n + 1) * V)
                fac = jnp.exp2(own * dn[i])
                x = fw[i] if d.H == 1 else pltpu.roll(fw[i], V - (d.H - 1), 0)
                y = bw[i] if d.H == 1 else pltpu.roll(bw[i], d.H - 1, 0)
                for t in range(1, d.H):
                    xn = pltpu.roll(fac * x + ends[0, rows, lane(j)], 1, 0)
                    yn = pltpu.roll(fac * y + ends[1, rows, lane(j)], V - 1, 0)
                    x = jnp.where(hidx == t, xn, x)
                    y = jnp.where(hidx == d.H - 1 - t, yn, y)
                start[0, rows, lane(j)] = x
                start[1, rows, lane(j)] = y
    for j in range(NB):
        dn = [jnp.broadcast_to(dec2[n : n + 1, lane(j)], (V, LN)) for n in range(N)]

        def ahead(q, hs, j=j, dn=dn):
            hs = list(hs)
            rows = pl.ds(pl.multiple_of(q * 2 * V, 2 * V), 2 * V)
            t, w = dtd[rows, lane(j)], u[rows, lane(j)]
            y = [jnp.zeros((V, LN), F32), jnp.zeros((V, LN), F32)]
            for n in range(N):
                b = bcb[rows, lane(n)].astype(F32)
                c = bcb[rows, lane(N + n)].astype(F32)
                ms = []
                for k, p in enumerate((TOP, BOT)):
                    m = jnp.exp2(t[p] * dn[n]) * hs[n]
                    hs[n] = m + w[p] * b[p]
                    y[k] = y[k] + c[p] * hs[n]
                    ms.append(m)
                m_s[j, rows, lane(n)] = jnp.concatenate(ms, axis=0).astype(m_s.dtype)
            y_s[rows, lane(j)] = jnp.concatenate(y, axis=0)
            return tuple(hs)

        lax.fori_loop(0, Q // 2, ahead, tuple(start[0, n * V : (n + 1) * V, lane(j)] for n in range(N)))

    def gating(i, sk):
        rows = pl.ds(pl.multiple_of(i * 64, 64), 64)
        out = []
        for j in range(NB):
            x = inp[rows, lane(j)].astype(F32)
            mixed = y_s[rows, lane(j)] + cp[6:7, lane(j)] * x
            g = gate[rows, lane(j)]
            s = sigmoid(g)
            gated[rows, lane(j)] = (mixed * (g * s)).astype(BF16)
            ggate[rows, lane(j)] = (
                gg[rows, lane(j)] * mixed * s * (1.0 + g * (1.0 - s))
            ).astype(BF16)
            p = gy[rows, lane(j)] * x
            out.append(sk[j] + jnp.sum(p.reshape(8, V, LN), axis=0))
        return tuple(out)

    sk = lax.fori_loop(0, T // 64, gating, tuple(jnp.zeros((V, LN), F32) for _ in range(NB)))
    gskip[...] = jnp.zeros_like(gskip)
    for j in range(NB):
        gskip[0:1, lane(j)] = jnp.sum(sk[j], axis=0, keepdims=True)
    back = from_scan(d, 0)
    gated_n[...] = dot(back, gated[...]).astype(BF16)
    ggate_n[...] = dot(back, ggate[...]).astype(BF16)
    for c in range(0, d.D, 256):
        outp[:, c : c + 256] = dot(gated_n[...], ow[:, c : c + 256]).astype(BF16)
        gow[:, c : c + 256] = dot(gated[...], cots[:, c : c + 256], 0, 0).astype(BF16)
    for c in range(0, CL, 256):
        giwg[:, c : c + 256] = dot(normed[0:T, :], ggate_n[:, c : c + 256], 0, 0).astype(BF16)
    half = N // 2
    for j in range(NB):
        for n0 in range(0, N, half):
            dn = [
                jnp.broadcast_to(dec2[n : n + 1, lane(j)], (V, LN)) for n in range(n0, n0 + half)
            ]

            def behind(i, carry, n0=n0, j=j, dn=dn):
                gs, gd = list(carry[0]), list(carry[1])
                rows = pl.ds(pl.multiple_of((Q - 2 - 2 * i) * V, 2 * V), 2 * V)
                t, w, g0 = dtd[rows, lane(j)], u[rows, lane(j)], gy[rows, lane(j)]
                t0 = jnp.where(t == RESET, 0.0, t)
                gu = [jnp.zeros((V, LN), F32), jnp.zeros((V, LN), F32)]
                gt = [jnp.zeros((V, LN), F32), jnp.zeros((V, LN), F32)]
                for i in range(half):
                    n = n0 + i
                    b = bcb[rows, lane(n)].astype(F32)
                    c = bcb[rows, lane(N + n)].astype(F32)
                    m = m_s[j, rows, lane(n)].astype(F32)
                    pc = g0 * (m + w * b)
                    pb = [None, None]
                    gc = g0 * c
                    for k, p in ((1, BOT), (0, TOP)):
                        g = gs[i] + gc[p]
                        pb[k] = g * w[p]
                        gu[k] = gu[k] + g * b[p]
                        x = g * m[p]
                        gt[k] = gt[k] + x * dn[i]
                        gd[i] = gd[i] + x * t0[p]
                        gs[i] = jnp.exp2(t[p] * dn[i]) * g
                    pb = jnp.concatenate(pb, axis=0)
                    if j > 0:
                        pb = pb + x_s[rows, lane(n)]
                        pc = pc + x_s[rows, lane(N + n)]
                    x_s[rows, lane(n)] = pb
                    x_s[rows, lane(N + n)] = pc
                gu, gt = jnp.concatenate(gu, axis=0), jnp.concatenate(gt, axis=0)
                if n0 > 0:
                    gu = gu + gsc[rows, lane(j)]
                    gt = gt + y_s[rows, lane(j)]
                gsc[rows, lane(j)] = gu
                y_s[rows, lane(j)] = gt
                return tuple(gs), tuple(gd)

            zero = tuple(jnp.zeros((V, LN), F32) for _ in range(half))
            first = tuple(start[1, n * V : (n + 1) * V, lane(j)] for n in range(n0, n0 + half))
            _, gd = lax.fori_loop(0, Q // 2, behind, (first, zero))
            for i in range(half):
                dec = dec2[n0 + i : n0 + i + 1, lane(j)] * (1.0 / LOG2E)
                gdec[n0 + i : n0 + i + 1, lane(j)] = jnp.sum(gd[i], axis=0, keepdims=True) * dec

    def finish(i, acc):
        rows = pl.ds(pl.multiple_of(i * 64, 64), 64)
        out = []
        for j in range(NB):
            x = inp[rows, lane(j)].astype(F32)
            z = dtpre[rows, lane(j)]
            gu = gsc[rows, lane(j)]
            gt = y_s[rows, lane(j)] * (1.0 / LOG2E) + gu * x
            dt = jnp.maximum(z, 0.0) + jnp.log1p(jnp.exp(-jnp.abs(z)))
            gz = gt * sigmoid(z)
            gpl[rows, lane(j)] = gz.astype(BF16)
            gsc[rows, lane(j)] = gu * dt + gy[rows, lane(j)] * cp[6:7, lane(j)]
            out.append(acc[j] + jnp.sum(gz.reshape(8, V, LN), axis=0))
        return tuple(out)

    db = lax.fori_loop(0, T // 64, finish, tuple(jnp.zeros((V, LN), F32) for _ in range(NB)))
    for j in range(NB):
        gskip[1:2, lane(j)] = jnp.sum(db[j], axis=0, keepdims=True)
    gwdt[...] = dot(gpl[...], lows[...], 0, 0)
    gx[:, 0 : d.R] = dot(gpl[...], wdt[...])
    acc = jnp.zeros((T, 2 * N), F32)
    for n in range(0, 2 * N, 4):
        row = lax.div(lax.broadcasted_iota(jnp.int32, (4 * LN, 2 * N), 0), LN) + n
        col = lax.broadcasted_iota(jnp.int32, (4 * LN, 2 * N), 1)
        pick = jnp.where(row == col, 1.0, 0.0).astype(BF16)
        acc = acc + dot(x_s[:, n * LN : (n + 4) * LN].astype(BF16), pick)
    gx[:, d.R : d.R + 2 * N] = acc


def rear(
    d, gxp, inp, gsc, xp, pre, rel, xb, cp, hid, normed, w, ggate_n, gain, gskip, gdec, gwdt,
    gnp, giwx, small, ggain,
    ga, gxe, gpn, rowsum,
):
    CL, T, NB = d.CL, d.T, d.NB
    s = gxp[0]
    for f in range(1, d.F):
        s = s + gxp[f]
    gxd = s.astype(BF16)
    W = d.R + 2 * d.N
    pad = HG * V
    for c in range(0, CL, 256):
        ga[pad : pad + T, c : c + 256] = gsc[:, c : c + 256] + dot(gxd, xp[c : c + 256, :], 1, 1)
    ga[0:pad, :] = jnp.zeros((pad, CL), F32)
    ga[pad + T :, :] = jnp.zeros((pad, CL), F32)

    def act(i, acc):
        r0 = pl.multiple_of(i * 64, 64)
        rows = pl.ds(r0, 64)
        shift = pl.ds(pl.multiple_of(r0 + pad, V), 64)
        age = rel[shift, :]
        out = []
        for j in range(NB):
            p = pre[rows, lane(j)]
            q = sigmoid(p)
            g = ga[shift, lane(j)] * q * (1.0 + p * (1.0 - q))
            ga[shift, lane(j)] = g
            a = list(acc[j])
            a[4] = a[4] + jnp.sum(g.reshape(8, V, LN), axis=0)
            for k in range(d.K):
                back = d.K - 1 - k
                xs = xb[pl.ds(pl.multiple_of(r0 + (HG - back) * V, V), 64), lane(j)]
                t = jnp.where(age >= back, g * xs, 0.0)
                a[k] = a[k] + jnp.sum(t.reshape(8, V, LN), axis=0)
            out.append(tuple(a))
        return tuple(out)

    zero = tuple(tuple(jnp.zeros((V, LN), F32) for _ in range(5)) for _ in range(NB))
    acc = lax.fori_loop(0, T // 64, act, zero)
    rowsum[...] = jnp.zeros_like(rowsum)
    for j in range(NB):
        for k in range(5):
            rowsum[k : k + 1, lane(j)] = jnp.sum(acc[j][k], axis=0, keepdims=True)
    rowsum[5:6, :] = gskip[1:2, :]
    rowsum[6:7, :] = gskip[0:1, :]
    rowsum[8 : 8 + d.N, :] = gdec[...]
    small[:, 0:LN] = rowsum[...].T.astype(BF16)
    small[:, LN : LN + W] = dot(inp[...], gxd, 0, 0).astype(BF16)
    small[:, LN + W : LN + W + d.R] = gwdt[...].astype(BF16)
    small[:, LN + W + d.R :] = jnp.zeros((CL, 3 * LN - LN - W - d.R), BF16)

    def spread(i, _):
        r0 = pl.multiple_of(i * 32, 32)
        for j in range(NB):
            acc = jnp.zeros((32, LN), F32)
            for k in range(d.K):
                back = d.K - 1 - k
                src = pl.ds(pl.multiple_of(r0 + back * V, V), 32)
                acc = acc + jnp.where(
                    rel[src, :] >= back, ga[src, lane(j)] * cp[k : k + 1, lane(j)], 0.0
                )
            gxe[pl.ds(r0, 32), lane(j)] = acc.astype(BF16)
        return 0

    lax.fori_loop(0, d.TE // 32, spread, 0)
    back_m = from_scan(d, HG)
    for c in range(0, CL, 256):
        gpn[:, c : c + 256] = dot(back_m, gxe[:, c : c + 256]).astype(BF16)
    gpn[0:T, CL:] = ggate_n[...]
    gpn[T:, CL:] = jnp.zeros((d.NAT - T, CL), BF16)
    for c in range(0, CL, 256):
        giwx[:, c : c + 256] = dot(normed[...], gpn[:, c : c + 256], 0, 0).astype(BF16)
    for c in range(0, d.D, 256):
        g = dot(gpn[:, 0:CL], w[0, c : c + 256, :], 1, 1) + dot(gpn[:, CL:], w[1, c : c + 256, :], 1, 1)
        gnp[:, c : c + 256] = g.astype(BF16)
    ggain[...] = jnp.zeros_like(ggain)

    def gains(i, acc):
        rows = pl.ds(pl.multiple_of(i * 64, 64), 64)
        h = hid[rows, :].astype(F32)
        inv = lax.rsqrt(jnp.mean(h * h, axis=-1, keepdims=True) + EPS)
        return acc + jnp.sum((gnp[rows, :].astype(F32) * h * inv).reshape(8, V, d.D), axis=0)

    tot = lax.fori_loop(0, d.NAT // 64, gains, jnp.zeros((V, d.D), F32))
    ggain[0:1, :] = jnp.sum(tot, axis=0, keepdims=True)


def vm(*shape, dtype=F32):
    return pltpu.VMEM(shape, dtype)


def per_device(
    d, hidden, cluster_lengths, norm_gain, in_weight, conv_weight, conv_bias, xproj_weight,
    dt_weight, dt_bias, a_log, skip, out_weight, cotangent,
):
    S, F, T, D, CL, N, tok = d.S, d.F, d.T, d.D, d.CL, d.N, d.tok
    fs, ss = range(F), range(S)
    DF = D // F
    part = functools.partial
    lens = jnp.broadcast_to(cluster_lengths[0][:, None], (cluster_lengths.shape[1], LN))
    gain8 = jnp.broadcast_to(norm_gain.astype(F32)[None, :], (V, DF))
    whole = lambda r, ms, mf, ps, pf: r
    hid_item = dict(
        src=hidden[0],
        shape=(d.NAT, D),
        sends=[(0, k, whole, lambda r, ms, mf: r.at[pl.ds(mf * tok, tok)]) for k in fs]
        + [
            (
                1,
                k,
                lambda r, ms, mf, ps, pf: r.at[pl.ds(tok - TAIL, TAIL)],
                lambda r, ms, mf: r.at[pl.ds(T + mf * TAIL, TAIL)],
            )
            for k in fs
        ],
    )
    w_item = dict(
        src=in_weight,
        shape=(2, D, CL),
        sends=[
            (
                0,
                k,
                lambda r, ms, mf, ps, pf, g=g: r.at[:, pl.ds(pl.multiple_of(g * d.DI + pf * CL, LN), CL)],
                lambda r, ms, mf, g=g: r.at[g, pl.ds(mf * DF, DF)],
            )
            for k in fs
            for g in (0, 1)
        ],
    )
    hid, w, cot, gains, lens = exchange(
        d, [hid_item, w_item, gather_f(d, cotangent[0]), gather_f(d, gain8), gather_f(d, lens)], 0
    )
    cot = cot.reshape(T, D)
    gain = gains[:, 0, :].reshape(1, D)
    rows = [conv_weight.astype(F32).T, conv_bias, dt_bias, skip]
    cp = jnp.concatenate([r.astype(F32).reshape(-1, CL) for r in rows], axis=0)
    cp = jnp.pad(cp, ((0, V - cp.shape[0]), (0, 0)))
    dec2 = -jnp.exp(a_log.astype(F32).T) * LOG2E
    W = d.R + 2 * N
    xp = jnp.pad(xproj_weight, ((0, 0), (0, LN - W)))
    TP = T + 2 * HG * V

    normed, xb, gate, pre, inp, rel, xd = kernel(
        part(front, d),
        (hid, gain, w, cp, xp, lens),
        [((d.NAT, D), BF16), ((d.TE, CL), F32), ((T, CL), F32), ((T, CL), F32), ((T, CL), BF16),
         ((TP, LN), F32), ((T, LN), F32)],
        [vm(d.TE, D, dtype=BF16)],
    )
    (xdp,) = exchange(d, [gather_f(d, xd.astype(BF16))], 1)
    lows, dtpre, dtd, u, bcb, gg, gy, cots, ends, e_out, sd = kernel(
        part(steps_and_local, d),
        (xdp.astype(F32), dt_weight, cp, gate, inp, rel, cot, out_weight, dec2),
        [((T, d.R), BF16), ((T, CL), F32), ((T, CL), F32), ((T, CL), F32), ((T, 2 * N * LN), F32 if T <= 512 else BF16),
         ((T, CL), F32), ((T, CL), F32), ((T, D), BF16), ((2, N * V, CL), F32),
         ((2, N * V, CL), BF16), ((2 * V, CL), F32)],
    )
    pieces = dict(
        src=e_out,
        shape=(S, N * V, CL),
        sends=[
            (
                k,
                0,
                lambda r, ms, mf, ps, pf: r.at[jnp.where(ps > ms, 0, 1)],
                lambda r, ms, mf: r.at[ms],
            )
            for k in ss
            if k > 0
        ],
    )
    totals = dict(
        src=sd[V:],
        shape=(S, V, CL),
        sends=[(k, 0, whole, lambda r, ms, mf: r.at[ms]) for k in ss if k > 0],
    )
    epieces, sdall = exchange(d, [pieces, totals], 2)
    outp, gow, giwg, gpl, gsc, gx, gdec, gwdt, gskip, ggate_n = kernel(
        lambda *r: scan_both(d, *r[:28], *r[29:36], r[28]),
        (epieces, sdall, ends, sd, dec2, dtpre, dtd, u, inp, bcb, gg, gy, gate, cp, cots, out_weight,
         normed, dt_weight, lows),
        [((T, D), BF16), ((CL, D), BF16), ((D, CL), BF16), ((T, CL), BF16), ((T, CL), F32),
         ((T, LN), F32), ((N, CL), F32), ((CL, d.R), F32), ((V, CL), F32), ((T, CL), BF16)],
        [vm(d.NB, T, N * LN, dtype=BF16), vm(T, CL), vm(2, N * V, CL), vm(T, 2 * N * LN),
         vm(T, CL, dtype=BF16), vm(T, CL, dtype=BF16), vm(T, CL, dtype=BF16)],
    )
    (gxp,) = exchange(d, [gather_f(d, gx.astype(BF16))], 3)
    gnp, giwx, small, ggain = kernel(
        part(rear, d),
        (gxp[:, :, :W].astype(F32), inp, gsc, xproj_weight, pre, rel, xb, cp, hid, normed, w, ggate_n, gain, gskip,
         gdec, gwdt),
        [((d.NAT, D), BF16), ((D, CL), BF16), ((CL, 3 * LN), BF16), ((V, D), F32)],
        [vm(TP, CL), vm(d.TE, CL, dtype=BF16), vm(d.NAT, 2 * CL, dtype=BF16), vm(LN, CL)],
    )
    normal = dict(
        src=gnp,
        shape=(F * (tok + TAIL), D),
        sends=[
            (
                0,
                k,
                lambda r, ms, mf, ps, pf: r.at[pl.ds(pf * tok, tok)],
                lambda r, ms, mf: r.at[pl.ds(mf * tok, tok)],
            )
            for k in fs
        ]
        + [
            (
                -1,
                k,
                lambda r, ms, mf, ps, pf: r.at[pl.ds(T + pf * TAIL, TAIL)],
                lambda r, ms, mf: r.at[pl.ds(T + mf * TAIL, TAIL)],
            )
            for k in fs
        ],
    )
    blocks = lambda a: a.reshape((S, a.shape[0] // S) + a.shape[1:])
    ggain = jnp.swapaxes(ggain.reshape(V, S, D // S), 0, 1)
    gnr, outr, gowr, smallr, gxr, ggr, gar = exchange(
        d,
        [normal, swap_f(d, outp.reshape(F, tok, D))]
        + [swap_s(d, a) for a in (blocks(gow), blocks(small), blocks(giwx), blocks(giwg), ggain)],
        4,
    )
    add = lambda a: jnp.sum(a.astype(F32), axis=0)
    DS = D // (S * F)
    gwx, gwg = (add(a).astype(BF16).reshape(F, DS, CL) for a in (gxr, ggr))
    ga = jnp.swapaxes(add(gar).reshape(V, F, DS), 0, 1)
    wx, wg, gg = exchange(d, [swap_f(d, a) for a in (gwx, gwg, ga)], 5)
    g_in = jnp.concatenate(
        [jnp.swapaxes(a, 0, 1).reshape(DS, d.DI) for a in (wx, wg)], axis=1
    ).astype(F32)
    g_gain = add(gg)[0]
    packed = jnp.concatenate([add(gowr), add(smallr)], axis=1).astype(BF16)
    perm = [(j * F + f, f * S + j) for f in fs for j in ss]
    packed = lax.ppermute(packed, ("seq", "fsdp"), perm).astype(F32)
    g_out, sm = packed[:, :D], packed[:, D:]
    h = hidden[0].astype(F32)
    inv = lax.rsqrt(jnp.mean(h * h, axis=-1, keepdims=True) + EPS)
    gn = add(gnr[:T].reshape(F, tok, D))
    gn = gn + jnp.pad(add(gnr[T:].reshape(F, TAIL, D)), ((tok - TAIL, 0), (0, 0)))
    g2 = gn * gain
    mean = jnp.mean(g2 * h, axis=-1, keepdims=True)
    g_hid = cotangent[0].astype(F32) + inv * g2 - h * (inv * inv * inv) * mean
    output = (h + add(outr)).astype(BF16)
    return (
        output[None],
        g_hid[None],
        g_gain,
        g_in,
        sm[:, 0 : d.K],
        sm[:, 4],
        sm[:, LN : LN + W],
        sm[:, LN + W : LN + W + d.R],
        sm[:, 5],
        sm[:, V : V + N],
        sm[:, 6],
        g_out,
    )


def solution(mesh):
    S, F = mesh.shape["seq"], mesh.shape["fsdp"]

    def run(*args):
        tok, D = args[0].shape[1] // S, args[0].shape[2]
        d = Dims(
            S, F, tok, D, args[11].shape[0], args[9].shape[1], args[7].shape[1], args[4].shape[1]
        )
        return jax.shard_map(
            functools.partial(per_device, d),
            mesh=mesh,
            in_specs=(
                P("fsdp", "seq", None), P("fsdp", None), P("fsdp"), P("fsdp", None),
                P("fsdp", None), P("fsdp"), P("fsdp", None), P("fsdp", None), P("fsdp"),
                P("fsdp", None), P("fsdp"), P("fsdp", None), P("fsdp", "seq", None),
            ),
            out_specs=(
                P("fsdp", "seq", None), P("fsdp", "seq", None), P(("seq", "fsdp")),
                P(("seq", "fsdp"), None), P(("seq", "fsdp"), None), P(("seq", "fsdp")),
                P(("seq", "fsdp"), None), P(("seq", "fsdp"), None), P(("seq", "fsdp")),
                P(("seq", "fsdp"), None), P(("seq", "fsdp")), P(("seq", "fsdp"), None),
            ),
            check_vma=False,
        )(*args)

    return run
```

time: 2340 us -> 315 us (0.13)
  other arithmetic: 1110 us -> 20.2 us
  waiting for transfers between devices: 826 us -> 0.01 us
  Pallas kernels: 0 us -> 274 us
  blocking collectives: 150 us -> 0 us
  local copies, waits for them, and re-layouts: 144 us -> 18.9 us
  matrix products: 42.6 us -> 0 us
  loops' own time: 30.4 us -> 0 us
    reduce_scatter x4 -> x0, waiting for transfers between devices: 595 us -> none  [the longest x1 182 us: per_device(): lax.psum_scatter(grad_w_in, ('seq', 'fsdp'), scatter_dimension=0, tiled=T...]
    reduce_sum x110 -> x10, other arithmetic: 483 us -> 8.1 us  [the longest x9 7.92 us: per_device(): add = lambda a: jnp.sum(a.astype(F32), axis=0)]
    mul x308 -> x1, other arithmetic: 286 us -> 1.34 us  [per_device(): dec2 = -jnp.exp(a_log.astype(F32).T) * LOG2E]
    pallas_call x0 -> x10, Pallas kernels: none -> 274 us  [the longest x6 194 us: exchange(): pl.pallas_call(kern, out_shape=[jax.ShapeDtypeStruct(it['shape'], it['src...]
    unnamed x12 -> x0, waiting for transfers between devices: 186 us -> none
    add x33 -> x0, other arithmetic: 172 us -> none  [the longest x2 82.2 us: end_block_fn(): factor * carried]
    add_any x16 -> x0, other arithmetic: 143 us -> none  [the longest x2 93.6 us: local_scan(): lax.scan(jax.checkpoint(local_block_fn), start_state, to_blocks((step_siz...]
    all_gather x10 -> x0, blocking collectives: 112 us -> none  [the longest x2 62.9 us: prefix(): lax.all_gather(a.astype(kind), axis)]
  transfers between devices with their start and end apart: 12 -> 1, of which waited for: 9 -> 0; matrix products, arithmetic and copies ran while one was open for 15% -> 4% of each run, Pallas kernels for 0% -> 3%
where the time goes in v1:
time: 315 us; the launch traced here: 314 us
  Pallas kernels  274 us (87%)
  other arithmetic  20.2 us (6%)
  local copies, waits for them, and re-layouts  18.9 us (6%)
    pallas_call x6, Pallas kernels, exchange(): pl.pallas_call(kern, out_shape=[jax.ShapeDtypeStruct(it['shape'], it['src...  194 us
    pallas_call x4, Pallas kernels, kernel(): pl.pallas_call(body, out_shape=[jax.ShapeDtypeStruct(s, t) for s, t in ou...  79.1 us
    reduce_sum x9, other arithmetic, per_device(): add = lambda a: jnp.sum(a.astype(F32), axis=0)  7.92 us
  transfers between devices with their start and end apart: 1, of which 0 were waited for; matrix products, arithmetic and copies ran while one was open for 4% of the time, Pallas kernels for 3%

profile of v1, /device:TPU:0, one launch (start us, length us, event | category | flops | bytes accessed | tf_op | source)
XLA Modules:
  0.0 314.3 jit_solution(5981929522366634866)
XLA Ops:
  0.7 0.7 reshape.100
  1.3 0.7 reshape.101
  2.0 0.7 reshape.102
  2.7 1.3 multiply_bitcast_fusion.dec2.r_4_
  4.1 1.0 copy.31.xp
  5.1 1.6 copy.32.wdt.r_17_
  6.7 1.3 broadcast_in_dim.10.refs_4_
  8.0 1.3 broadcast_in_dim.8.refs_3_
  9.3 53.1 %shard_map.220 = (bf16[576,1024]{1,0:T(8,128)(2,1)}, bf16[2,1024,512]{2,1,0:T(8,128)(2,1)}, bf16[4,128,1024]{2,1,0:T(8,128)(2,1)}, f32[4,8,256]{2,1,0:T(8,128)}, s32[4,8,128]{2,1,0:T(8,128)}) custom-call(bf16[128,1024]{1,0:T(8,128)(2,1)} %bitcast.45, bf16[256,4096]{1,0:T(8,128)(2,1)} %refs_1_.1, bf16[128,1024]{1,0:T(8,128)(2,1)} %bitcast.47, ...), custom_call_target="tpu_custom_call" | custom-call | tf_op jit(solution)/shard_map/pallas_call | solution.py:76
  62.4 1.4 slice.50
  63.8 0.7 pad.16.xp
  64.4 0.6 fusion.13.cp.r_13_
  65.1 9.5 %shard_map.221 = (bf16[576,1024]{1,0:T(8,128)(2,1)}, f32[544,512]{1,0:T(8,128)}, f32[512,512]{1,0:T(8,128)}, f32[512,512]{1,0:T(8,128)}, bf16[512,512]{1,0:T(8,1...) custom-call(bf16[576,1024]{1,0:T(8,128)(2,1)} %get-tuple-element.60.hid, f32[1,1024]{1,0:T(1,128)} %bitcast.60, ...), custom_call_target="tpu_custom_call" | custom-call | tf_op jit(solution)/shard_map/pallas_call | solution.py:117
  74.6 1.6 convert_element_type.75.refs_0_
  76.2 7.9 %shard_map.222 = bf16[4,512,128]{2,1,0:T(8,128)(2,1)} custom-call(bf16[512,128]{1,0:T(8,128)(2,1)} %convert_element_type.75.refs_0_), custom_call_target="tpu_custom_call" | custom-call | tf_op jit(solution)/shard_map/pallas_call | solution.py:76
  84.2 2.1 convert_element_type.76.xdp
  86.3 21.4 %shard_map.223 = (bf16[512,64]{1,0:T(8,128)(2,1)}, f32[512,512]{1,0:T(8,128)}, f32[512,512]{1,0:T(8,128)}, f32[512,512]{1,0:T(8,128)}, f32[512,4096]{1,0:T(8,128...) custom-call(f32[4,512,128]{2,1,0:T(8,128)} %convert_element_type.76., ...), custom_call_target="tpu_custom_call" | custom-call | tf_op jit(solution)/shard_map/pallas_call | solution.py:117
  107.7 1.3 slice.51.refs_1_
  109.0 31.5 %shard_map.224 = (bf16[8,128,512]{2,1,0:T(8,128)(2,1)}, f32[8,8,512]{2,1,0:T(8,128)}) custom-call(bf16[2,128,512]{2,1,0:T(8,128)(2,1)} %get-tuple-element.69.refs_0_, f32[8,512]{1,0:T(8,128)} %slice.51.refs_1_), custom_call_target="tpu_custom_call" | custom-call | tf_op jit(solution)/shard_map/pallas_call | solution.py:76
  140.5 36.3 %shard_map.225 = (bf16[512,1024]{1,0:T(8,128)(2,1)}, bf16[512,1024]{1,0:T(8,128)(2,1)}, bf16[1024,512]{1,0:T(8,128)(2,1)}, bf16[512,512]{1,0:T(8,128)(2,1)}, f32...) custom-call(bf16[8,128,512]{2,1,0:T(8,128)(2,1)} %get-tuple-element., ...), custom_call_target="tpu_custom_call" | custom-call | tf_op jit(solution)/shard_map/pallas_call | solution.py:117
  176.9 1.6 convert_element_type.78.refs_0_
  178.5 7.0 %shard_map.226 = bf16[4,512,128]{2,1,0:T(8,128)(2,1)} custom-call(bf16[512,128]{1,0:T(8,128)(2,1)} %convert_element_type.78.refs_0_), custom_call_target="tpu_custom_call" | custom-call | tf_op jit(solution)/shard_map/pallas_call | solution.py:76
  185.5 2.1 slice_convert_fusion.gxp
  187.7 11.8 %shard_map.227 = (bf16[576,1024]{1,0:T(8,128)(2,1)}, bf16[1024,512]{1,0:T(8,128)(2,1)}, bf16[512,384]{1,0:T(8,128)(2,1)}, f32[8,1024]{1,0:T(8,128)}) custom-call(f32[4,512,96]{2,1,0:T(8,128)} %slice_convert_fusion.gxp, bf16[512,512]{1,0:T(8,128)(2,1)} %get-tuple-element.66.inp.r_8_, f32[512,512]{1,0:T(8,128)} %get-tuple-element.84.gsc, ...), custom_call_target="tpu_custom_call" | custom-call | tf_op jit(solution)/shard_map/pallas_call | solution.py:117
  199.5 86.5 %shard_map.228 = (bf16[576,1024]{1,0:T(8,128)(2,1)}, bf16[4,128,1024]{2,1,0:T(8,128)(2,1)}, bf16[8,64,1024]{2,1,0:T(8,128)(2,1)}, bf16[8,64,384]{2,1,0:T(8,128)(...) custom-call(bf16[576,1024]{1,0:T(8,128)(2,1)} %get-tuple-element.91.refs_0_, ...), custom_call_target="tpu_custom_call" | custom-call | tf_op jit(solution)/shard_map/pallas_call | solution.py:76
  286.0 1.2 reduce.3
  287.1 1.4 reduce.2
  288.6 0.8 collective-permute-start
  289.4 0.9 slice.54
  290.4 1.5 convert_reduce_fusion.1
  292.0 0.8 fusion.5
  292.8 0.6 copy.43
  293.5 2.1 reduce_sum.113
  295.5 0.8 reduce_sum.114
  296.3 8.3 %shard_map.229 = (bf16[4,32,512]{2,1,0:T(8,128)(2,1)}, bf16[4,32,512]{2,1,0:T(8,128)(2,1)}, f32[4,8,32]{2,1,0:T(8,128)}) custom-call(bf16[4,32,512]{2,1,0:T(8,128)(2,1)} %bitcast.52, bf16[4,32,512]{2,1,0:T(8,128)(2,1)} %bitcast.53, f32[4,8,32]{2,1,0:T(8,128)} %bitcast.64), custom_call_target="tpu_custom_call" | custom-call | tf_op jit(solution)/shard_map/pallas_call | solution.py:76
  304.7 0.7 reduce_sum.116
  305.4 0.9 copy.40
  306.3 0.9 copy.41
  307.5 0.2 fusion
  307.7 0.8 maximum_convert_fusion
  308.5 1.1 fusion.3
  309.6 0.5 slice_bitcast_fusion
  310.2 0.7 copy.39
  310.8 0.7 copy.38
  311.5 0.7 slice_reduce_fusion
  312.3 0.7 slice.67
  312.9 0.6 slice.66
  313.6 0.7 slice.71
  (28 shorter events, 0.5 us)
Async XLA Ops:
  0.6 63.8 %copy-start.7 = (bf16[512,4]{0,1:T(4,128)(2,1)S(1)}, bf16[512,4]{0,1:T(4,128)(2,1)}, u32[]{:S(2)}) copy-start(bf16[512,4]{0,1:T(4,128)(2,1)} %param.17) | copy-start | bytes 12292
  5.1 69.5 %copy-start.1 = (bf16[512,96]{1,0:T(8,128)(2,1)}, bf16[512,96]{1,0:T(8,128)(2,1)S(1)}, u32[]{:S(2)}) copy-start(bf16[512,96]{1,0:T(8,128)(2,1)S(1)} %copy.31.xp) | copy-start | bytes 294916
  286.0 4.3 %copy-start.2 = (bf16[576,1024]{1,0:T(8,128)(2,1)S(1)}, bf16[576,1024]{1,0:T(8,128)(2,1)}, u32[]{:S(2)}) copy-start(bf16[576,1024]{1,0:T(8,128)(2,1)} %get-tuple-element.99) | copy-start | bytes 3538948
  288.6 3.4 %copy-start = (bf16[1,128,1024]{2,1,0:T(8,128)(2,1)S(1)}, bf16[1,128,1024]{2,1,0:T(8,128)(2,1)}, u32[]{:S(2)}) copy-start(bf16[1,128,1024]{2,1,0:T(8,128)(2,1)} %param.13) | copy-start | bytes 786436
  288.6 21.5 %collective-permute-start = (bf16[64,1408]{1,0:T(8,128)(2,1)S(1)}, bf16[64,1408]{1,0:T(8,128)(2,1)S(1)}, u32[]{:S(2)}, u32[]{:S(2)}) collective-permute-start(bf16[64,1408]{1,0:T(8,128)(2,1)S(1)} %pad_maximum_fusion), channel_id=1, source_target_pairs={{0,0},{4,1},{8,2},{12,3},{16,4},{20,5},{24,6},{28,7},{1,8},{5,9},{... | collective-permute-start | bytes 540680 | tf_op jit(solution)/shard_map/ppermute | solution.py:711
  290.3 2.4 copy-start.6
  290.4 5.1 %copy-start.3 = (bf16[8,128,512]{2,1,0:T(8,128)(2,1)S(1)}, bf16[8,128,512]{2,1,0:T(8,128)(2,1)}, u32[]{:S(2)}) copy-start(bf16[8,128,512]{2,1,0:T(8,128)(2,1)} %get-tuple-element.101) | copy-start | bytes 3145732
  295.5 11.9 %copy-start.5 = (f32[4,1,256]{2,1,0:T(1,128)S(1)}, f32[4,1,256]{2,1,0:T(1,128)}, u32[]{:S(2)}) copy-start(f32[4,1,256]{2,1,0:T(1,128)} %slice.50) | copy-start | bytes 12292
  296.3 12.2 %copy-start.4 = (bf16[1,128,1024]{2,1,0:T(8,128)(2,1)S(1)}, bf16[1,128,1024]{2,1,0:T(8,128)(2,1)}, u32[]{:S(2)}) copy-start(bf16[1,128,1024]{2,1,0:T(8,128)(2,1)} %param.25) | copy-start | bytes 786436

commit v2 on v1

v2 whole, which is shorter than its diff:
```python
import functools
import math

import jax
import jax.numpy as jnp
from jax import lax
from jax.experimental import pallas as pl
from jax.experimental.pallas import tpu as pltpu
from jax.sharding import PartitionSpec as P

EPS = 1e-05
V = 8
LN = 128
HG = 4
TAIL = 16
LOG2E = 1.0 / math.log(2.0)
RESET = 1e30
F32 = jnp.float32
TOP, BOT = slice(0, V), slice(V, 2 * V)
BF16 = jnp.bfloat16
MESH = pl.DeviceIdType.MESH


class Dims:
    def __init__(self, S, F, tok, D, DI, N, R, K, clusters):
        self.S, self.F, self.tok, self.D, self.DI = S, F, tok, D, DI
        self.N, self.R, self.K, self.clusters = N, R, K, clusters
        self.H = V // F
        self.Q = tok // self.H
        self.T = F * tok
        self.TE = (self.Q + HG) * V
        self.NAT = F * (tok + TAIL)
        self.CL = DI // F
        self.NB = self.CL // LN


def dot(a, b, ca=1, cb=0):
    return lax.dot_general(a, b, (((ca,), (cb,)), ((), ())), preferred_element_type=F32)


def sigmoid(v):
    return 1.0 / (1.0 + jnp.exp(-v))


def kernel(body, args, outs, scratch=()):
    return pl.pallas_call(
        body,
        out_shape=[jax.ShapeDtypeStruct(s, t) for s, t in outs],
        in_specs=[pl.BlockSpec(memory_space=pltpu.VMEM)] * len(args),
        out_specs=[pl.BlockSpec(memory_space=pltpu.VMEM)] * len(outs),
        scratch_shapes=list(scratch),
        compiler_params=pltpu.CompilerParams(vmem_limit_bytes=60 * 1024 * 1024),
    )(*args)


def lane(j):
    return slice(j * LN, (j + 1) * LN)


def natural_of(d, row, halo):
    q = lax.div(row, V) - halo
    v = lax.rem(row, V)
    f = lax.div(v, d.H)
    p = lax.rem(v, d.H) * d.Q + q
    return jnp.where(p >= 0, f * d.tok + p, d.T + f * TAIL + TAIL + p)


def to_scan(d, halo):
    rows, cols = (d.TE, d.NAT) if halo else (d.T, d.T)
    want = natural_of(d, lax.broadcasted_iota(jnp.int32, (rows, 1), 0), halo)
    have = lax.broadcasted_iota(jnp.int32, (rows, cols), 1)
    return jnp.where(have == want, 1.0, 0.0).astype(BF16)


def from_scan(d, halo):
    rows, cols = (d.NAT, d.TE) if halo else (d.T, d.T)
    want = natural_of(d, lax.broadcasted_iota(jnp.int32, (1, cols), 1), halo)
    have = lax.broadcasted_iota(jnp.int32, (rows, cols), 0)
    return jnp.where(have == want, 1.0, 0.0).astype(BF16)


class Refs:
    pass


class Copy:
    def __init__(self, copy, remote):
        self.copy, self.sent, self.got = copy, not remote, False
        self.remote = remote

    def wait_send(self):
        if not self.sent:
            self.copy.wait_send()
            self.sent = True

    def wait_recv(self):
        if not self.got:
            if self.remote:
                self.copy.wait_recv()
            else:
                self.copy.wait()
            self.got = True

    def wait(self):
        self.wait_send()
        self.wait_recv()


class Net:
    def __init__(self, d, ssem, rsem):
        self.d, self.ssem, self.rsem, self.used = d, ssem, rsem, 0
        self.ms, self.mf = lax.axis_index("seq"), lax.axis_index("fsdp")
        self.open = []

    def at(self, ds, df):
        return lax.rem(self.ms + ds % self.d.S, self.d.S), lax.rem(self.mf + df % self.d.F, self.d.F)

    def start(self, copy, remote):
        copy.start()
        self.open.append(Copy(copy, remote))
        return self.open[-1]

    def send(self, src, dst, ps, pf):
        i = self.used
        self.used += 1
        return self.start(
            pltpu.make_async_remote_copy(
                src, dst, self.ssem.at[i], self.rsem.at[i], {"seq": ps, "fsdp": pf}, device_id_type=MESH
            ),
            True,
        )

    def local(self, src, dst):
        i = self.used
        self.used += 1
        return self.start(pltpu.make_async_copy(src, dst, self.rsem.at[i]), False)

    def drain(self):
        for c in self.open:
            c.wait()


class Scatter:
    def __init__(self, net, mine, near, far):
        self.net, self.mine, self.near, self.far = net, mine, near, far
        d = net.d
        self.half = d.S // 2
        self.x, self.z = lax.rem(net.ms, 2), lax.div(net.ms, 2)
        self.pal = net.ms + 1 - 2 * self.x
        self.order = [lax.rem(self.z + k, self.half) for k in list(range(1, self.half)) + [0]]
        self.out, self.ins = [], []

    def first(self):
        for z in self.order:
            self.out.append(
                self.net.send(self.mine.at[1 - self.x, z], self.near.at[z], self.pal, self.net.mf)
            )

    def second(self):
        for k, z in enumerate(self.order):
            self.out[k].wait()
            both = self.mine[self.x, z].astype(F32) + self.near[z].astype(F32)
            self.mine[self.x, z] = both.astype(self.mine.dtype)
            if k < self.half - 1:
                self.ins.append(
                    self.net.send(
                        self.mine.at[self.x, z], self.far.at[k], z * 2 + self.x, self.net.mf
                    )
                )

    def total(self):
        acc = self.mine[self.x, self.z].astype(F32)
        for k, c in enumerate(self.ins):
            c.wait()
            acc = acc + self.far[k].astype(F32)
        return acc


def layer(d, names, *refs):
    r = Refs()
    for name, ref in zip(names, refs):
        setattr(r, name, ref)
    S, F, CL, T, N, Q, NB, D, tok, H = d.S, d.F, d.CL, d.T, d.N, d.Q, d.NB, d.D, d.tok, d.H
    DF = D // F
    net = Net(d, r.ssem, r.rsem)
    ms, mf = net.ms, net.mf
    x_bit = lax.rem(ms, 2)
    pal = ms + 1 - 2 * x_bit
    core = mf + 1 - 2 * lax.rem(mf, 2)
    spot = mf * S + ms
    home_s, home_f = lax.div(spot, F), lax.rem(spot, F)
    mine = ms * F + mf
    from_s, from_f = lax.rem(mine, S), lax.div(mine, S)
    moves = spot != mine
    greet = {(0, k) for k in range(F)} | {(k, 0) for k in range(S)}
    greet |= {(k % S, g) for k in (1, -1) for g in range(F)}
    greet = sorted(greet - {(0, 0)})
    bar = pltpu.get_barrier_semaphore()
    for ds, df in greet:
        ps, pf = net.at(-ds, -df)
        pl.semaphore_signal(bar, inc=1, device_id={"seq": ps, "fsdp": pf}, device_id_type=MESH)

    @pl.when(moves)
    def _():
        pl.semaphore_signal(
            bar, inc=1, device_id={"seq": from_s, "fsdp": from_f}, device_id_type=MESH
        )

    own = [
        net.local(r.hidden, r.hid.at[pl.ds(mf * tok, tok)]),
        net.local(r.params, r.pg.at[mf]),
        net.local(r.in_weight.at[:, pl.ds(pl.multiple_of(mf * CL, LN), CL)], r.w.at[0, pl.ds(mf * DF, DF)]),
        net.local(
            r.in_weight.at[:, pl.ds(pl.multiple_of(d.DI + mf * CL, LN), CL)],
            r.w.at[1, pl.ds(mf * DF, DF)],
        ),
        net.local(r.cotangent, r.cot.at[pl.ds(mf * tok, tok)]),
        net.local(r.out_weight, r.ow),
        net.local(r.xproj_weight, r.xp),
        net.local(r.dt_weight, r.wdt),
        net.local(r.conv_weight, r.cw),
        net.local(r.a_log, r.al),
    ]
    pl.semaphore_wait(bar, len(greet) + moves.astype(jnp.int32))

    rows_of = lambda ref, f, n: ref.at[pl.ds(f * n, n)]
    same_core = [lax.rem(mf + 2 * k, F) for k in range(1, F // 2)]
    other_chip = [(lax.rem(mf + 2 * k, F), lax.rem(core + 2 * k, F)) for k in range(1, F // 2)]

    def spread_rows(src, dst):
        direct = [net.send(src, rows_of(dst, mf, tok), ms, f) for f in same_core]
        beside = [net.send(src, rows_of(dst, mf, tok), ms, core)]
        return direct, beside

    def relay_rows(dst, direct, beside):
        for k, c in enumerate(direct):
            c.wait()
            f = lax.rem(mf + F - 2 * (k + 1), F)
            beside.append(net.send(rows_of(dst, f, tok), rows_of(dst, f, tok), ms, core))

    pgs = [net.send(r.params, r.pg.at[mf], ms, net.at(0, k)[1]) for k in range(1, F)]
    h_direct, h_beside = spread_rows(r.hidden, r.hid)
    halo = [
        net.send(
            r.hidden.at[pl.ds(tok - TAIL, TAIL)],
            r.hid.at[pl.ds(T + mf * TAIL, TAIL)],
            *net.at(1, k),
        )
        for k in range(F)
    ]

    def w_slice(g, f):
        return r.in_weight.at[:, pl.ds(pl.multiple_of(g * d.DI + f * CL, LN), CL)]

    w_beside = [net.send(w_slice(g, core), r.w.at[g, pl.ds(mf * DF, DF)], ms, core) for g in (0, 1)]
    HF = DF // 2

    def w_far(g):
        out = []
        for pair in other_chip:
            for f in pair:
                src = r.in_weight.at[
                    pl.ds(x_bit * HF, HF), pl.ds(pl.multiple_of(g * d.DI + f * CL, LN), CL)
                ]
                out.append(net.send(src, r.w.at[g, pl.ds(mf * DF + x_bit * HF, HF)], ms, f))
        return out

    def w_relay(g, far):
        out = []
        i = 0
        for k in range(1, F // 2):
            for flip in (0, 1):
                far[i].wait()
                i += 1
                f0 = lax.rem(mf + F - 2 * k, F)
                if flip:
                    f0 = f0 + 1 - 2 * lax.rem(f0, 2)
                place = r.w.at[g, pl.ds(f0 * DF + x_bit * HF, HF)]
                out.append(net.send(place, place, pal, mf))
        return out

    back0 = from_scan(d, 0)
    for c in h_direct:
        c.wait_send()
    wx_far = w_far(0)
    for k, c in enumerate(h_direct):
        c.wait_recv()
        f = lax.rem(mf + F - 2 * (k + 1), F)
        h_beside.append(net.send(rows_of(r.hid, f, tok), rows_of(r.hid, f, tok), ms, core))
    for c in pgs + own[:2]:
        c.wait()
    for f in range(F):
        r.gain[0:1, f * DF : (f + 1) * DF] = r.pg[f, 3:4, 0:DF]
    sub = lax.broadcasted_iota(jnp.int32, (V, LN), 0)
    hidx = lax.rem(sub, H)
    stream = lax.div(sub, H)
    offs, run = [], jnp.zeros((V, LN), F32)
    for j in range(d.clusters - 1):
        for f in range(F):
            run = run + jnp.where(stream == f, r.pg[f, 4:5, j : j + 1], 0.0)
        offs.append(run)
    base = ms * tok + hidx * Q
    r.rel[0 : HG * V, :] = jnp.zeros((HG * V, LN), F32)
    r.rel[HG * V + T :, :] = jnp.zeros((HG * V, LN), F32)

    def mark(q, _):
        pos = (base + q).astype(F32)
        last = jnp.zeros((V, LN), F32)
        for o in offs:
            last = jnp.maximum(last, jnp.where(o <= pos, o, 0.0))
        r.rel[pl.ds(pl.multiple_of((q + HG) * V, V), V), :] = jnp.where(pos == 0.0, 0.5, pos - last)
        return 0

    lax.fori_loop(0, Q, mark, 0)
    own[8].wait()
    own[9].wait()
    eye = lambda n: jnp.where(
        lax.broadcasted_iota(jnp.int32, (n, n), 0) == lax.broadcasted_iota(jnp.int32, (n, n), 1), 1.0, 0.0
    ).astype(BF16)
    r.cp[0 : d.K, :] = dot(eye(d.K), r.cw[...], 1, 1)
    r.cp[4:7, :] = r.pg[mf, 0:3, :]
    r.dec[...] = -LOG2E * jnp.exp(dot(eye(N), r.al[...], 1, 1))
    for c in h_beside + halo:
        c.wait()

    def rms(i, _):
        rows = pl.ds(pl.multiple_of(i * 64, 64), 64)
        h = r.hid[rows, :].astype(F32)
        inv = lax.rsqrt(jnp.mean(h * h, axis=-1, keepdims=True) + EPS)
        r.normed[rows, :] = (h * inv * r.gain[...]).astype(BF16)
        return 0

    lax.fori_loop(0, d.NAT // 64, rms, 0)
    perm = to_scan(d, HG)
    for c in range(0, D, 256):
        r.big[:, c : c + 256] = dot(perm, r.normed[:, c : c + 256]).astype(BF16)
    wx_near = w_relay(0, wx_far)
    wg_far = w_far(1)
    c_direct, c_beside = spread_rows(r.cotangent, r.cot)
    own[2].wait()
    w_beside[0].wait()
    for c in wx_near:
        c.wait()
    for c in range(0, CL, 256):
        r.xb[:, c : c + 256] = (
            dot(r.big[:, :], r.w[0, :, c : c + 256]).astype(BF16).astype(F32)
        )

    def conv(i, _):
        r0 = pl.multiple_of(i * 64, 64)
        rows = pl.ds(r0, 64)
        age = r.rel[pl.ds(pl.multiple_of(r0 + HG * V, V), 64), :]
        for j in range(NB):
            acc = jnp.zeros((64, LN), F32) + r.cp[4:5, lane(j)]
            for k in range(d.K):
                back = d.K - 1 - k
                xs = r.xb[pl.ds(pl.multiple_of(r0 + (HG - back) * V, V), 64), lane(j)]
                acc = acc + jnp.where(age >= back, xs * r.cp[k : k + 1, lane(j)], 0.0)
            r.pre[rows, lane(j)] = acc
            r.inp[rows, lane(j)] = (acc * sigmoid(acc)).astype(BF16)
        return 0

    lax.fori_loop(0, T // 64, conv, 0)
    own[6].wait()
    W = d.R + 2 * N
    r.xd[:, 0:W] = dot(r.inp[...], r.xp[...]).astype(BF16)
    xds = [net.send(r.xd, r.xdr.at[k - 1], *net.at(0, k)) for k in range(1, F)]
    wg_near = w_relay(1, wg_far)
    relay_rows(r.cot, c_direct, c_beside)
    for c in [own[3], own[4], own[5], w_beside[1]] + wg_near + c_beside:
        c.wait()
    for c in range(0, CL, 256):
        r.gate[:, c : c + 256] = dot(r.big[HG * V :, :], r.w[1, :, c : c + 256])
    perm = to_scan(d, 0)
    for c in range(0, D, 256):
        r.big[0:T, c : c + 256] = dot(perm, r.cot[:, c : c + 256]).astype(BF16)
    for c in range(0, CL, 256):
        r.gg[0:T, c : c + 256] = dot(r.big[0:T, :], r.ow[c : c + 256, :], 1, 1)

    def gys(i, _):
        rows = pl.ds(pl.multiple_of(i * 64, 64), 64)
        for j in range(NB):
            g = r.gate[rows, lane(j)]
            r.gy[rows, lane(j)] = r.gg[rows, lane(j)] * (g * sigmoid(g))
        return 0

    lax.fori_loop(0, T // 64, gys, 0)
    for c in xds:
        c.wait()
    xd = r.xd[:, 0:W].astype(F32)
    for k in range(F - 1):
        xd = xd + r.xdr[k, :, 0:W].astype(F32)
    own[7].wait()
    low = xd[:, : d.R].astype(BF16)
    r.xd[:, 0 : d.R] = low
    for c in range(0, CL, 256):
        r.dtpre[:, c : c + 256] = dot(low, r.wdt[c : c + 256, :], 1, 1)

    def steps(i, acc):
        rows = pl.ds(pl.multiple_of(i * 64, 64), 64)
        age = r.rel[pl.ds(pl.multiple_of(i * 64 + HG * V, V), 64), :]
        out = []
        for j in range(NB):
            z = r.dtpre[rows, lane(j)] + r.cp[5:6, lane(j)]
            dt = jnp.maximum(z, 0.0) + jnp.log1p(jnp.exp(-jnp.abs(z)))
            r.dtpre[rows, lane(j)] = z
            e = jnp.where(age == 0.0, RESET, dt)
            r.dtd[rows, lane(j)] = e
            r.u[rows, lane(j)] = dt * r.inp[rows, lane(j)].astype(F32)
            out.append(acc[j] + jnp.sum(e.reshape(8, V, LN), axis=0))
        return tuple(out)

    sums = lax.fori_loop(0, T // 64, steps, tuple(jnp.zeros((V, LN), F32) for _ in range(NB)))
    for j in range(NB):
        whole, t = sums[j], 1
        while t < H:
            low_half = lax.rem(lax.div(hidx, t), 2) == 0
            whole = whole + jnp.where(low_half, pltpu.roll(whole, V - t, 0), pltpu.roll(whole, t, 0))
            t *= 2
        r.sd[0:V, lane(j)] = sums[j]
        r.tot[:, lane(j)] = whole
    tots = [net.send(r.tot, r.totr.at[k - 1], *net.at(k, 0)) for k in range(1, S)]
    bc = xd[:, d.R : W]
    hi = bc.astype(BF16)
    rest = (bc - hi.astype(F32)).astype(BF16)
    both = jnp.concatenate([hi, rest], axis=1)
    for n in range(0, 2 * N, 4):
        row = lax.rem(lax.broadcasted_iota(jnp.int32, (4 * N, 4 * LN), 0), 2 * N)
        col = lax.div(lax.broadcasted_iota(jnp.int32, (4 * N, 4 * LN), 1), LN) + n
        pick = jnp.where(row == col, 1.0, 0.0).astype(BF16)
        r.bcb[:, n * LN : (n + 4) * LN] = dot(both, pick).astype(r.bcb.dtype)

    half = N // 2
    row_n = lambda n: slice(n * V, (n + 1) * V)
    dec_of = lambda n, j: jnp.broadcast_to(r.dec[n : n + 1, lane(j)], (V, LN))

    def own_ends(j):
        for n0 in range(0, N, half):
            dn = [dec_of(n, j) for n in range(n0, n0 + half)]

            def local(q, carry, n0=n0, dn=dn):
                hs, gs = list(carry[0]), list(carry[1])
                up = pl.ds(pl.multiple_of(q * 2 * V, 2 * V), 2 * V)
                down = pl.ds(pl.multiple_of((Q - 2 - 2 * q) * V, 2 * V), 2 * V)
                a_dt, a_u = r.dtd[up, lane(j)], r.u[up, lane(j)]
                b_dt, b_gy = r.dtd[down, lane(j)], r.gy[down, lane(j)]
                for i in range(half):
                    b = r.bcb[up, lane(n0 + i)].astype(F32)
                    c = r.bcb[down, lane(N + n0 + i)].astype(F32)
                    for t in (TOP, BOT):
                        hs[i] = jnp.exp2(a_dt[t] * dn[i]) * hs[i] + a_u[t] * b[t]
                    for t in (BOT, TOP):
                        gs[i] = jnp.exp2(b_dt[t] * dn[i]) * (gs[i] + b_gy[t] * c[t])
                return tuple(hs), tuple(gs)

            zero = tuple(jnp.zeros((V, LN), F32) for _ in range(half))
            hs, gs = lax.fori_loop(0, Q // 2, local, (zero, zero))
            for i in range(half):
                r.ends[0, row_n(n0 + i), lane(j)] = hs[i]
                r.ends[1, row_n(n0 + i), lane(j)] = gs[i]
        one = r.sd[0:V, lane(j)]
        fw, bw = [], []
        for n0 in range(0, N, H):
            a, b = jnp.zeros((V, LN), F32), jnp.zeros((V, LN), F32)
            for t in range(H):
                fac = jnp.exp2(one * dec_of(n0 + t, j))
                e, g = r.ends[0, row_n(n0 + t), lane(j)], r.ends[1, row_n(n0 + t), lane(j)]
                x, y = e, g
                for h in range(1, H):
                    x = jnp.where(hidx == h, fac * pltpu.roll(x, 1, 0) + e, x)
                    y = jnp.where(hidx == H - 1 - h, fac * pltpu.roll(y, V - 1, 0) + g, y)
                a = jnp.where(hidx == t, turn(x, t - (H - 1)), a)
                b = jnp.where(hidx == t, turn(y, t), b)
            fw.append(a)
            bw.append(b)
        for i in range(0, len(fw), 2):
            band = slice(i * V, (i + 2) * V)
            r.epack[0, j, band, :] = jnp.concatenate(fw[i : i + 2], axis=0).astype(BF16)
            r.epack[1, j, band, :] = jnp.concatenate(bw[i : i + 2], axis=0).astype(BF16)
        out = []
        for k in range(1, S):
            ps, pf = net.at(k, 0)
            out.append(
                net.send(r.epack.at[jnp.where(ps > ms, 0, 1), j], r.eget.at[j, ms], ps, pf)
            )
        return out

    def turn(x, by):
        return x if by % V == 0 else pltpu.roll(x, by % V, 0)

    def begin(j, copies):
        for c in copies:
            c.wait()
        tiles = N // H
        dn = []
        for i in range(tiles):
            x = dec_of(i * H, j)
            for t in range(1, H):
                x = jnp.where(hidx == t, dec_of(i * H + t, j), x)
            dn.append(x)

        def join(p, acc):
            tot = r.totr[lax.rem(ms + S - p, S) - 1, :, lane(j)]
            e = r.eget[j, p].astype(F32)
            return tuple(jnp.exp2(tot * dn[i]) * acc[i] + e[row_n(i)] for i in range(tiles))

        zero = tuple(jnp.zeros((V, LN), F32) for _ in range(tiles))
        fw = lax.fori_loop(0, ms, join, zero)
        bw = lax.fori_loop(0, S - 1 - ms, lambda i, acc: join(S - 1 - i, acc), zero)
        one = r.sd[0:V, lane(j)]
        for i in range(tiles):
            for t in range(H):
                n = i * H + t
                fac = jnp.exp2(one * dec_of(n, j))
                x, y = turn(fw[i], -t), turn(bw[i], H - 1 - t)
                for h in range(1, H):
                    xn = pltpu.roll(fac * x + r.ends[0, row_n(n), lane(j)], 1, 0)
                    yn = pltpu.roll(fac * y + r.ends[1, row_n(n), lane(j)], V - 1, 0)
                    x = jnp.where(hidx == h, xn, x)
                    y = jnp.where(hidx == H - 1 - h, yn, y)
                r.start[0, row_n(n), lane(j)] = x
                r.start[1, row_n(n), lane(j)] = y

    def forward(j):
        dn = [dec_of(n, j) for n in range(N)]

        def ahead(q, hs):
            hs = list(hs)
            rows = pl.ds(pl.multiple_of(q * 2 * V, 2 * V), 2 * V)
            t, w = r.dtd[rows, lane(j)], r.u[rows, lane(j)]
            y = [jnp.zeros((V, LN), F32), jnp.zeros((V, LN), F32)]
            for n in range(N):
                b = r.bcb[rows, lane(n)].astype(F32)
                c = r.bcb[rows, lane(N + n)].astype(F32)
                keep = []
                for k, p in enumerate((TOP, BOT)):
                    m = jnp.exp2(t[p] * dn[n]) * hs[n]
                    hs[n] = m + w[p] * b[p]
                    y[k] = y[k] + c[p] * hs[n]
                    keep.append(m)
                r.m_s[j, rows, lane(n)] = jnp.concatenate(keep, axis=0).astype(BF16)
            r.y_s[rows, lane(j)] = jnp.concatenate(y, axis=0)
            return tuple(hs)

        lax.fori_loop(0, Q // 2, ahead, tuple(r.start[0, row_n(n), lane(j)] for n in range(N)))

    def backward(j):
        for n0 in range(0, N, half):
            dn = [dec_of(n, j) for n in range(n0, n0 + half)]

            def behind(i, carry, n0=n0, dn=dn):
                gs, gd = list(carry[0]), list(carry[1])
                rows = pl.ds(pl.multiple_of((Q - 2 - 2 * i) * V, 2 * V), 2 * V)
                t, w, g0 = r.dtd[rows, lane(j)], r.u[rows, lane(j)], r.gy[rows, lane(j)]
                t0 = jnp.where(t == RESET, 0.0, t)
                gu = [jnp.zeros((V, LN), F32), jnp.zeros((V, LN), F32)]
                gt = [jnp.zeros((V, LN), F32), jnp.zeros((V, LN), F32)]
                for i in range(half):
                    n = n0 + i
                    b = r.bcb[rows, lane(n)].astype(F32)
                    c = r.bcb[rows, lane(N + n)].astype(F32)
                    m = r.m_s[j, rows, lane(n)].astype(F32)
                    pc = g0 * (m + w * b)
                    pb = [None, None]
                    gc = g0 * c
                    for k, p in ((1, BOT), (0, TOP)):
                        g = gs[i] + gc[p]
                        pb[k] = g * w[p]
                        gu[k] = gu[k] + g * b[p]
                        x = g * m[p]
                        gt[k] = gt[k] + x * dn[i]
                        gd[i] = gd[i] + x * t0[p]
                        gs[i] = jnp.exp2(t[p] * dn[i]) * g
                    pb = jnp.concatenate(pb, axis=0)
                    if j > 0:
                        pb = pb + r.x_s[rows, lane(n)].astype(F32)
                        pc = pc + r.x_s[rows, lane(N + n)].astype(F32)
                    r.x_s[rows, lane(n)] = pb.astype(r.x_s.dtype)
                    r.x_s[rows, lane(N + n)] = pc.astype(r.x_s.dtype)
                gu, gt = jnp.concatenate(gu, axis=0), jnp.concatenate(gt, axis=0)
                if n0 > 0:
                    gu = gu + r.gsc[rows, lane(j)]
                    gt = gt + r.y_s[rows, lane(j)]
                r.gsc[rows, lane(j)] = gu
                r.y_s[rows, lane(j)] = gt
                return tuple(gs), tuple(gd)

            zero = tuple(jnp.zeros((V, LN), F32) for _ in range(half))
            first = tuple(r.start[1, row_n(n), lane(j)] for n in range(n0, n0 + half))
            _, gd = lax.fori_loop(0, Q // 2, behind, (first, zero))
            for i in range(half):
                dec = r.dec[n0 + i : n0 + i + 1, lane(j)] * (1.0 / LOG2E)
                r.rowsum[8 + n0 + i : 9 + n0 + i, lane(j)] = (
                    jnp.sum(gd[i], axis=0, keepdims=True) * dec
                )

    def gating(j):
        def body(i, sk):
            rows = pl.ds(pl.multiple_of(i * 64, 64), 64)
            x = r.inp[rows, lane(j)].astype(F32)
            mixed = r.y_s[rows, lane(j)] + r.cp[6:7, lane(j)] * x
            g = r.gate[rows, lane(j)]
            s = sigmoid(g)
            r.gated[rows, lane(j)] = (mixed * (g * s)).astype(BF16)
            r.ggate[rows, lane(j)] = (
                r.gg[rows, lane(j)] * mixed * s * (1.0 + g * (1.0 - s))
            ).astype(BF16)
            p = r.gy[rows, lane(j)] * x
            return sk + jnp.sum(p.reshape(8, V, LN), axis=0)

        sk = lax.fori_loop(0, T // 64, body, jnp.zeros((V, LN), F32))
        r.rowsum[6:7, lane(j)] = jnp.sum(sk, axis=0, keepdims=True)

    r.rowsum[...] = jnp.zeros_like(r.rowsum)
    states = [own_ends(j) for j in range(NB)]
    for c in tots:
        c.wait()
    for j in range(NB):
        begin(j, states[j])
        forward(j)
        gating(j)
        if 0 < j < NB - 1:
            backward(j - 1)
    late = list(range(max(NB - 2, 0), NB))

    def put(dst, first, res):
        n = dst.shape[2]
        for t in range(res.shape[0] // n):
            s = first // n + t
            dst[s % 2, s // 2] = res[t * n : (t + 1) * n].astype(dst.dtype)

    back0 = from_scan(d, 0)
    r.gatn[...] = dot(back0, r.ggate[0:T, :]).astype(BF16)
    for c in range(0, D, LN):
        put(r.giwg, c, dot(r.normed[0:T, c : c + LN], r.gatn[...], 0, 0))
    sum_g = Scatter(net, r.giwg, r.giwg_n, r.giwg_f)
    sum_g.first()
    for j in range(NB):
        put(r.gow, j * LN, dot(r.gated[0:T, lane(j)], r.big[0:T, :], 0, 0))
    sum_o = Scatter(net, r.gow, r.gow_n, r.gow_f)
    sum_o.first()
    r.gated[0:T, :] = dot(back0, r.gated[0:T, :]).astype(BF16)
    for c in range(0, D, 256):
        r.cot[:, c : c + 256] = dot(r.gated[0:T, :], r.ow[:, c : c + 256]).astype(BF16)
    outs = [net.send(rows_of(r.cot, net.at(0, k)[1], tok), r.outr.at[mf], *net.at(0, k)) for k in range(1, F)]
    outs.append(net.local(rows_of(r.cot, mf, tok), r.outr.at[mf]))
    for i, j in enumerate(late):
        backward(j)
        if i == 0:
            sum_g.second()
            sum_o.second()

    def finish(i, acc):
        rows = pl.ds(pl.multiple_of(i * 64, 64), 64)
        out = []
        for j in range(NB):
            x = r.inp[rows, lane(j)].astype(F32)
            z = r.dtpre[rows, lane(j)]
            gu = r.gsc[rows, lane(j)]
            gt = r.y_s[rows, lane(j)] * (1.0 / LOG2E) + gu * x
            dt = jnp.maximum(z, 0.0) + jnp.log1p(jnp.exp(-jnp.abs(z)))
            gz = gt * sigmoid(z)
            r.ggate[rows, lane(j)] = gz.astype(BF16)
            r.gsc[rows, lane(j)] = gu * dt + r.gy[rows, lane(j)] * r.cp[6:7, lane(j)]
            out.append(acc[j] + jnp.sum(gz.reshape(8, V, LN), axis=0))
        return tuple(out)

    db = lax.fori_loop(0, T // 64, finish, tuple(jnp.zeros((V, LN), F32) for _ in range(NB)))
    for j in range(NB):
        r.rowsum[5:6, lane(j)] = jnp.sum(db[j], axis=0, keepdims=True)
    r.gx[:, 0 : d.R] = dot(r.ggate[0:T, :], r.wdt[...]).astype(BF16)
    acc = jnp.zeros((T, 2 * N), F32)
    for n in range(0, 2 * N, 4):
        row = lax.div(lax.broadcasted_iota(jnp.int32, (4 * LN, 2 * N), 0), LN) + n
        col = lax.broadcasted_iota(jnp.int32, (4 * LN, 2 * N), 1)
        pick = jnp.where(row == col, 1.0, 0.0).astype(BF16)
        acc = acc + dot(r.x_s[:, n * LN : (n + 4) * LN].astype(BF16), pick)
    r.gx[:, d.R : W] = acc.astype(BF16)
    gxs = [net.send(r.gx, r.gxr.at[k - 1], *net.at(0, k)) for k in range(1, F)]

    def to_rows(total, out, keep):
        n = total.shape[0] // F
        for f in range(F):
            keep[f] = total[f * n : (f + 1) * n].astype(keep.dtype)
        cs = [net.send(keep.at[net.at(0, k)[1]], out.at[mf], *net.at(0, k)) for k in range(1, F)]
        return cs + [net.local(keep.at[mf], out.at[mf])]

    def to_home(total, keep, out):
        keep[...] = total.astype(keep.dtype)
        i = net.used
        net.used += 2
        far = pltpu.make_async_remote_copy(
            keep, out, r.ssem.at[i], r.rsem.at[i], {"seq": home_s, "fsdp": home_f}, device_id_type=MESH
        )
        near = pltpu.make_async_copy(keep, out, r.rsem.at[i + 1])

        @pl.when(moves)
        def _():
            far.start()

        @pl.when(jnp.logical_not(moves))
        def _():
            near.start()

        return far, near

    def home_wait(pair):
        @pl.when(moves)
        def _():
            pair[0].wait()

        @pl.when(jnp.logical_not(moves))
        def _():
            pair[1].wait()

    g_cs = to_rows(sum_g.total(), r.o_wg, r.k_wg)
    o_cs = to_home(sum_o.total(), r.k_out, r.o_out)
    gwdt = dot(r.ggate[0:T, :], r.xd[:, 0 : d.R], 0, 0)

    for c in gxs:
        c.wait()
    s = r.gx[:, 0:W].astype(F32)
    for k in range(F - 1):
        s = s + r.gxr[k, :, 0:W].astype(F32)
    gxd = s.astype(BF16)
    pad = HG * V
    r.gg[0:pad, :] = jnp.zeros((pad, CL), F32)
    r.gg[pad + T :, :] = jnp.zeros((pad, CL), F32)
    for c in range(0, CL, 256):
        r.gg[pad : pad + T, c : c + 256] = r.gsc[:, c : c + 256] + dot(gxd, r.xp[c : c + 256, :], 1, 1)

    def act(i, acc):
        r0 = pl.multiple_of(i * 64, 64)
        rows = pl.ds(r0, 64)
        shift = pl.ds(pl.multiple_of(r0 + pad, V), 64)
        age = r.rel[shift, :]
        out = []
        for j in range(NB):
            p = r.pre[rows, lane(j)]
            q = sigmoid(p)
            g = r.gg[shift, lane(j)] * q * (1.0 + p * (1.0 - q))
            r.gg[shift, lane(j)] = g
            a = list(acc[j])
            a[4] = a[4] + jnp.sum(g.reshape(8, V, LN), axis=0)
            for k in range(d.K):
                back = d.K - 1 - k
                xs = r.xb[pl.ds(pl.multiple_of(r0 + (HG - back) * V, V), 64), lane(j)]
                t = jnp.where(age >= back, g * xs, 0.0)
                a[k] = a[k] + jnp.sum(t.reshape(8, V, LN), axis=0)
            out.append(tuple(a))
        return tuple(out)

    zero = tuple(tuple(jnp.zeros((V, LN), F32) for _ in range(5)) for _ in range(NB))
    acc = lax.fori_loop(0, T // 64, act, zero)
    for j in range(NB):
        for k in range(5):
            r.rowsum[k : k + 1, lane(j)] = jnp.sum(acc[j][k], axis=0, keepdims=True)

    def gather_taps(i, _):
        r0 = pl.multiple_of(i * 32, 32)
        for j in range(NB):
            acc = jnp.zeros((32, LN), F32)
            for k in range(d.K):
                back = d.K - 1 - k
                src = pl.ds(pl.multiple_of(r0 + back * V, V), 32)
                acc = acc + jnp.where(
                    r.rel[src, :] >= back, r.gg[src, lane(j)] * r.cp[k : k + 1, lane(j)], 0.0
                )
            r.gated[pl.ds(r0, 32), lane(j)] = acc.astype(BF16)
        return 0

    lax.fori_loop(0, d.TE // 32, gather_taps, 0)
    r.ggate[...] = dot(from_scan(d, HG), r.gated[...]).astype(BF16)
    for c in range(0, D, LN):
        put(r.giwx, c, dot(r.normed[:, c : c + LN], r.ggate[...], 0, 0))
    sum_x = Scatter(net, r.giwx, r.giwx_n, r.giwx_f)
    sum_x.first()
    r.y_s[0:CL, 0:LN] = r.rowsum[...].T
    r.y_s[0:CL, LN : LN + W] = dot(r.inp[...], gxd, 0, 0)
    r.y_s[0:CL, LN + W : 2 * LN] = jnp.zeros((CL, LN - W), F32)
    r.y_s[0:CL, 32 : 32 + d.R] = gwdt
    put(r.small, 0, r.y_s[0:CL, 0 : 2 * LN])
    sum_s = Scatter(net, r.small, r.small_n, r.small_f)
    sum_s.first()
    for c in range(0, D, 256):
        g = dot(r.ggate[...], r.w[0, c : c + 256, :], 1, 1)
        r.hid[0:T, c : c + 256] = (
            g[0:T] + dot(r.gatn[...], r.w[1, c : c + 256, :], 1, 1)
        ).astype(BF16)
        r.hid[T:, c : c + 256] = g[T:].astype(BF16)
    gns = [
        net.send(rows_of(r.hid, net.at(0, k)[1], tok), rows_of(r.o_gn, mf, tok), *net.at(0, k))
        for k in range(1, F)
    ]
    gns.append(net.local(rows_of(r.hid, mf, tok), rows_of(r.o_gn, mf, tok)))
    for k in range(F):
        ps, pf = net.at(-1, k)
        gns.append(
            net.send(
                r.hid.at[pl.ds(T + pf * TAIL, TAIL)], r.o_gn.at[pl.ds(T + mf * TAIL, TAIL)], ps, pf
            )
        )
    sum_x.second()
    sum_s.second()

    def gains(i, acc):
        rows = pl.ds(pl.multiple_of(i * 64, 64), 64)
        t = r.hid[rows, :].astype(F32) * r.normed[rows, :].astype(F32)
        return acc + jnp.sum(t.reshape(8, V, D), axis=0)

    gtot = lax.fori_loop(0, d.NAT // 64, gains, jnp.zeros((V, D), F32)) / r.gain[...]
    n = D // S
    for s in range(S):
        r.gg8[s % 2, s // 2] = gtot[:, s * n : (s + 1) * n]
    sum_n = Scatter(net, r.gg8, r.gg8_n, r.gg8_f)
    sum_n.first()
    sum_n.second()
    x_cs = to_rows(sum_x.total(), r.o_wx, r.k_wx)
    s_cs = to_home(sum_s.total(), r.k_small, r.o_small)
    r.k_gain[...] = sum_n.total()
    n_cs = [net.send(r.k_gain, r.o_gain.at[mf], *net.at(0, k)) for k in range(1, F)]
    n_cs.append(net.local(r.k_gain, r.o_gain.at[mf]))
    net.drain()
    home_wait(o_cs)
    home_wait(s_cs)


def close(d, gn, outr, hid, cot, gain, wx, wg, out, small, ggain,
          o_out, o_hid, o_gain, o_in, o_conv, o_rows, o_xp, o_dt, o_al, o_gout):
    F, T, tok, D = d.F, d.T, d.tok, d.D
    W = d.R + 2 * d.N

    def rows_(i, _):
        rows = pl.ds(pl.multiple_of(i * 16, 16), 16)
        h = hid[rows, :].astype(F32)
        g = gn[pl.ds(pl.multiple_of(i * 16, 16), 16), :].astype(F32)
        o = outr[0, rows, :].astype(F32)
        for f in range(1, F):
            g = g + gn[pl.ds(pl.multiple_of(f * tok + i * 16, 16), 16), :].astype(F32)
            o = o + outr[f, rows, :].astype(F32)
        late = jnp.zeros((TAIL, D), F32)
        for f in range(F):
            late = late + gn[T + f * TAIL : T + (f + 1) * TAIL, :].astype(F32)
        g = g + jnp.where(i == tok // 16 - 1, late, 0.0)
        inv = lax.rsqrt(jnp.mean(h * h, axis=-1, keepdims=True) + EPS)
        g2 = g * gain[...]
        mean = jnp.mean(g2 * h, axis=-1, keepdims=True)
        o_hid[0, rows, :] = cot[rows, :].astype(F32) + inv * g2 - h * (inv * inv * inv) * mean
        o_out[0, rows, :] = (h + o).astype(BF16)
        return 0

    lax.fori_loop(0, tok // 16, rows_, 0)
    for f in range(F):
        o_in[:, f * d.CL : (f + 1) * d.CL] = wx[f].astype(F32)
        o_in[:, d.DI + f * d.CL : d.DI + (f + 1) * d.CL] = wg[f].astype(F32)
    o_gout[...] = out[...].astype(F32)
    sm = small[...]
    o_conv[...] = sm[:, 0 : d.K]
    o_al[...] = sm[:, V : V + d.N]
    o_dt[...] = sm[:, 32 : 32 + d.R]
    o_xp[...] = sm[:, LN : LN + W]
    o_rows[...] = sm[:, 0:LN].T[0:V, :]
    tot = ggain[0]
    for f in range(1, F):
        tot = tot + ggain[f]
    n, k = D // d.S, D // d.S // F
    row = lax.broadcasted_iota(jnp.int32, (n, k), 0) - lax.axis_index("fsdp") * k
    pick = jnp.where(row == lax.broadcasted_iota(jnp.int32, (n, k), 1), 1.0, 0.0)
    one = lax.dot_general(
        jnp.sum(tot, axis=0, keepdims=True) + jnp.zeros((V, n), F32), pick, (((1,), (0,)), ((), ())),
        precision=lax.Precision.HIGHEST, preferred_element_type=F32,
    )
    o_gain[...] = one[0:1, :]


def vm(*shape, dtype=F32):
    return pltpu.VMEM(shape, dtype)


def per_device(
    d, hidden, cluster_lengths, norm_gain, in_weight, conv_weight, conv_bias, xproj_weight,
    dt_weight, dt_bias, a_log, skip, out_weight, cotangent,
):
    S, F, T, D, CL, N, NB, R = d.S, d.F, d.T, d.D, d.CL, d.N, d.NB, d.R
    wide = lambda a: jnp.pad(a.astype(F32), (0, CL - a.shape[0]))
    params = jnp.stack(
        [conv_bias.astype(F32), dt_bias.astype(F32), skip.astype(F32), wide(norm_gain),
         wide(cluster_lengths[0])] + [jnp.zeros((CL,), F32)] * (V - 5)
    )
    ins = dict(
        hidden=hidden[0], params=params, in_weight=in_weight, conv_weight=conv_weight,
        xproj_weight=xproj_weight, dt_weight=dt_weight, a_log=a_log, out_weight=out_weight,
        cotangent=cotangent[0],
    )
    DS, CS, W, W2 = D // S, CL // S, R + 2 * N, 2 * LN
    TP = T + 2 * HG * V
    outs = dict(
        o_gn=((d.NAT, D), BF16), outr=((F, d.tok, D), BF16), gain=((1, D), F32),
        o_wx=((F, DS // F, CL), BF16), o_wg=((F, DS // F, CL), BF16), o_out=((CS, D), F32),
        o_small=((CS, W2), F32), o_gain=((F, V, DS), F32),
    )
    rt = BF16 if CS >= 16 else F32
    small_t = T <= 512
    half = S // 2
    EP = N // d.H * V
    scratch = dict(
        hid=((d.NAT, D), BF16), normed=((d.NAT, D), BF16), big=((d.TE, D), BF16),
        cot=((T, D), BF16), w=((2, D, CL), BF16), ow=((CL, D), BF16),
        xp=((CL, W), BF16), wdt=((CL, R), BF16), cw=((CL, d.K), BF16), al=((CL, N), BF16),
        pg=((F, V, CL), F32), cp=((V, CL), F32), dec=((N, CL), F32), rel=((TP, LN), F32),
        xb=((d.TE, CL), F32), gate=((T, CL), F32), pre=((T, CL), F32), inp=((T, CL), BF16),
        xd=((T, LN), BF16), xdr=((F - 1, T, LN), BF16),
        dtpre=((T, CL), F32), dtd=((T, CL), F32), u=((T, CL), F32), gg=((TP, CL), F32),
        gy=((T, CL), F32), bcb=((T, 2 * N * LN), F32 if small_t else BF16),
        sd=((V, CL), F32), tot=((V, CL), F32), totr=((S - 1, V, CL), F32),
        ends=((2, N * V, CL), F32), epack=((2, NB, EP, LN), BF16), eget=((NB, S, EP, LN), BF16),
        start=((2, N * V, CL), F32), m_s=((NB, T, N * LN), BF16), y_s=((T, CL), F32),
        gsc=((T, CL), F32), x_s=((T, 2 * N * LN), F32 if small_t else BF16),
        gated=((d.TE, CL), BF16), ggate=((d.NAT, CL), BF16), gatn=((T, CL), BF16),
        gx=((T, LN), BF16), gxr=((F - 1, T, LN), BF16), rowsum=((LN, CL), F32),

        giwg=((2, half, DS, CL), BF16), giwg_n=((half, DS, CL), BF16), giwg_f=((half - 1, DS, CL), BF16),
        giwx=((2, half, DS, CL), BF16), giwx_n=((half, DS, CL), BF16), giwx_f=((half - 1, DS, CL), BF16),
        gow=((2, half, CS, D), rt), gow_n=((half, CS, D), rt), gow_f=((half - 1, CS, D), rt),
        small=((2, half, CS, W2), rt), small_n=((half, CS, W2), rt), small_f=((half - 1, CS, W2), rt),
        gg8=((2, half, V, DS), F32), gg8_n=((half, V, DS), F32), gg8_f=((half - 1, V, DS), F32),
        k_wg=((F, DS // F, CL), BF16), k_wx=((F, DS // F, CL), BF16), k_out=((CS, D), F32),
        k_small=((CS, W2), F32), k_gain=((V, DS), F32),
    )
    names = list(ins) + list(outs) + list(scratch) + ["ssem", "rsem"]
    sems = 160 + (NB + 6) * S + 12 * F
    res = pl.pallas_call(
        functools.partial(layer, d, names),
        out_shape=[jax.ShapeDtypeStruct(*o) for o in outs.values()],
        in_specs=[pl.BlockSpec(memory_space=pl.ANY)] * len(ins),
        out_specs=[
            pl.BlockSpec(memory_space=pltpu.VMEM if k == "gain" else pl.ANY) for k in outs
        ],
        scratch_shapes=[vm(*s, dtype=t) for s, t in scratch.values()]
        + [pltpu.SemaphoreType.DMA((sems,)), pltpu.SemaphoreType.DMA((sems,))],
        compiler_params=pltpu.CompilerParams(
            collective_id=0, has_side_effects=True, vmem_limit_bytes=65250 * 1024
        ),
    )(*ins.values())
    o = dict(zip(outs, res))
    fin = kernel(
        functools.partial(close, d),
        (o["o_gn"], o["outr"], hidden[0], cotangent[0], o["gain"], o["o_wx"], o["o_wg"], o["o_out"],
         o["o_small"], o["o_gain"]),
        [((1, d.tok, D), BF16), ((1, d.tok, D), F32), ((1, DS // F), F32), ((DS // F, 2 * d.DI), F32),
         ((CS, d.K), F32), ((V, CS), F32), ((CS, W), F32), ((CS, R), F32), ((CS, N), F32), ((CS, D), F32)],
    )
    out, g_hid, g_gain, g_in, g_conv, rows, g_xp, g_dt, g_al, g_out = fin
    return (
        out, g_hid, g_gain[0], g_in, g_conv, rows[4], g_xp, g_dt, rows[5], g_al, rows[6], g_out,
    )


def solution(mesh):
    S, F = mesh.shape["seq"], mesh.shape["fsdp"]

    def run(*args):
        tok, D = args[0].shape[1] // S, args[0].shape[2]
        d = Dims(
            S, F, tok, D, args[11].shape[0], args[9].shape[1], args[7].shape[1], args[4].shape[1],
            args[1].shape[1],
        )
        return jax.shard_map(
            functools.partial(per_device, d),
            mesh=mesh,
            in_specs=(
                P("fsdp", "seq", None), P("fsdp", None), P("fsdp"), P("fsdp", None),
                P("fsdp", None), P("fsdp"), P("fsdp", None), P("fsdp", None), P("fsdp"),
                P("fsdp", None), P("fsdp"), P("fsdp", None), P("fsdp", "seq", None),
            ),
            out_specs=(
                P("fsdp", "seq", None), P("fsdp", "seq", None), P(("seq", "fsdp")),
                P(("seq", "fsdp"), None), P(("seq", "fsdp"), None), P(("seq", "fsdp")),
                P(("seq", "fsdp"), None), P(("seq", "fsdp"), None), P(("seq", "fsdp")),
                P(("seq", "fsdp"), None), P(("seq", "fsdp")), P(("seq", "fsdp"), None),
            ),
            check_vma=False,
        )(*args)

    return run
```

time: 315 us -> 165 us (0.52)
  Pallas kernels: 274 us -> 150 us
  other arithmetic: 20.2 us -> 3.36 us
  local copies, waits for them, and re-layouts: 18.9 us -> 11 us
    pallas_call x4 -> x1, Pallas kernels: 79.1 us -> 4.17 us  [kernel(): pl.pallas_call(body, out_shape=[jax.ShapeDtypeStruct(s, t) for s, t in ou...]
    pallas_call x6 -> x1, Pallas kernels: 194 us -> 145 us  [per_device(): pl.pallas_call(functools.partial(layer, d, names), out_shape=[jax.ShapeDt...]
    convert_element_type x7 -> x1, other arithmetic: 9.09 us -> 0.66 us  [per_device(): wide = lambda a: jnp.pad(a.astype(F32), (0, CL - a.shape[0]))]
    reduce_sum x10 -> x0, other arithmetic: 8.1 us -> none  [the longest x9 7.92 us: per_device(): add = lambda a: jnp.sum(a.astype(F32), axis=0)]
    slice x10 -> x0, local copies, waits for them, and re-layouts: 6.51 us -> none  [the longest x1 1.35 us: per_device(): gain = gains[:, 0, :].reshape(1, D)]
    unnamed x20 -> x6, local copies, waits for them, and re-layouts: 4.01 us -> 9.05 us
    reshape x7 -> x0, local copies, waits for them, and re-layouts: 4.57 us -> none  [the longest x3 2.05 us: per_device(): cp = jnp.concatenate([r.astype(F32).reshape(-1, CL) for r in rows], axis=0)]
  transfers between devices with their start and end apart: 1 -> 0, of which waited for: 0 -> 0; matrix products, arithmetic and copies ran while one was open for 4% -> 0% of each run, Pallas kernels for 3% -> 0%
where the time goes in v2:
time: 165 us
  Pallas kernels  150 us (91%)
  local copies, waits for them, and re-layouts  11 us (7%)
  other arithmetic  3.36 us (2%)
    pallas_call x1, Pallas kernels, per_device(): pl.pallas_call(functools.partial(layer, d, names), out_shape=[jax.ShapeDt...  145 us
    unnamed x6, local copies, waits for them, and re-layouts  9.05 us
    pallas_call x1, Pallas kernels, kernel(): pl.pallas_call(body, out_shape=[jax.ShapeDtypeStruct(s, t) for s, t in ou...  4.17 us

profile of v2, /device:TPU:0, one launch (start us, length us, event | category | flops | bytes accessed | tf_op | source)
XLA Modules:
  0.0 164.6 jit_solution(17440161550756852867)
XLA Ops:
  0.6 0.7 convert_bitcast_fusion
  1.3 0.7 pad_convert_fusion
  2.0 0.7 stack.44
  2.6 0.7 stack.45
  3.3 0.7 stack.46
  4.0 0.6 stack.43.refs_1_
  4.6 1.5 copy.25.refs_3_
  6.1 1.7 %copy.26.refs_4_ = bf16[512,96]{1,0:T(8,128)(2,1)} copy(bf16[512,96]{0,1:T(8,128)(2,1)} %param.19) | data formatting | bytes 196608 | tf_op args[6]
  7.8 1.6 copy.27.refs_5_
  9.4 1.5 copy.28.refs_6_
  10.9 145.4 %shard_map.220 = (bf16[576,1024]{1,0:T(8,128)(2,1)}, bf16[4,128,1024]{2,1,0:T(8,128)(2,1)}, f32[1,1024]{1,0:T(1,128)}, bf16[4,32,512]{2,1,0:T(8,128)(2,1)}, bf16...) custom-call(bf16[128,1024]{1,0:T(8,128)(2,1)} %bitcast.16, ...), custom_call_target="tpu_custom_call" | custom-call | tf_op jit(solution)/shard_map/pallas_call | solution.py:932
  156.3 4.2 %shard_map.221 = (bf16[1,128,1024]{2,1,0:T(8,128)(2,1)}, f32[1,128,1024]{2,1,0:T(8,128)}, f32[1,32]{1,0:T(1,128)}, f32[32,4096]{1,0:T(8,128)}, f32[64,4]{1,0:T(8...) custom-call(bf16[576,1024]{1,0:T(8,128)(2,1)} %get-tuple-element.30., ...), custom_call_target="tpu_custom_call" | custom-call | tf_op jit(solution)/shard_map/pallas_call | solution.py:46
  160.5 1.3 slice_bitcast_fusion
  161.8 1.4 copy.29
  163.2 1.4 copy.30
  (3 shorter events, 0.0 us)

commit v3 on v2

--- a/solution.py
+++ b/solution.py
@@ -106,14 +106,39 @@
         self.wait_recv()
 
 
+class Batch:
+    def __init__(self, net, sends, whole):
+        i, j = net.pair()
+        self.open = True
+        for src, dst, ps, pf in sends:
+            net.remote(src, dst, i, j, ps, pf).start()
+        self.all = net.remote(whole, whole, i, j, *net.at(0, 1))
+
+    def wait(self):
+        if self.open:
+            self.all.wait_send()
+            self.all.wait_recv()
+            self.open = False
+
+
 class Net:
     def __init__(self, d, ssem, rsem):
-        self.d, self.ssem, self.rsem, self.used = d, ssem, rsem, 0
+        self.d, self.ssem, self.rsem, self.s_used, self.r_used = d, ssem, rsem, 0, 0
         self.ms, self.mf = lax.axis_index("seq"), lax.axis_index("fsdp")
         self.open = []
 
     def at(self, ds, df):
         return lax.rem(self.ms + ds % self.d.S, self.d.S), lax.rem(self.mf + df % self.d.F, self.d.F)
+
+    def pair(self):
+        self.s_used += 1
+        self.r_used += 1
+        return self.s_used - 1, self.r_used - 1
+
+    def remote(self, src, dst, i, j, ps, pf):
+        return pltpu.make_async_remote_copy(
+            src, dst, self.ssem.at[i], self.rsem.at[j], {"seq": ps, "fsdp": pf}, device_id_type=MESH
+        )
 
     def start(self, copy, remote):
         copy.start()
@@ -121,19 +146,16 @@
         return self.open[-1]
 
     def send(self, src, dst, ps, pf):
-        i = self.used
-        self.used += 1
-        return self.start(
-            pltpu.make_async_remote_copy(
-                src, dst, self.ssem.at[i], self.rsem.at[i], {"seq": ps, "fsdp": pf}, device_id_type=MESH
-            ),
-            True,
-        )
+        i, j = self.pair()
+        return self.start(self.remote(src, dst, i, j, ps, pf), True)
+
+    def batch(self, sends, whole):
+        self.open.append(Batch(self, sends, whole))
+        return self.open[-1]
 
     def local(self, src, dst):
-        i = self.used
-        self.used += 1
-        return self.start(pltpu.make_async_copy(src, dst, self.rsem.at[i]), False)
+        self.r_used += 1
+        return self.start(pltpu.make_async_copy(src, dst, self.rsem.at[self.r_used - 1]), False)
 
     def drain(self):
         for c in self.open:
@@ -141,39 +163,66 @@
 
 
 class Scatter:
-    def __init__(self, net, mine, near, far):
-        self.net, self.mine, self.near, self.far = net, mine, near, far
+    def __init__(self, net, mine, near, out, spread, split=True):
+        self.net, self.mine, self.near, self.out_ref = net, mine, near, out
+        self.spread, self.split = spread, split
         d = net.d
         self.half = d.S // 2
         self.x, self.z = lax.rem(net.ms, 2), lax.div(net.ms, 2)
         self.pal = net.ms + 1 - 2 * self.x
         self.order = [lax.rem(self.z + k, self.half) for k in list(range(1, self.half)) + [0]]
-        self.out, self.ins = [], []
-
-    def first(self):
-        for z in self.order:
-            self.out.append(
-                self.net.send(self.mine.at[1 - self.x, z], self.near.at[z], self.pal, self.net.mf)
-            )
-
-    def second(self):
-        for k, z in enumerate(self.order):
-            self.out[k].wait()
+        self.first = [
+            net.send(mine.at[1 - self.x, z], near.at[z], self.pal, net.mf) for z in self.order
+        ]
+        self.done, self.tails = 0, []
+        self.into = net.r_used
+        net.r_used += 1
+        net.open.append(self)
+
+    def step(self, upto=None):
+        net, d = self.net, self.net.d
+        upto = self.half if upto is None else upto
+        while self.done < upto:
+            k, z = self.done, self.order[self.done]
+            self.done += 1
+            self.first[k].wait()
             both = self.mine[self.x, z].astype(F32) + self.near[z].astype(F32)
             self.mine[self.x, z] = both.astype(self.mine.dtype)
-            if k < self.half - 1:
-                self.ins.append(
-                    self.net.send(
-                        self.mine.at[self.x, z], self.far.at[k], z * 2 + self.x, self.net.mf
-                    )
-                )
-
-    def total(self):
-        acc = self.mine[self.x, self.z].astype(F32)
-        for k, c in enumerate(self.ins):
-            c.wait()
-            acc = acc + self.far[k].astype(F32)
-        return acc
+            i = net.s_used
+            net.s_used += 1
+            if self.spread:
+                last = k == self.half - 1
+                for g in range(1, d.F + (0 if last else 1)):
+                    f = lax.rem(net.mf + g, d.F)
+                    src = self.mine.at[self.x, z, f] if self.split else self.mine.at[self.x, z]
+                    net.remote(
+                        src, self.out_ref.at[k, net.mf], i, self.into, z * 2 + self.x, f
+                    ).start()
+                if last:
+                    src = self.mine.at[self.x, z, net.mf] if self.split else self.mine.at[self.x, z]
+                    pltpu.make_async_copy(
+                        src, self.out_ref.at[k, net.mf], net.rsem.at[self.into]
+                    ).start()
+                sent = self.out_ref.at[k, pl.ds(0, d.F - 1)] if last else self.out_ref.at[k]
+                self.tails.append((None, net.remote(sent, sent, i, self.into, *net.at(0, 1))))
+            else:
+                spot = net.mf * d.S + z * 2 + self.x
+                away = spot != net.ms * d.F + net.mf
+                src, dst = self.mine.at[self.x, z], self.out_ref.at[self.z]
+                far = net.remote(src, dst, i, self.into, lax.div(spot, d.F), lax.rem(spot, d.F))
+                near = pltpu.make_async_copy(src, dst, net.rsem.at[self.into])
+                pl.when(away)(far.start)
+                pl.when(jnp.logical_not(away))(near.start)
+                self.tails.append((away, far))
+
+    def wait(self):
+        for away, c in self.tails:
+            if away is None:
+                c.wait_send()
+            else:
+                pl.when(away)(c.wait_send)
+        net = self.net
+        net.remote(self.out_ref, self.out_ref, 0, self.into, *net.at(0, 1)).wait_recv()
 
 
 def layer(d, names, *refs):
@@ -184,31 +233,16 @@
     DF = D // F
     net = Net(d, r.ssem, r.rsem)
     ms, mf = net.ms, net.mf
-    x_bit = lax.rem(ms, 2)
-    pal = ms + 1 - 2 * x_bit
     core = mf + 1 - 2 * lax.rem(mf, 2)
-    spot = mf * S + ms
-    home_s, home_f = lax.div(spot, F), lax.rem(spot, F)
-    mine = ms * F + mf
-    from_s, from_f = lax.rem(mine, S), lax.div(mine, S)
-    moves = spot != mine
-    greet = {(0, k) for k in range(F)} | {(k, 0) for k in range(S)}
-    greet |= {(k % S, g) for k in (1, -1) for g in range(F)}
-    greet = sorted(greet - {(0, 0)})
+    greet = [(i, k) for i in range(S) for k in range(F) if (i, k) != (0, 0)]
     bar = pltpu.get_barrier_semaphore()
     for ds, df in greet:
         ps, pf = net.at(-ds, -df)
         pl.semaphore_signal(bar, inc=1, device_id={"seq": ps, "fsdp": pf}, device_id_type=MESH)
 
-    @pl.when(moves)
-    def _():
-        pl.semaphore_signal(
-            bar, inc=1, device_id={"seq": from_s, "fsdp": from_f}, device_id_type=MESH
-        )
-
     own = [
         net.local(r.hidden, r.hid.at[pl.ds(mf * tok, tok)]),
-        net.local(r.params, r.pg.at[mf]),
+        net.local(r.norm_gain, r.row_g),
         net.local(r.in_weight.at[:, pl.ds(pl.multiple_of(mf * CL, LN), CL)], r.w.at[0, pl.ds(mf * DF, DF)]),
         net.local(
             r.in_weight.at[:, pl.ds(pl.multiple_of(d.DI + mf * CL, LN), CL)],
@@ -220,12 +254,23 @@
         net.local(r.dt_weight, r.wdt),
         net.local(r.conv_weight, r.cw),
         net.local(r.a_log, r.al),
+        net.local(r.lens, r.row_l),
+        net.local(r.conv_bias, r.row_cb),
+        net.local(r.dt_bias, r.row_db),
+        net.local(r.skip, r.row_sk),
     ]
-    pl.semaphore_wait(bar, len(greet) + moves.astype(jnp.int32))
+    pl.semaphore_wait(bar, len(greet))
 
     rows_of = lambda ref, f, n: ref.at[pl.ds(f * n, n)]
     same_core = [lax.rem(mf + 2 * k, F) for k in range(1, F // 2)]
     other_chip = [(lax.rem(mf + 2 * k, F), lax.rem(core + 2 * k, F)) for k in range(1, F // 2)]
+
+    for i in (1, 10):
+        own[i].wait()
+    as_row = lambda ref: ref[...].astype(F32).reshape(1, ref.shape[-1])
+    r.pg_own[0:1, :] = as_row(r.row_g)
+    r.pg_own[1:2, 0 : d.clusters] = as_row(r.row_l)
+    r.pg[mf] = r.pg_own[...]
 
     def spread_rows(src, dst):
         direct = [net.send(src, rows_of(dst, mf, tok), ms, f) for f in same_core]
@@ -238,7 +283,42 @@
             f = lax.rem(mf + F - 2 * (k + 1), F)
             beside.append(net.send(rows_of(dst, f, tok), rows_of(dst, f, tok), ms, core))
 
-    pgs = [net.send(r.params, r.pg.at[mf], ms, net.at(0, k)[1]) for k in range(1, F)]
+    def w_slice(g, f):
+        return r.in_weight.at[:, pl.ds(pl.multiple_of(g * d.DI + f * CL, LN), CL)]
+
+    quart, ring = lax.rem(ms, 4), ms - lax.rem(ms, 4)
+    QF = DF // 4
+
+    def w_far(g):
+        out = []
+        for pair in other_chip:
+            for f in pair:
+                src = r.in_weight.at[
+                    pl.ds(quart * QF, QF), pl.ds(pl.multiple_of(g * d.DI + f * CL, LN), CL)
+                ]
+                out.append(net.send(src, r.w.at[g, pl.ds(mf * DF + quart * QF, QF)], ms, f))
+        return out
+
+    def w_relay(g, far):
+        out = []
+        i = 0
+        for k in range(1, F // 2):
+            for flip in (0, 1):
+                far[i].wait_recv()
+                i += 1
+                f0 = lax.rem(mf + F - 2 * k, F)
+                if flip:
+                    f0 = f0 + 1 - 2 * lax.rem(f0, 2)
+                place = r.w.at[g, pl.ds(f0 * DF + quart * QF, QF)]
+                for t in (1, 2, 3):
+                    out.append(net.send(place, place, ring + lax.rem(quart + t, 4), mf))
+        return out
+
+    wx_far = w_far(0)
+    pgs = [net.send(r.pg_own, r.pg.at[mf], *net.at(0, k)) for k in range(1, F)]
+    w_beside = [net.send(w_slice(g, core), r.w.at[g, pl.ds(mf * DF, DF)], ms, core) for g in (0, 1)]
+    for c in wx_far:
+        c.wait_send()
     h_direct, h_beside = spread_rows(r.hidden, r.hid)
     halo = [
         net.send(
@@ -248,56 +328,18 @@
         )
         for k in range(F)
     ]
-
-    def w_slice(g, f):
-        return r.in_weight.at[:, pl.ds(pl.multiple_of(g * d.DI + f * CL, LN), CL)]
-
-    w_beside = [net.send(w_slice(g, core), r.w.at[g, pl.ds(mf * DF, DF)], ms, core) for g in (0, 1)]
-    HF = DF // 2
-
-    def w_far(g):
-        out = []
-        for pair in other_chip:
-            for f in pair:
-                src = r.in_weight.at[
-                    pl.ds(x_bit * HF, HF), pl.ds(pl.multiple_of(g * d.DI + f * CL, LN), CL)
-                ]
-                out.append(net.send(src, r.w.at[g, pl.ds(mf * DF + x_bit * HF, HF)], ms, f))
-        return out
-
-    def w_relay(g, far):
-        out = []
-        i = 0
-        for k in range(1, F // 2):
-            for flip in (0, 1):
-                far[i].wait()
-                i += 1
-                f0 = lax.rem(mf + F - 2 * k, F)
-                if flip:
-                    f0 = f0 + 1 - 2 * lax.rem(f0, 2)
-                place = r.w.at[g, pl.ds(f0 * DF + x_bit * HF, HF)]
-                out.append(net.send(place, place, pal, mf))
-        return out
-
-    back0 = from_scan(d, 0)
-    for c in h_direct:
-        c.wait_send()
-    wx_far = w_far(0)
-    for k, c in enumerate(h_direct):
-        c.wait_recv()
-        f = lax.rem(mf + F - 2 * (k + 1), F)
-        h_beside.append(net.send(rows_of(r.hid, f, tok), rows_of(r.hid, f, tok), ms, core))
-    for c in pgs + own[:2]:
+    wx_near = w_relay(0, wx_far)
+    for c in pgs + own[:1]:
         c.wait()
     for f in range(F):
-        r.gain[0:1, f * DF : (f + 1) * DF] = r.pg[f, 3:4, 0:DF]
+        r.gain[0:1, f * DF : (f + 1) * DF] = r.pg[f, 0:1, :]
     sub = lax.broadcasted_iota(jnp.int32, (V, LN), 0)
     hidx = lax.rem(sub, H)
     stream = lax.div(sub, H)
     offs, run = [], jnp.zeros((V, LN), F32)
     for j in range(d.clusters - 1):
         for f in range(F):
-            run = run + jnp.where(stream == f, r.pg[f, 4:5, j : j + 1], 0.0)
+            run = run + jnp.where(stream == f, r.pg[f, 1:2, j : j + 1], 0.0)
         offs.append(run)
     base = ms * tok + hidx * Q
     r.rel[0 : HG * V, :] = jnp.zeros((HG * V, LN), F32)
@@ -312,14 +354,19 @@
         return 0
 
     lax.fori_loop(0, Q, mark, 0)
-    own[8].wait()
-    own[9].wait()
-    eye = lambda n: jnp.where(
-        lax.broadcasted_iota(jnp.int32, (n, n), 0) == lax.broadcasted_iota(jnp.int32, (n, n), 1), 1.0, 0.0
-    ).astype(BF16)
-    r.cp[0 : d.K, :] = dot(eye(d.K), r.cw[...], 1, 1)
-    r.cp[4:7, :] = r.pg[mf, 0:3, :]
-    r.dec[...] = -LOG2E * jnp.exp(dot(eye(N), r.al[...], 1, 1))
+    for c in own[8:]:
+        c.wait()
+    r.cp[0 : d.K, :] = r.cw[...].astype(F32)
+    for i, ref in enumerate((r.row_cb, r.row_db, r.row_sk)):
+        r.cp[4 + i : 5 + i, :] = as_row(ref)
+    r.dec[...] = -LOG2E * jnp.exp(r.al[...].astype(F32))
+    for c in h_direct:
+        c.wait_send()
+    c_direct, c_beside = spread_rows(r.cotangent, r.cot)
+    for k, c in enumerate(h_direct):
+        c.wait_recv()
+        f = lax.rem(mf + F - 2 * (k + 1), F)
+        h_beside.append(net.send(rows_of(r.hid, f, tok), rows_of(r.hid, f, tok), ms, core))
     for c in h_beside + halo:
         c.wait()
 
@@ -334,9 +381,7 @@
     perm = to_scan(d, HG)
     for c in range(0, D, 256):
         r.big[:, c : c + 256] = dot(perm, r.normed[:, c : c + 256]).astype(BF16)
-    wx_near = w_relay(0, wx_far)
     wg_far = w_far(1)
-    c_direct, c_beside = spread_rows(r.cotangent, r.cot)
     own[2].wait()
     w_beside[0].wait()
     for c in wx_near:
@@ -363,8 +408,22 @@
     lax.fori_loop(0, T // 64, conv, 0)
     own[6].wait()
     W = d.R + 2 * N
-    r.xd[:, 0:W] = dot(r.inp[...], r.xp[...]).astype(BF16)
-    xds = [net.send(r.xd, r.xdr.at[k - 1], *net.at(0, k)) for k in range(1, F)]
+    r.xd[:, 0:W] = dot(r.inp[...], r.xp[...], 1, 1).astype(BF16)
+    xd_near = net.send(r.xd, r.xdn, ms, core)
+
+    def chips(src, near_copy, near, far):
+        near_copy.wait()
+        src[...] = (src[...].astype(F32) + near[...].astype(F32)).astype(BF16)
+        return net.batch([(src, far.at[k - 1], *net.at(0, 2 * k)) for k in range(1, F // 2)], far)
+
+    def chips_total(src, batch, far):
+        batch.wait()
+        tot = src[:, 0:W].astype(F32)
+        for k in range(F // 2 - 1):
+            tot = tot + far[k, :, 0:W].astype(F32)
+        return tot
+
+    xd_far = chips(r.xd, xd_near, r.xdn, r.xdr)
     wg_near = w_relay(1, wg_far)
     relay_rows(r.cot, c_direct, c_beside)
     for c in [own[3], own[4], own[5], w_beside[1]] + wg_near + c_beside:
@@ -385,16 +444,12 @@
         return 0
 
     lax.fori_loop(0, T // 64, gys, 0)
-    for c in xds:
-        c.wait()
-    xd = r.xd[:, 0:W].astype(F32)
-    for k in range(F - 1):
-        xd = xd + r.xdr[k, :, 0:W].astype(F32)
+    xd = chips_total(r.xd, xd_far, r.xdr)
     own[7].wait()
     low = xd[:, : d.R].astype(BF16)
     r.xd[:, 0 : d.R] = low
     for c in range(0, CL, 256):
-        r.dtpre[:, c : c + 256] = dot(low, r.wdt[c : c + 256, :], 1, 1)
+        r.dtpre[:, c : c + 256] = dot(low, r.wdt[:, c : c + 256])
 
     def steps(i, acc):
         rows = pl.ds(pl.multiple_of(i * 64, 64), 64)
@@ -419,7 +474,7 @@
             t *= 2
         r.sd[0:V, lane(j)] = sums[j]
         r.tot[:, lane(j)] = whole
-    tots = [net.send(r.tot, r.totr.at[k - 1], *net.at(k, 0)) for k in range(1, S)]
+    tots = net.batch([(r.tot, r.totr.at[k - 1], *net.at(k, 0)) for k in range(1, S)], r.totr)
     bc = xd[:, d.R : W]
     hi = bc.astype(BF16)
     rest = (bc - hi.astype(F32)).astype(BF16)
@@ -480,17 +535,14 @@
         out = []
         for k in range(1, S):
             ps, pf = net.at(k, 0)
-            out.append(
-                net.send(r.epack.at[jnp.where(ps > ms, 0, 1), j], r.eget.at[j, ms], ps, pf)
-            )
-        return out
+            out.append((r.epack.at[jnp.where(ps > ms, 0, 1), j], r.eget.at[j, k - 1], ps, pf))
+        return net.batch(out, r.eget.at[j])
 
     def turn(x, by):
         return x if by % V == 0 else pltpu.roll(x, by % V, 0)
 
     def begin(j, copies):
-        for c in copies:
-            c.wait()
+        copies.wait()
         tiles = N // H
         dn = []
         for i in range(tiles):
@@ -500,8 +552,9 @@
             dn.append(x)
 
         def join(p, acc):
-            tot = r.totr[lax.rem(ms + S - p, S) - 1, :, lane(j)]
-            e = r.eget[j, p].astype(F32)
+            slot = lax.rem(ms + S - p, S) - 1
+            tot = r.totr[slot, :, lane(j)]
+            e = r.eget[j, slot].astype(F32)
             return tuple(jnp.exp2(tot * dn[i]) * acc[i] + e[row_n(i)] for i in range(tiles))
 
         zero = tuple(jnp.zeros((V, LN), F32) for _ in range(tiles))
@@ -613,15 +666,14 @@
 
     r.rowsum[...] = jnp.zeros_like(r.rowsum)
     states = [own_ends(j) for j in range(NB)]
-    for c in tots:
-        c.wait()
+    tots.wait()
     for j in range(NB):
         begin(j, states[j])
         forward(j)
         gating(j)
-        if 0 < j < NB - 1:
-            backward(j - 1)
-    late = list(range(max(NB - 2, 0), NB))
+        if j == NB - 2:
+            backward(0)
+    late = list(range(1, NB))
 
     def put(dst, first, res):
         n = dst.shape[2]
@@ -629,16 +681,20 @@
             s = first // n + t
             dst[s % 2, s // 2] = res[t * n : (t + 1) * n].astype(dst.dtype)
 
+    def put_split(dst, first, res):
+        n = dst.shape[3]
+        for t in range(res.shape[0] // n):
+            s, f = divmod(first // n + t, F)
+            dst[s % 2, s // 2, f] = res[t * n : (t + 1) * n].astype(dst.dtype)
+
     back0 = from_scan(d, 0)
     r.gatn[...] = dot(back0, r.ggate[0:T, :]).astype(BF16)
     for c in range(0, D, LN):
-        put(r.giwg, c, dot(r.normed[0:T, c : c + LN], r.gatn[...], 0, 0))
-    sum_g = Scatter(net, r.giwg, r.giwg_n, r.giwg_f)
-    sum_g.first()
+        put_split(r.giwg, c, dot(r.normed[0:T, c : c + LN], r.gatn[...], 0, 0))
+    sum_g = Scatter(net, r.giwg, r.giwg_n, r.o_wg, True)
     for j in range(NB):
         put(r.gow, j * LN, dot(r.gated[0:T, lane(j)], r.big[0:T, :], 0, 0))
-    sum_o = Scatter(net, r.gow, r.gow_n, r.gow_f)
-    sum_o.first()
+    sum_o = Scatter(net, r.gow, r.gow_n, r.o_out, False)
     r.gated[0:T, :] = dot(back0, r.gated[0:T, :]).astype(BF16)
     for c in range(0, D, 256):
         r.cot[:, c : c + 256] = dot(r.gated[0:T, :], r.ow[:, c : c + 256]).astype(BF16)
@@ -646,9 +702,8 @@
     outs.append(net.local(rows_of(r.cot, mf, tok), r.outr.at[mf]))
     for i, j in enumerate(late):
         backward(j)
-        if i == 0:
-            sum_g.second()
-            sum_o.second()
+        if i > 0:
+            sum_g.step((S // 2) * i // (len(late) - 1))
 
     def finish(i, acc):
         rows = pl.ds(pl.multiple_of(i * 64, 64), 64)
@@ -668,7 +723,7 @@
     db = lax.fori_loop(0, T // 64, finish, tuple(jnp.zeros((V, LN), F32) for _ in range(NB)))
     for j in range(NB):
         r.rowsum[5:6, lane(j)] = jnp.sum(db[j], axis=0, keepdims=True)
-    r.gx[:, 0 : d.R] = dot(r.ggate[0:T, :], r.wdt[...]).astype(BF16)
+    r.gx[:, 0 : d.R] = dot(r.ggate[0:T, :], r.wdt[...], 1, 1).astype(BF16)
     acc = jnp.zeros((T, 2 * N), F32)
     for n in range(0, 2 * N, 4):
         row = lax.div(lax.broadcasted_iota(jnp.int32, (4 * LN, 2 * N), 0), LN) + n
@@ -676,58 +731,19 @@
         pick = jnp.where(row == col, 1.0, 0.0).astype(BF16)
         acc = acc + dot(r.x_s[:, n * LN : (n + 4) * LN].astype(BF16), pick)
     r.gx[:, d.R : W] = acc.astype(BF16)
-    gxs = [net.send(r.gx, r.gxr.at[k - 1], *net.at(0, k)) for k in range(1, F)]
-
-    def to_rows(total, out, keep):
-        n = total.shape[0] // F
-        for f in range(F):
-            keep[f] = total[f * n : (f + 1) * n].astype(keep.dtype)
-        cs = [net.send(keep.at[net.at(0, k)[1]], out.at[mf], *net.at(0, k)) for k in range(1, F)]
-        return cs + [net.local(keep.at[mf], out.at[mf])]
-
-    def to_home(total, keep, out):
-        keep[...] = total.astype(keep.dtype)
-        i = net.used
-        net.used += 2
-        far = pltpu.make_async_remote_copy(
-            keep, out, r.ssem.at[i], r.rsem.at[i], {"seq": home_s, "fsdp": home_f}, device_id_type=MESH
-        )
-        near = pltpu.make_async_copy(keep, out, r.rsem.at[i + 1])
-
-        @pl.when(moves)
-        def _():
-            far.start()
-
-        @pl.when(jnp.logical_not(moves))
-        def _():
-            near.start()
-
-        return far, near
-
-    def home_wait(pair):
-        @pl.when(moves)
-        def _():
-            pair[0].wait()
-
-        @pl.when(jnp.logical_not(moves))
-        def _():
-            pair[1].wait()
-
-    g_cs = to_rows(sum_g.total(), r.o_wg, r.k_wg)
-    o_cs = to_home(sum_o.total(), r.k_out, r.o_out)
+    gx_near = net.send(r.gx, r.gxn, ms, core)
+    gx_far = chips(r.gx, gx_near, r.gxn, r.gxr)
+
+    sum_g.step()
+    sum_o.step(S // 4)
     gwdt = dot(r.ggate[0:T, :], r.xd[:, 0 : d.R], 0, 0)
 
-    for c in gxs:
-        c.wait()
-    s = r.gx[:, 0:W].astype(F32)
-    for k in range(F - 1):
-        s = s + r.gxr[k, :, 0:W].astype(F32)
-    gxd = s.astype(BF16)
+    gxd = chips_total(r.gx, gx_far, r.gxr).astype(BF16)
     pad = HG * V
     r.gg[0:pad, :] = jnp.zeros((pad, CL), F32)
     r.gg[pad + T :, :] = jnp.zeros((pad, CL), F32)
     for c in range(0, CL, 256):
-        r.gg[pad : pad + T, c : c + 256] = r.gsc[:, c : c + 256] + dot(gxd, r.xp[c : c + 256, :], 1, 1)
+        r.gg[pad : pad + T, c : c + 256] = r.gsc[:, c : c + 256] + dot(gxd, r.xp[:, c : c + 256])
 
     def act(i, acc):
         r0 = pl.multiple_of(i * 64, 64)
@@ -772,16 +788,15 @@
     lax.fori_loop(0, d.TE // 32, gather_taps, 0)
     r.ggate[...] = dot(from_scan(d, HG), r.gated[...]).astype(BF16)
     for c in range(0, D, LN):
-        put(r.giwx, c, dot(r.normed[:, c : c + LN], r.ggate[...], 0, 0))
-    sum_x = Scatter(net, r.giwx, r.giwx_n, r.giwx_f)
-    sum_x.first()
+        put_split(r.giwx, c, dot(r.normed[:, c : c + LN], r.ggate[...], 0, 0))
+    sum_x = Scatter(net, r.giwx, r.giwx_n, r.o_wx, True)
     r.y_s[0:CL, 0:LN] = r.rowsum[...].T
     r.y_s[0:CL, LN : LN + W] = dot(r.inp[...], gxd, 0, 0)
     r.y_s[0:CL, LN + W : 2 * LN] = jnp.zeros((CL, LN - W), F32)
     r.y_s[0:CL, 32 : 32 + d.R] = gwdt
     put(r.small, 0, r.y_s[0:CL, 0 : 2 * LN])
-    sum_s = Scatter(net, r.small, r.small_n, r.small_f)
-    sum_s.first()
+    sum_s = Scatter(net, r.small, r.small_n, r.o_small, False)
+    sum_o.step()
     for c in range(0, D, 256):
         g = dot(r.ggate[...], r.w[0, c : c + 256, :], 1, 1)
         r.hid[0:T, c : c + 256] = (
@@ -800,8 +815,8 @@
                 r.hid.at[pl.ds(T + pf * TAIL, TAIL)], r.o_gn.at[pl.ds(T + mf * TAIL, TAIL)], ps, pf
             )
         )
-    sum_x.second()
-    sum_s.second()
+    sum_x.step()
+    sum_s.step()
 
     def gains(i, acc):
         rows = pl.ds(pl.multiple_of(i * 64, 64), 64)
@@ -812,21 +827,14 @@
     n = D // S
     for s in range(S):
         r.gg8[s % 2, s // 2] = gtot[:, s * n : (s + 1) * n]
-    sum_n = Scatter(net, r.gg8, r.gg8_n, r.gg8_f)
-    sum_n.first()
-    sum_n.second()
-    x_cs = to_rows(sum_x.total(), r.o_wx, r.k_wx)
-    s_cs = to_home(sum_s.total(), r.k_small, r.o_small)
-    r.k_gain[...] = sum_n.total()
-    n_cs = [net.send(r.k_gain, r.o_gain.at[mf], *net.at(0, k)) for k in range(1, F)]
-    n_cs.append(net.local(r.k_gain, r.o_gain.at[mf]))
+    sum_n = Scatter(net, r.gg8, r.gg8_n, r.o_gain, True, False)
+    sum_n.step()
     net.drain()
-    home_wait(o_cs)
-    home_wait(s_cs)
+    assert (net.s_used, net.r_used) == semaphores(d), (net.s_used, net.r_used)
 
 
 def close(d, gn, outr, hid, cot, gain, wx, wg, out, small, ggain,
-          o_out, o_hid, o_gain, o_in, o_conv, o_rows, o_xp, o_dt, o_al, o_gout):
+          o_out, o_hid, o_gain, o_in, o_conv, o_cb, o_db, o_sk, o_xp, o_dt, o_al, o_gout):
     F, T, tok, D = d.F, d.T, d.tok, d.D
     W = d.R + 2 * d.N
 
@@ -851,18 +859,21 @@
 
     lax.fori_loop(0, tok // 16, rows_, 0)
     for f in range(F):
-        o_in[:, f * d.CL : (f + 1) * d.CL] = wx[f].astype(F32)
-        o_in[:, d.DI + f * d.CL : d.DI + (f + 1) * d.CL] = wg[f].astype(F32)
-    o_gout[...] = out[...].astype(F32)
-    sm = small[...]
-    o_conv[...] = sm[:, 0 : d.K]
-    o_al[...] = sm[:, V : V + d.N]
+        for at, part in ((f * d.CL, wx), (d.DI + f * d.CL, wg)):
+            o_in[:, at : at + d.CL] = jnp.sum(part[:, f].astype(F32), axis=0)
+    o_gout[...] = jnp.sum(out[...].astype(F32), axis=0)
+    sm = jnp.sum(small[...].astype(F32), axis=0)
+    first = sm[:, 0:LN].T
+    for i, o_row in enumerate((o_cb, o_db, o_sk)):
+        o_row[...] = first[4 + i : 5 + i, :]
+    o_conv[...] = first[0 : d.K, :]
+    o_al[...] = first[V : V + d.N, :]
     o_dt[...] = sm[:, 32 : 32 + d.R]
     o_xp[...] = sm[:, LN : LN + W]
-    o_rows[...] = sm[:, 0:LN].T[0:V, :]
-    tot = ggain[0]
-    for f in range(1, F):
-        tot = tot + ggain[f]
+    tot = jnp.zeros(ggain.shape[2:], F32)
+    for k in range(ggain.shape[0]):
+        for f in range(F):
+            tot = tot + ggain[k, f]
     n, k = D // d.S, D // d.S // F
     row = lax.broadcasted_iota(jnp.int32, (n, k), 0) - lax.axis_index("fsdp") * k
     pick = jnp.where(row == lax.broadcasted_iota(jnp.int32, (n, k), 1), 1.0, 0.0)
@@ -873,6 +884,13 @@
     o_gain[...] = one[0:1, :]
 
 
+def semaphores(d):
+    half, far = d.S // 2, d.F // 2 - 1
+    one = (d.F - 1) + 2 * (2 * far + 1) + d.F + 2 * (2 * far) + 2 + 2 * (6 * far) + (d.F - 1) + (2 * d.F - 1)
+    one += 2 * 2 + 1 + d.NB
+    return one + 5 * 2 * half, one + 5 * (half + 1) + 16
+
+
 def vm(*shape, dtype=F32):
     return pltpu.VMEM(shape, dtype)
 
@@ -882,53 +900,48 @@
     dt_weight, dt_bias, a_log, skip, out_weight, cotangent,
 ):
     S, F, T, D, CL, N, NB, R = d.S, d.F, d.T, d.D, d.CL, d.N, d.NB, d.R
-    wide = lambda a: jnp.pad(a.astype(F32), (0, CL - a.shape[0]))
-    params = jnp.stack(
-        [conv_bias.astype(F32), dt_bias.astype(F32), skip.astype(F32), wide(norm_gain),
-         wide(cluster_lengths[0])] + [jnp.zeros((CL,), F32)] * (V - 5)
-    )
     ins = dict(
-        hidden=hidden[0], params=params, in_weight=in_weight, conv_weight=conv_weight,
-        xproj_weight=xproj_weight, dt_weight=dt_weight, a_log=a_log, out_weight=out_weight,
+        hidden=hidden[0], lens=cluster_lengths, norm_gain=norm_gain, conv_bias=conv_bias,
+        dt_bias=dt_bias, skip=skip, in_weight=in_weight, conv_weight=conv_weight.T,
+        xproj_weight=xproj_weight.T, dt_weight=dt_weight.T, a_log=a_log.T, out_weight=out_weight,
         cotangent=cotangent[0],
     )
     DS, CS, W, W2 = D // S, CL // S, R + 2 * N, 2 * LN
     TP = T + 2 * HG * V
+    rt = BF16 if CS >= 16 else F32
+    half = S // 2
     outs = dict(
         o_gn=((d.NAT, D), BF16), outr=((F, d.tok, D), BF16), gain=((1, D), F32),
-        o_wx=((F, DS // F, CL), BF16), o_wg=((F, DS // F, CL), BF16), o_out=((CS, D), F32),
-        o_small=((CS, W2), F32), o_gain=((F, V, DS), F32),
+        o_wx=((half, F, DS // F, CL), BF16), o_wg=((half, F, DS // F, CL), BF16),
+        o_out=((half, CS, D), rt), o_small=((half, CS, W2), rt), o_gain=((half, F, V, DS), F32),
     )
-    rt = BF16 if CS >= 16 else F32
     small_t = T <= 512
-    half = S // 2
     EP = N // d.H * V
     scratch = dict(
         hid=((d.NAT, D), BF16), normed=((d.NAT, D), BF16), big=((d.TE, D), BF16),
         cot=((T, D), BF16), w=((2, D, CL), BF16), ow=((CL, D), BF16),
-        xp=((CL, W), BF16), wdt=((CL, R), BF16), cw=((CL, d.K), BF16), al=((CL, N), BF16),
-        pg=((F, V, CL), F32), cp=((V, CL), F32), dec=((N, CL), F32), rel=((TP, LN), F32),
+        xp=((W, CL), BF16), wdt=((R, CL), BF16), cw=((d.K, CL), BF16), al=((N, CL), BF16),
+        row_cb=((CL,), BF16), row_db=((CL,), BF16), row_sk=((CL,), BF16), row_g=((D // F,), BF16),
+        row_l=((1, d.clusters), jnp.int32), pg=((F, V, D // F), F32), pg_own=((V, D // F), F32), cp=((V, CL), F32), dec=((N, CL), F32), rel=((TP, LN), F32),
         xb=((d.TE, CL), F32), gate=((T, CL), F32), pre=((T, CL), F32), inp=((T, CL), BF16),
-        xd=((T, LN), BF16), xdr=((F - 1, T, LN), BF16),
+        xd=((T, LN), BF16), xdn=((T, LN), BF16), xdr=((F // 2 - 1, T, LN), BF16),
         dtpre=((T, CL), F32), dtd=((T, CL), F32), u=((T, CL), F32), gg=((TP, CL), F32),
         gy=((T, CL), F32), bcb=((T, 2 * N * LN), F32 if small_t else BF16),
         sd=((V, CL), F32), tot=((V, CL), F32), totr=((S - 1, V, CL), F32),
-        ends=((2, N * V, CL), F32), epack=((2, NB, EP, LN), BF16), eget=((NB, S, EP, LN), BF16),
+        ends=((2, N * V, CL), F32), epack=((2, NB, EP, LN), BF16), eget=((NB, S - 1, EP, LN), BF16),
         start=((2, N * V, CL), F32), m_s=((NB, T, N * LN), BF16), y_s=((T, CL), F32),
         gsc=((T, CL), F32), x_s=((T, 2 * N * LN), F32 if small_t else BF16),
         gated=((d.TE, CL), BF16), ggate=((d.NAT, CL), BF16), gatn=((T, CL), BF16),
-        gx=((T, LN), BF16), gxr=((F - 1, T, LN), BF16), rowsum=((LN, CL), F32),
-
-        giwg=((2, half, DS, CL), BF16), giwg_n=((half, DS, CL), BF16), giwg_f=((half - 1, DS, CL), BF16),
-        giwx=((2, half, DS, CL), BF16), giwx_n=((half, DS, CL), BF16), giwx_f=((half - 1, DS, CL), BF16),
-        gow=((2, half, CS, D), rt), gow_n=((half, CS, D), rt), gow_f=((half - 1, CS, D), rt),
-        small=((2, half, CS, W2), rt), small_n=((half, CS, W2), rt), small_f=((half - 1, CS, W2), rt),
-        gg8=((2, half, V, DS), F32), gg8_n=((half, V, DS), F32), gg8_f=((half - 1, V, DS), F32),
-        k_wg=((F, DS // F, CL), BF16), k_wx=((F, DS // F, CL), BF16), k_out=((CS, D), F32),
-        k_small=((CS, W2), F32), k_gain=((V, DS), F32),
+        gx=((T, LN), BF16), gxn=((T, LN), BF16), gxr=((F // 2 - 1, T, LN), BF16), rowsum=((LN, CL), F32),
+
+        giwg=((2, half, F, DS // F, CL), BF16), giwg_n=((half, F, DS // F, CL), BF16),
+        giwx=((2, half, F, DS // F, CL), BF16), giwx_n=((half, F, DS // F, CL), BF16),
+        gow=((2, half, CS, D), rt), gow_n=((half, CS, D), rt),
+        small=((2, half, CS, W2), rt), small_n=((half, CS, W2), rt),
+        gg8=((2, half, V, DS), F32), gg8_n=((half, V, DS), F32),
     )
     names = list(ins) + list(outs) + list(scratch) + ["ssem", "rsem"]
-    sems = 160 + (NB + 6) * S + 12 * F
+    sends, gets = semaphores(d)
     res = pl.pallas_call(
         functools.partial(layer, d, names),
         out_shape=[jax.ShapeDtypeStruct(*o) for o in outs.values()],
@@ -937,7 +950,7 @@
             pl.BlockSpec(memory_space=pltpu.VMEM if k == "gain" else pl.ANY) for k in outs
         ],
         scratch_shapes=[vm(*s, dtype=t) for s, t in scratch.values()]
-        + [pltpu.SemaphoreType.DMA((sems,)), pltpu.SemaphoreType.DMA((sems,))],
+        + [pltpu.SemaphoreType.DMA((sends,)), pltpu.SemaphoreType.DMA((gets,))],
         compiler_params=pltpu.CompilerParams(
             collective_id=0, has_side_effects=True, vmem_limit_bytes=65250 * 1024
         ),
@@ -948,11 +961,12 @@
         (o["o_gn"], o["outr"], hidden[0], cotangent[0], o["gain"], o["o_wx"], o["o_wg"], o["o_out"],
          o["o_small"], o["o_gain"]),
         [((1, d.tok, D), BF16), ((1, d.tok, D), F32), ((1, DS // F), F32), ((DS // F, 2 * d.DI), F32),
-         ((CS, d.K), F32), ((V, CS), F32), ((CS, W), F32), ((CS, R), F32), ((CS, N), F32), ((CS, D), F32)],
+         ((d.K, CS), F32), ((1, CS), F32), ((1, CS), F32), ((1, CS), F32), ((CS, W), F32), ((CS, R), F32),
+         ((N, CS), F32), ((CS, D), F32)],
     )
-    out, g_hid, g_gain, g_in, g_conv, rows, g_xp, g_dt, g_al, g_out = fin
+    out, g_hid, g_gain, g_in, g_conv, g_cb, g_db, g_sk, g_xp, g_dt, g_al, g_out = fin
     return (
-        out, g_hid, g_gain[0], g_in, g_conv, rows[4], g_xp, g_dt, rows[5], g_al, rows[6], g_out,
+        out, g_hid, g_gain[0], g_in, g_conv.T, g_cb[0], g_xp, g_dt, g_db[0], g_al.T, g_sk[0], g_out,
     )
 
 

time: 165 us -> 133 us (0.81)
  Pallas kernels: 150 us -> 132 us
  local copies, waits for them, and re-layouts: 11 us -> 0 us
  other arithmetic: 3.36 us -> 0 us
    pallas_call x1, Pallas kernels: 145 us -> 128 us  [per_device(): pl.pallas_call(functools.partial(layer, d, names), out_shape=[jax.ShapeDt...]
    unnamed x6 -> x0, local copies, waits for them, and re-layouts: 9.05 us -> none
    another operation x4 -> x0, other arithmetic: 2.7 us -> none  [per_device(): jnp.stack([conv_bias.astype(F32), dt_bias.astype(F32), skip.astype(F32),...]
where the time goes in v3:
time: 133 us
  Pallas kernels  132 us (99%)
    pallas_call x1, Pallas kernels, per_device(): pl.pallas_call(functools.partial(layer, d, names), out_shape=[jax.ShapeDt...  128 us
    pallas_call x1, Pallas kernels, kernel(): pl.pallas_call(body, out_shape=[jax.ShapeDtypeStruct(s, t) for s, t in ou...  4.48 us

profile of v3, /device:TPU:0, one launch (start us, length us, event | category | flops | bytes accessed | tf_op | source)
XLA Modules:
  0.0 133.1 jit_solution(8252674285538214021)
XLA Ops:
  0.6 127.9 %shard_map.220 = (bf16[576,1024]{1,0:T(8,128)(2,1)}, bf16[4,128,1024]{2,1,0:T(8,128)(2,1)}, f32[1,1024]{1,0:T(1,128)}, bf16[4,4,32,512]{3,2,1,0:T(8,128)(2,1)}, ...) custom-call(bf16[128,1024]{1,0:T(8,128)(2,1)} %bitcast.12, ...), custom_call_target="tpu_custom_call" | custom-call | tf_op jit(solution)/shard_map/pallas_call | solution.py:945
  128.6 4.5 %shard_map.221 = (bf16[1,128,1024]{2,1,0:T(8,128)(2,1)}, f32[1,128,1024]{2,1,0:T(8,128)}, f32[1,32]{1,0:T(1,128)}, f32[32,4096]{1,0:T(8,128)}, f32[4,64]{1,0:T(4...) custom-call(bf16[576,1024]{1,0:T(8,128)(2,1)} %get-tuple-element.32., ...), custom_call_target="tpu_custom_call" | custom-call | tf_op jit(solution)/shard_map/pallas_call | solution.py:46

commit v4 on v3

--- a/solution.py
+++ b/solution.py
@@ -162,67 +162,129 @@
             c.wait()
 
 
+def flip(value, mask):
+    bit = 0
+    out = value
+    while 1 << bit <= mask:
+        if mask >> bit & 1:
+            out = out + (1 - 2 * lax.rem(lax.div(value, 1 << bit), 2)) * (1 << bit)
+        bit += 1
+    return out
+
+
 class Scatter:
-    def __init__(self, net, mine, near, out, spread, split=True):
-        self.net, self.mine, self.near, self.out_ref = net, mine, near, out
-        self.spread, self.split = spread, split
-        d = net.d
-        self.half = d.S // 2
-        self.x, self.z = lax.rem(net.ms, 2), lax.div(net.ms, 2)
-        self.pal = net.ms + 1 - 2 * self.x
-        self.order = [lax.rem(self.z + k, self.half) for k in list(range(1, self.half)) + [0]]
-        self.first = [
-            net.send(mine.at[1 - self.x, z], near.at[z], self.pal, net.mf) for z in self.order
-        ]
-        self.done, self.tails = 0, []
+    def __init__(self, net, mine, near, out, bits, spread, split=True):
+        self.net, self.mine, self.near, self.out = net, mine, near, out
+        self.bits, self.spread, self.split = bits, spread, split
+        self.tails, self.queue, self.last = [], [], {}
         self.into = net.r_used
         net.r_used += 1
+        slot = 0
+        self.slots = []
+        for level in range(len(bits) - 1):
+            sides = self.sides(level)
+            self.slots.append({side: slot + i for i, side in enumerate(sides)})
+            slot += len(sides)
+            self.queue += [(level, side) for side in sides]
+        self.copies = {}
+        for side in self.sides(0):
+            self.push(0, side)
+        self.done = 0
         net.open.append(self)
 
-    def step(self, upto=None):
+    def sides(self, level):
+        masks = [0]
+        for bit in reversed(self.bits[level + 1 :]):
+            masks = [m | 1 << bit for m in masks] + masks
+        return masks
+
+    def push(self, level, side):
+        net = self.net
+        to = flip(net.ms, 1 << self.bits[level])
+        self.copies[level, side] = net.send(
+            self.mine.at[flip(to, side)], self.near.at[self.slots[level][side]], to, net.mf
+        )
+
+    def step(self, count=1000):
+        net = self.net
+        for level, side in self.queue[self.done : self.done + count]:
+            self.done += 1
+            self.copies[level, side].wait()
+            at = flip(net.ms, side)
+            both = self.mine[at].astype(F32) + self.near[self.slots[level][side]].astype(F32)
+            self.mine[at] = both.astype(self.mine.dtype)
+            bit = 1 << self.bits[level + 1]
+            if level + 2 < len(self.bits):
+                if side & bit:
+                    self.push(level + 1, side ^ bit)
+            else:
+                self.finish(at, 1 if side else 0)
+
+    def finish(self, at, side):
         net, d = self.net, self.net.d
-        upto = self.half if upto is None else upto
-        while self.done < upto:
-            k, z = self.done, self.order[self.done]
-            self.done += 1
-            self.first[k].wait()
-            both = self.mine[self.x, z].astype(F32) + self.near[z].astype(F32)
-            self.mine[self.x, z] = both.astype(self.mine.dtype)
-            i = net.s_used
-            net.s_used += 1
-            if self.spread:
-                last = k == self.half - 1
-                for g in range(1, d.F + (0 if last else 1)):
-                    f = lax.rem(net.mf + g, d.F)
-                    src = self.mine.at[self.x, z, f] if self.split else self.mine.at[self.x, z]
-                    net.remote(
-                        src, self.out_ref.at[k, net.mf], i, self.into, z * 2 + self.x, f
-                    ).start()
-                if last:
-                    src = self.mine.at[self.x, z, net.mf] if self.split else self.mine.at[self.x, z]
-                    pltpu.make_async_copy(
-                        src, self.out_ref.at[k, net.mf], net.rsem.at[self.into]
-                    ).start()
-                sent = self.out_ref.at[k, pl.ds(0, d.F - 1)] if last else self.out_ref.at[k]
-                self.tails.append((None, net.remote(sent, sent, i, self.into, *net.at(0, 1))))
-            else:
-                spot = net.mf * d.S + z * 2 + self.x
-                away = spot != net.ms * d.F + net.mf
-                src, dst = self.mine.at[self.x, z], self.out_ref.at[self.z]
-                far = net.remote(src, dst, i, self.into, lax.div(spot, d.F), lax.rem(spot, d.F))
-                near = pltpu.make_async_copy(src, dst, net.rsem.at[self.into])
-                pl.when(away)(far.start)
-                pl.when(jnp.logical_not(away))(near.start)
-                self.tails.append((away, far))
+        i = net.s_used
+        net.s_used += 1
+        if self.spread:
+            for g in range(1 - side, d.F):
+                f = lax.rem(net.mf + g, d.F)
+                src = self.mine.at[at, f] if self.split else self.mine.at[at]
+                net.remote(src, self.out.at[side, net.mf], i, self.into, at, f).start()
+            if not side:
+                src = self.mine.at[at, net.mf] if self.split else self.mine.at[at]
+                pltpu.make_async_copy(src, self.out.at[0, net.mf], net.rsem.at[self.into]).start()
+            sent = self.out.at[side] if side else self.out.at[0, pl.ds(0, d.F - 1)]
+            self.tails.append((None, net.remote(sent, sent, i, self.into, *net.at(0, 1))))
+        else:
+            spot = net.mf * d.S + at
+            away = spot != net.ms * d.F + net.mf
+            src, dst = self.mine.at[at], self.out.at[side]
+            far = net.remote(src, dst, i, self.into, lax.div(spot, d.F), lax.rem(spot, d.F))
+            near = pltpu.make_async_copy(src, dst, net.rsem.at[self.into])
+            pl.when(away)(far.start)
+            pl.when(jnp.logical_not(away))(near.start)
+            self.tails.append((away, far))
 
     def wait(self):
+        self.step()
         for away, c in self.tails:
             if away is None:
                 c.wait_send()
             else:
                 pl.when(away)(c.wait_send)
         net = self.net
-        net.remote(self.out_ref, self.out_ref, 0, self.into, *net.at(0, 1)).wait_recv()
+        net.remote(self.out, self.out, 0, self.into, *net.at(0, 1)).wait_recv()
+
+
+class Rows:
+    def __init__(self, net, core, src, land, out):
+        self.net, self.src, self.land, self.out = net, src, land, out
+        d = net.d
+        self.rows = lambda f: src.at[pl.ds(f * d.tok, d.tok)]
+        self.far = range(1, d.F // 2)
+        step = lambda f, k: lax.rem(f + 2 * k, d.F)
+        self.to = [step(net.mf, k) for k in self.far]
+        self.near = [
+            net.send(self.rows(step(core, k)), land.at[pl.ds((k - 1) * d.tok, d.tok)], net.ms, core)
+            for k in self.far
+        ]
+        net.send(self.rows(core), out.at[1], net.ms, core)
+        net.local(self.rows(net.mf), out.at[0])
+
+    def cross(self):
+        net, d = self.net, self.net.d
+        for k, f, c in zip(self.far, self.to, self.near):
+            c.wait()
+
+            def add(i, _, k=k, f=f):
+                here = pl.ds(pl.multiple_of(f * d.tok + i * 32, 32), 32)
+                there = pl.ds(pl.multiple_of((k - 1) * d.tok + i * 32, 32), 32)
+                self.src[here, :] = (
+                    self.src[here, :].astype(F32) + self.land[there, :].astype(F32)
+                ).astype(BF16)
+                return 0
+
+            lax.fori_loop(0, d.tok // 32, add, 0)
+            net.send(self.rows(f), self.out.at[1 + k], net.ms, f)
 
 
 def layer(d, names, *refs):
@@ -363,25 +425,33 @@
     for c in h_direct:
         c.wait_send()
     c_direct, c_beside = spread_rows(r.cotangent, r.cot)
+    wg_far = w_far(1)
     for k, c in enumerate(h_direct):
         c.wait_recv()
         f = lax.rem(mf + F - 2 * (k + 1), F)
         h_beside.append(net.send(rows_of(r.hid, f, tok), rows_of(r.hid, f, tok), ms, core))
-    for c in h_beside + halo:
+    perm = to_scan(d, HG)
+
+    def rms(first, count):
+        def body(i, _):
+            rows = pl.ds(pl.multiple_of(first + i * 64, 64), 64)
+            h = r.hid[rows, :].astype(F32)
+            inv = lax.rsqrt(jnp.mean(h * h, axis=-1, keepdims=True) + EPS)
+            r.normed[rows, :] = (h * inv * r.gain[...]).astype(BF16)
+            return 0
+
+        lax.fori_loop(0, count // 64, body, 0)
+
+    for k in range(F // 2):
+        rms(lax.rem(mf + F - 2 * k, F) * tok, tok)
+    for k, c in enumerate(h_beside):
         c.wait()
-
-    def rms(i, _):
-        rows = pl.ds(pl.multiple_of(i * 64, 64), 64)
-        h = r.hid[rows, :].astype(F32)
-        inv = lax.rsqrt(jnp.mean(h * h, axis=-1, keepdims=True) + EPS)
-        r.normed[rows, :] = (h * inv * r.gain[...]).astype(BF16)
-        return 0
-
-    lax.fori_loop(0, d.NAT // 64, rms, 0)
-    perm = to_scan(d, HG)
+        rms(lax.rem(core + F - 2 * k, F) * tok, tok)
+    for c in halo:
+        c.wait()
+    rms(T, F * TAIL)
     for c in range(0, D, 256):
         r.big[:, c : c + 256] = dot(perm, r.normed[:, c : c + 256]).astype(BF16)
-    wg_far = w_far(1)
     own[2].wait()
     w_beside[0].wait()
     for c in wx_near:
@@ -424,26 +494,15 @@
         return tot
 
     xd_far = chips(r.xd, xd_near, r.xdn, r.xdr)
+    relay_rows(r.cot, c_direct, c_beside)
     wg_near = w_relay(1, wg_far)
-    relay_rows(r.cot, c_direct, c_beside)
-    for c in [own[3], own[4], own[5], w_beside[1]] + wg_near + c_beside:
+    perm = to_scan(d, 0)
+    for c in [own[4], own[5]] + c_beside:
         c.wait()
+    for c in range(0, D, 256):
+        r.cot[:, c : c + 256] = dot(perm, r.cot[:, c : c + 256]).astype(BF16)
     for c in range(0, CL, 256):
-        r.gate[:, c : c + 256] = dot(r.big[HG * V :, :], r.w[1, :, c : c + 256])
-    perm = to_scan(d, 0)
-    for c in range(0, D, 256):
-        r.big[0:T, c : c + 256] = dot(perm, r.cot[:, c : c + 256]).astype(BF16)
-    for c in range(0, CL, 256):
-        r.gg[0:T, c : c + 256] = dot(r.big[0:T, :], r.ow[c : c + 256, :], 1, 1)
-
-    def gys(i, _):
-        rows = pl.ds(pl.multiple_of(i * 64, 64), 64)
-        for j in range(NB):
-            g = r.gate[rows, lane(j)]
-            r.gy[rows, lane(j)] = r.gg[rows, lane(j)] * (g * sigmoid(g))
-        return 0
-
-    lax.fori_loop(0, T // 64, gys, 0)
+        r.gg[0:T, c : c + 256] = dot(r.cot[...], r.ow[c : c + 256, :], 1, 1)
     xd = chips_total(r.xd, xd_far, r.xdr)
     own[7].wait()
     low = xd[:, : d.R].astype(BF16)
@@ -489,60 +548,68 @@
     row_n = lambda n: slice(n * V, (n + 1) * V)
     dec_of = lambda n, j: jnp.broadcast_to(r.dec[n : n + 1, lane(j)], (V, LN))
 
-    def own_ends(j):
-        for n0 in range(0, N, half):
-            dn = [dec_of(n, j) for n in range(n0, n0 + half)]
-
-            def local(q, carry, n0=n0, dn=dn):
-                hs, gs = list(carry[0]), list(carry[1])
-                up = pl.ds(pl.multiple_of(q * 2 * V, 2 * V), 2 * V)
-                down = pl.ds(pl.multiple_of((Q - 2 - 2 * q) * V, 2 * V), 2 * V)
-                a_dt, a_u = r.dtd[up, lane(j)], r.u[up, lane(j)]
-                b_dt, b_gy = r.dtd[down, lane(j)], r.gy[down, lane(j)]
-                for i in range(half):
-                    b = r.bcb[up, lane(n0 + i)].astype(F32)
-                    c = r.bcb[down, lane(N + n0 + i)].astype(F32)
-                    for t in (TOP, BOT):
-                        hs[i] = jnp.exp2(a_dt[t] * dn[i]) * hs[i] + a_u[t] * b[t]
-                    for t in (BOT, TOP):
-                        gs[i] = jnp.exp2(b_dt[t] * dn[i]) * (gs[i] + b_gy[t] * c[t])
-                return tuple(hs), tuple(gs)
-
-            zero = tuple(jnp.zeros((V, LN), F32) for _ in range(half))
-            hs, gs = lax.fori_loop(0, Q // 2, local, (zero, zero))
-            for i in range(half):
-                r.ends[0, row_n(n0 + i), lane(j)] = hs[i]
-                r.ends[1, row_n(n0 + i), lane(j)] = gs[i]
+    def state_scan(j):
+        dn = [dec_of(n, j) for n in range(N)]
+
+        def ahead(q, hs):
+            hs = list(hs)
+            rows = pl.ds(pl.multiple_of(q * 2 * V, 2 * V), 2 * V)
+            t, w = r.dtd[rows, lane(j)], r.u[rows, lane(j)]
+            for n in range(N):
+                b = r.bcb[rows, lane(n)].astype(F32)
+                for p in (TOP, BOT):
+                    hs[n] = jnp.exp2(t[p] * dn[n]) * hs[n] + w[p] * b[p]
+            return tuple(hs)
+
+        hs = lax.fori_loop(0, Q // 2, ahead, tuple(jnp.zeros((V, LN), F32) for _ in range(N)))
+        for n in range(N):
+            r.ends[0, row_n(n), lane(j)] = hs[n]
+
+    def adjoint_scan(j):
+        dn = [dec_of(n, j) for n in range(N)]
+
+        def behind(q, gs):
+            gs = list(gs)
+            rows = pl.ds(pl.multiple_of((Q - 2 - 2 * q) * V, 2 * V), 2 * V)
+            t, g0 = r.dtd[rows, lane(j)], r.gy[rows, lane(j)]
+            for n in range(N):
+                c = r.bcb[rows, lane(N + n)].astype(F32)
+                for p in (BOT, TOP):
+                    gs[n] = jnp.exp2(t[p] * dn[n]) * (gs[n] + g0[p] * c[p])
+            return tuple(gs)
+
+        gs = lax.fori_loop(0, Q // 2, behind, tuple(jnp.zeros((V, LN), F32) for _ in range(N)))
+        for n in range(N):
+            r.ends[1, row_n(n), lane(j)] = gs[n]
+
+    def piece_ends(j, way):
         one = r.sd[0:V, lane(j)]
-        fw, bw = [], []
+        tiles = []
         for n0 in range(0, N, H):
-            a, b = jnp.zeros((V, LN), F32), jnp.zeros((V, LN), F32)
+            a = jnp.zeros((V, LN), F32)
             for t in range(H):
                 fac = jnp.exp2(one * dec_of(n0 + t, j))
-                e, g = r.ends[0, row_n(n0 + t), lane(j)], r.ends[1, row_n(n0 + t), lane(j)]
-                x, y = e, g
+                e = r.ends[way, row_n(n0 + t), lane(j)]
+                x = e
                 for h in range(1, H):
-                    x = jnp.where(hidx == h, fac * pltpu.roll(x, 1, 0) + e, x)
-                    y = jnp.where(hidx == H - 1 - h, fac * pltpu.roll(y, V - 1, 0) + g, y)
-                a = jnp.where(hidx == t, turn(x, t - (H - 1)), a)
-                b = jnp.where(hidx == t, turn(y, t), b)
-            fw.append(a)
-            bw.append(b)
-        for i in range(0, len(fw), 2):
+                    at = H - 1 - h if way else h
+                    x = jnp.where(hidx == at, fac * pltpu.roll(x, V - 1 if way else 1, 0) + e, x)
+                a = jnp.where(hidx == t, turn(x, t if way else t - (H - 1)), a)
+            tiles.append(a)
+        for i in range(0, len(tiles), 2):
             band = slice(i * V, (i + 2) * V)
-            r.epack[0, j, band, :] = jnp.concatenate(fw[i : i + 2], axis=0).astype(BF16)
-            r.epack[1, j, band, :] = jnp.concatenate(bw[i : i + 2], axis=0).astype(BF16)
-        out = []
+            r.epack[way, j, band, :] = jnp.concatenate(tiles[i : i + 2], axis=0).astype(BF16)
         for k in range(1, S):
             ps, pf = net.at(k, 0)
-            out.append((r.epack.at[jnp.where(ps > ms, 0, 1), j], r.eget.at[j, k - 1], ps, pf))
-        return net.batch(out, r.eget.at[j])
+            copy = net.remote(r.epack.at[way, j], r.eget.at[j, k - 1], *state_sems[j], ps, pf)
+            pl.when(ps < ms if way else ps > ms)(copy.start)
 
     def turn(x, by):
         return x if by % V == 0 else pltpu.roll(x, by % V, 0)
 
     def begin(j, copies):
-        copies.wait()
+        copies.wait_send()
+        copies.wait_recv()
         tiles = N // H
         dn = []
         for i in range(tiles):
@@ -664,47 +731,97 @@
         sk = lax.fori_loop(0, T // 64, body, jnp.zeros((V, LN), F32))
         r.rowsum[6:7, lane(j)] = jnp.sum(sk, axis=0, keepdims=True)
 
+    def put(dst, first, res):
+        n = dst.shape[1]
+        for t in range(res.shape[0] // n):
+            dst[first // n + t] = res[t * n : (t + 1) * n].astype(dst.dtype)
+
+    def put_split(dst, first, res):
+        n = dst.shape[2]
+        for t in range(res.shape[0] // n):
+            s, f = divmod(first // n + t, F)
+            dst[s, f] = res[t * n : (t + 1) * n].astype(dst.dtype)
+
+    levels = list(range(S.bit_length() - 1))
+    orders = (levels, [1, 0] + levels[2:])
+
+    def start_sum(name, out, t, spread):
+        parts = getattr(r, name + t), getattr(r, name + t + "n"), getattr(r, out + t)
+        return Scatter(net, *parts, orders["ab".index(t)], spread)
+
+    def sum_pair(name, out, spread):
+        return [start_sum(name, out, t, spread) for t in "ab"]
+
+    def both_halves(putter, name, first, res):
+        n = getattr(r, name + "a").shape[-1]
+        putter(getattr(r, name + "a"), first, res[:, :n])
+        putter(getattr(r, name + "b"), first, res[:, n:])
+
+    def step(sums, count=S - 2):
+        for _ in range(count):
+            for one in sums:
+                one.step(1)
+
+    back0 = from_scan(d, 0)
+    cut = r.giwga.shape[-1]
+
+    def gate_grads(t, cols):
+        r.gatn[:, cols] = dot(back0, r.ggate[0:T, cols]).astype(BF16)
+        for c in range(0, D, 256):
+            res = dot(r.normed[0:T, c : c + 256], r.gatn[:, cols], 0, 0)
+            put_split(getattr(r, "giwg" + t), c, res)
+        return start_sum("giwg", "o_wg", t, True)
+
     r.rowsum[...] = jnp.zeros_like(r.rowsum)
-    states = [own_ends(j) for j in range(NB)]
+    state_sems = [net.pair() for _ in range(NB)]
+    states = [
+        net.remote(r.eget.at[j], r.eget.at[j], *state_sems[j], *net.at(0, 1)) for j in range(NB)
+    ]
+    for j in range(NB):
+        state_scan(j)
+        piece_ends(j, 0)
+    for c in [own[3], w_beside[1]] + wg_near:
+        c.wait()
+    for c in range(0, CL, 256):
+        r.gate[:, c : c + 256] = dot(r.big[HG * V :, :], r.w[1, :, c : c + 256])
+
+    def gys(i, _):
+        rows = pl.ds(pl.multiple_of(i * 64, 64), 64)
+        for j in range(NB):
+            g = r.gate[rows, lane(j)]
+            r.gy[rows, lane(j)] = r.gg[rows, lane(j)] * (g * sigmoid(g))
+        return 0
+
+    lax.fori_loop(0, T // 64, gys, 0)
+    for j in range(NB):
+        adjoint_scan(j)
+        piece_ends(j, 1)
     tots.wait()
     for j in range(NB):
         begin(j, states[j])
         forward(j)
         gating(j)
+        if (j + 1) * LN == cut:
+            sum_g = [gate_grads("a", slice(0, cut))]
         if j == NB - 2:
             backward(0)
     late = list(range(1, NB))
 
-    def put(dst, first, res):
-        n = dst.shape[2]
-        for t in range(res.shape[0] // n):
-            s = first // n + t
-            dst[s % 2, s // 2] = res[t * n : (t + 1) * n].astype(dst.dtype)
-
-    def put_split(dst, first, res):
-        n = dst.shape[3]
-        for t in range(res.shape[0] // n):
-            s, f = divmod(first // n + t, F)
-            dst[s % 2, s // 2, f] = res[t * n : (t + 1) * n].astype(dst.dtype)
-
-    back0 = from_scan(d, 0)
-    r.gatn[...] = dot(back0, r.ggate[0:T, :]).astype(BF16)
-    for c in range(0, D, LN):
-        put_split(r.giwg, c, dot(r.normed[0:T, c : c + LN], r.gatn[...], 0, 0))
-    sum_g = Scatter(net, r.giwg, r.giwg_n, r.o_wg, True)
+    sum_g.append(gate_grads("b", slice(cut, CL)))
     for j in range(NB):
-        put(r.gow, j * LN, dot(r.gated[0:T, lane(j)], r.big[0:T, :], 0, 0))
-    sum_o = Scatter(net, r.gow, r.gow_n, r.o_out, False)
+        both_halves(put, "gow", j * LN, dot(r.gated[0:T, lane(j)], r.cot[...], 0, 0))
     r.gated[0:T, :] = dot(back0, r.gated[0:T, :]).astype(BF16)
     for c in range(0, D, 256):
         r.cot[:, c : c + 256] = dot(r.gated[0:T, :], r.ow[:, c : c + 256]).astype(BF16)
-    outs = [net.send(rows_of(r.cot, net.at(0, k)[1], tok), r.outr.at[mf], *net.at(0, k)) for k in range(1, F)]
-    outs.append(net.local(rows_of(r.cot, mf, tok), r.outr.at[mf]))
+    outs = Rows(net, core, r.cot, r.hid, r.outr)
     for i, j in enumerate(late):
         backward(j)
-        if i > 0:
-            sum_g.step((S // 2) * i // (len(late) - 1))
-
+        if i == 0:
+            outs.cross()
+            sum_o = sum_pair("gow", "o_out", False)
+        if j == NB - 2:
+            step(sum_g, S // 2)
+    step(sum_o, S // 4)
     def finish(i, acc):
         rows = pl.ds(pl.multiple_of(i * 64, 64), 64)
         out = []
@@ -734,11 +851,12 @@
     gx_near = net.send(r.gx, r.gxn, ms, core)
     gx_far = chips(r.gx, gx_near, r.gxn, r.gxr)
 
-    sum_g.step()
-    sum_o.step(S // 4)
+    step(sum_g, S - 2 - S // 2)
+    step(sum_o, S // 2 - S // 4)
     gwdt = dot(r.ggate[0:T, :], r.xd[:, 0 : d.R], 0, 0)
 
     gxd = chips_total(r.gx, gx_far, r.gxr).astype(BF16)
+    step(sum_o, S - 2 - S // 2)
     pad = HG * V
     r.gg[0:pad, :] = jnp.zeros((pad, CL), F32)
     r.gg[pad + T :, :] = jnp.zeros((pad, CL), F32)
@@ -788,52 +906,60 @@
     lax.fori_loop(0, d.TE // 32, gather_taps, 0)
     r.ggate[...] = dot(from_scan(d, HG), r.gated[...]).astype(BF16)
     for c in range(0, D, LN):
-        put_split(r.giwx, c, dot(r.normed[:, c : c + LN], r.ggate[...], 0, 0))
-    sum_x = Scatter(net, r.giwx, r.giwx_n, r.o_wx, True)
+        both_halves(put_split, "giwx", c, dot(r.normed[:, c : c + LN], r.ggate[...], 0, 0))
+    sum_x = sum_pair("giwx", "o_wx", True)
     r.y_s[0:CL, 0:LN] = r.rowsum[...].T
     r.y_s[0:CL, LN : LN + W] = dot(r.inp[...], gxd, 0, 0)
     r.y_s[0:CL, LN + W : 2 * LN] = jnp.zeros((CL, LN - W), F32)
     r.y_s[0:CL, 32 : 32 + d.R] = gwdt
     put(r.small, 0, r.y_s[0:CL, 0 : 2 * LN])
-    sum_s = Scatter(net, r.small, r.small_n, r.o_small, False)
-    sum_o.step()
+    sum_s = Scatter(net, r.small, r.small_n, r.o_small, orders[1], False)
     for c in range(0, D, 256):
         g = dot(r.ggate[...], r.w[0, c : c + 256, :], 1, 1)
         r.hid[0:T, c : c + 256] = (
             g[0:T] + dot(r.gatn[...], r.w[1, c : c + 256, :], 1, 1)
         ).astype(BF16)
         r.hid[T:, c : c + 256] = g[T:].astype(BF16)
-    gns = [
-        net.send(rows_of(r.hid, net.at(0, k)[1], tok), rows_of(r.o_gn, mf, tok), *net.at(0, k))
-        for k in range(1, F)
-    ]
-    gns.append(net.local(rows_of(r.hid, mf, tok), rows_of(r.o_gn, mf, tok)))
-    for k in range(F):
-        ps, pf = net.at(-1, k)
-        gns.append(
-            net.send(
-                r.hid.at[pl.ds(T + pf * TAIL, TAIL)], r.o_gn.at[pl.ds(T + mf * TAIL, TAIL)], ps, pf
-            )
-        )
-    sum_x.step()
-    sum_s.step()
-
     def gains(i, acc):
         rows = pl.ds(pl.multiple_of(i * 64, 64), 64)
         t = r.hid[rows, :].astype(F32) * r.normed[rows, :].astype(F32)
         return acc + jnp.sum(t.reshape(8, V, D), axis=0)
 
     gtot = lax.fori_loop(0, d.NAT // 64, gains, jnp.zeros((V, D), F32)) / r.gain[...]
+    gtot = jnp.sum(gtot, axis=0, keepdims=True)
     n = D // S
     for s in range(S):
-        r.gg8[s % 2, s // 2] = gtot[:, s * n : (s + 1) * n]
-    sum_n = Scatter(net, r.gg8, r.gg8_n, r.o_gain, True, False)
-    sum_n.step()
+        r.gg8[s] = gtot[:, s * n : (s + 1) * n]
+    gns = Rows(net, core, r.hid, r.m_s.at[0, :, pl.ds(0, D)], r.o_gn)
+    for k in range(F):
+        ps, pf = net.at(-1, k)
+        net.send(r.hid.at[pl.ds(T + pf * TAIL, TAIL)], r.o_gnh.at[mf], ps, pf)
+    step(sum_x, 2)
+    gns.cross()
+    step([sum_s], 2)
+
+    i, j = net.pair()
+
+    def gain_copy(k):
+        ps, pf = lax.rem(ms + lax.div(k, F), S), lax.rem(mf + lax.rem(k, F), F)
+        return net.remote(r.gg8.at[ps], r.o_gain.at[k], i, j, ps, pf)
+
+    def gain_send(k, _):
+        gain_copy(k).start()
+        return 0
+
+    lax.fori_loop(1, S * F, gain_send, 0)
+    net.local(r.gg8.at[ms], r.o_gain.at[0])
+    others = r.o_gain.at[pl.ds(1, S * F - 1)]
+    gain_all = net.remote(others, others, i, j, *net.at(0, 1))
+    step(sum_x + [sum_s])
+    gain_all.wait_send()
+    gain_all.wait_recv()
     net.drain()
     assert (net.s_used, net.r_used) == semaphores(d), (net.s_used, net.r_used)
 
 
-def close(d, gn, outr, hid, cot, gain, wx, wg, out, small, ggain,
+def close(d, gn, gnh, outr, hid, cot, gain, wxa, wxb, wga, wgb, outa, outb, small, ggain,
           o_out, o_hid, o_gain, o_in, o_conv, o_cb, o_db, o_sk, o_xp, o_dt, o_al, o_gout):
     F, T, tok, D = d.F, d.T, d.tok, d.D
     W = d.R + 2 * d.N
@@ -841,14 +967,13 @@
     def rows_(i, _):
         rows = pl.ds(pl.multiple_of(i * 16, 16), 16)
         h = hid[rows, :].astype(F32)
-        g = gn[pl.ds(pl.multiple_of(i * 16, 16), 16), :].astype(F32)
-        o = outr[0, rows, :].astype(F32)
-        for f in range(1, F):
-            g = g + gn[pl.ds(pl.multiple_of(f * tok + i * 16, 16), 16), :].astype(F32)
-            o = o + outr[f, rows, :].astype(F32)
+        g, o = jnp.zeros((16, D), F32), jnp.zeros((16, D), F32)
+        for k in range(gn.shape[0]):
+            g = g + gn[k, rows, :].astype(F32)
+            o = o + outr[k, rows, :].astype(F32)
         late = jnp.zeros((TAIL, D), F32)
         for f in range(F):
-            late = late + gn[T + f * TAIL : T + (f + 1) * TAIL, :].astype(F32)
+            late = late + gnh[f].astype(F32)
         g = g + jnp.where(i == tok // 16 - 1, late, 0.0)
         inv = lax.rsqrt(jnp.mean(h * h, axis=-1, keepdims=True) + EPS)
         g2 = g * gain[...]
@@ -859,9 +984,14 @@
 
     lax.fori_loop(0, tok // 16, rows_, 0)
     for f in range(F):
-        for at, part in ((f * d.CL, wx), (d.DI + f * d.CL, wg)):
-            o_in[:, at : at + d.CL] = jnp.sum(part[:, f].astype(F32), axis=0)
-    o_gout[...] = jnp.sum(out[...].astype(F32), axis=0)
+        at = f * d.CL
+        for part in (wxa, wxb, wga, wgb):
+            n = part.shape[-1]
+            at = d.DI + f * d.CL if part is wga else at
+            o_in[:, at : at + n] = part[0, f].astype(F32) + part[1, f].astype(F32)
+            at += n
+    o_gout[:, : D // 2] = outa[0].astype(F32) + outa[1].astype(F32)
+    o_gout[:, D // 2 :] = outb[0].astype(F32) + outb[1].astype(F32)
     sm = jnp.sum(small[...].astype(F32), axis=0)
     first = sm[:, 0:LN].T
     for i, o_row in enumerate((o_cb, o_db, o_sk)):
@@ -870,25 +1000,22 @@
     o_al[...] = first[V : V + d.N, :]
     o_dt[...] = sm[:, 32 : 32 + d.R]
     o_xp[...] = sm[:, LN : LN + W]
-    tot = jnp.zeros(ggain.shape[2:], F32)
-    for k in range(ggain.shape[0]):
-        for f in range(F):
-            tot = tot + ggain[k, f]
+    tot = jnp.sum(ggain[...], axis=0)
     n, k = D // d.S, D // d.S // F
     row = lax.broadcasted_iota(jnp.int32, (n, k), 0) - lax.axis_index("fsdp") * k
     pick = jnp.where(row == lax.broadcasted_iota(jnp.int32, (n, k), 1), 1.0, 0.0)
     one = lax.dot_general(
-        jnp.sum(tot, axis=0, keepdims=True) + jnp.zeros((V, n), F32), pick, (((1,), (0,)), ((), ())),
+        tot + jnp.zeros((V, n), F32), pick, (((1,), (0,)), ((), ())),
         precision=lax.Precision.HIGHEST, preferred_element_type=F32,
     )
     o_gain[...] = one[0:1, :]
 
 
 def semaphores(d):
-    half, far = d.S // 2, d.F // 2 - 1
-    one = (d.F - 1) + 2 * (2 * far + 1) + d.F + 2 * (2 * far) + 2 + 2 * (6 * far) + (d.F - 1) + (2 * d.F - 1)
-    one += 2 * 2 + 1 + d.NB
-    return one + 5 * 2 * half, one + 5 * (half + 1) + 16
+    far = d.F // 2 - 1
+    one = (d.F - 1) + 2 * (2 * far + 1) + d.F + 2 * (2 * far) + 2 + 2 * (6 * far) + 2 * (2 * far + 1) + d.F
+    one += 2 * 2 + 1 + d.NB + 1
+    return one + 7 * d.S, one + 7 * (d.S - 1) + 17
 
 
 def vm(*shape, dtype=F32):
@@ -909,11 +1036,14 @@
     DS, CS, W, W2 = D // S, CL // S, R + 2 * N, 2 * LN
     TP = T + 2 * HG * V
     rt = BF16 if CS >= 16 else F32
-    half = S // 2
+    half, most = CL // 2, CL // LN * 3 // 4 * LN or CL // 2
+    two = lambda name, shape, t: {name + k: (shape, t) for k in "ab"}
     outs = dict(
-        o_gn=((d.NAT, D), BF16), outr=((F, d.tok, D), BF16), gain=((1, D), F32),
-        o_wx=((half, F, DS // F, CL), BF16), o_wg=((half, F, DS // F, CL), BF16),
-        o_out=((half, CS, D), rt), o_small=((half, CS, W2), rt), o_gain=((half, F, V, DS), F32),
+        o_gn=((F // 2 + 1, d.tok, D), BF16), o_gnh=((F, TAIL, D), BF16),
+        outr=((F // 2 + 1, d.tok, D), BF16), gain=((1, D), F32),
+        o_wxa=((2, F, DS // F, most), BF16), o_wxb=((2, F, DS // F, CL - most), BF16),
+        **two("o_wg", (2, F, DS // F, half), BF16),
+        **two("o_out", (2, CS, D // 2), rt), o_small=((2, CS, W2), rt), o_gain=((S * F, 1, DS), F32),
     )
     small_t = T <= 512
     EP = N // d.H * V
@@ -934,12 +1064,16 @@
         gated=((d.TE, CL), BF16), ggate=((d.NAT, CL), BF16), gatn=((T, CL), BF16),
         gx=((T, LN), BF16), gxn=((T, LN), BF16), gxr=((F // 2 - 1, T, LN), BF16), rowsum=((LN, CL), F32),
 
-        giwg=((2, half, F, DS // F, CL), BF16), giwg_n=((half, F, DS // F, CL), BF16),
-        giwx=((2, half, F, DS // F, CL), BF16), giwx_n=((half, F, DS // F, CL), BF16),
-        gow=((2, half, CS, D), rt), gow_n=((half, CS, D), rt),
-        small=((2, half, CS, W2), rt), small_n=((half, CS, W2), rt),
-        gg8=((2, half, V, DS), F32), gg8_n=((half, V, DS), F32),
+        small=((S, CS, W2), rt), small_n=((S - 2, CS, W2), rt),
+        gg8=((S, 1, DS), F32),
     )
+    for name, wide in (("giwg", half), ("giwx", most)):
+        for t, n in (("a", wide), ("b", CL - wide)):
+            scratch[name + t] = ((S, F, DS // F, n), BF16)
+            scratch[name + t + "n"] = ((S - 2, F, DS // F, n), BF16)
+    for t in "ab":
+        scratch["gow" + t] = ((S, CS, D // 2), rt)
+        scratch["gow" + t + "n"] = ((S - 2, CS, D // 2), rt)
     names = list(ins) + list(outs) + list(scratch) + ["ssem", "rsem"]
     sends, gets = semaphores(d)
     res = pl.pallas_call(
@@ -958,8 +1092,8 @@
     o = dict(zip(outs, res))
     fin = kernel(
         functools.partial(close, d),
-        (o["o_gn"], o["outr"], hidden[0], cotangent[0], o["gain"], o["o_wx"], o["o_wg"], o["o_out"],
-         o["o_small"], o["o_gain"]),
+        (o["o_gn"], o["o_gnh"], o["outr"], hidden[0], cotangent[0], o["gain"])
+        + tuple(o[k] for k in ("o_wxa", "o_wxb", "o_wga", "o_wgb", "o_outa", "o_outb", "o_small", "o_gain")),
         [((1, d.tok, D), BF16), ((1, d.tok, D), F32), ((1, DS // F), F32), ((DS // F, 2 * d.DI), F32),
          ((d.K, CS), F32), ((1, CS), F32), ((1, CS), F32), ((1, CS), F32), ((CS, W), F32), ((CS, R), F32),
          ((N, CS), F32), ((CS, D), F32)],

time: 133 us -> 120 us (0.902)
  Pallas kernels: 132 us -> 119 us
    pallas_call x1, Pallas kernels: 128 us -> 115 us  [per_device(): pl.pallas_call(functools.partial(layer, d, names), out_shape=[jax.ShapeDt...]
where the time goes in v4:
time: 120 us
  Pallas kernels  119 us (99%)
    pallas_call x1, Pallas kernels, per_device(): pl.pallas_call(functools.partial(layer, d, names), out_shape=[jax.ShapeDt...  115 us
    pallas_call x1, Pallas kernels, kernel(): pl.pallas_call(body, out_shape=[jax.ShapeDtypeStruct(s, t) for s, t in ou...  4.09 us

profile of v4, /device:TPU:0, one launch (start us, length us, event | category | flops | bytes accessed | tf_op | source)
XLA Modules:
  0.0 119.7 jit_solution(14972595733394094692)
XLA Ops:
  0.6 114.8 %shard_map.220 = (bf16[3,128,1024]{2,1,0:T(8,128)(2,1)}, bf16[4,16,1024]{2,1,0:T(8,128)(2,1)}, bf16[3,128,1024]{2,1,0:T(8,128)(2,1)}, f32[1,1024]{1,0:T(1,128)},...) custom-call(bf16[128,1024]{1,0:T(8,128)(2,1)} %bitcast.12, ...), custom_call_target="tpu_custom_call" | custom-call | tf_op jit(solution)/shard_map/pallas_call | solution.py:1079
  115.5 4.1 %shard_map.221 = (bf16[1,128,1024]{2,1,0:T(8,128)(2,1)}, f32[1,128,1024]{2,1,0:T(8,128)}, f32[1,32]{1,0:T(1,128)}, f32[32,4096]{1,0:T(8,128)}, f32[4,64]{1,0:T(4...) custom-call(bf16[3,128,1024]{2,1,0:T(8,128)(2,1)} %get-tuple-element, ...), custom_call_target="tpu_custom_call" | custom-call | tf_op jit(solution)/shard_map/pallas_call | solution.py:46

commit v5 on v4

--- a/solution.py
+++ b/solution.py
@@ -475,25 +475,36 @@
             r.inp[rows, lane(j)] = (acc * sigmoid(acc)).astype(BF16)
         return 0
 
-    lax.fori_loop(0, T // 64, conv, 0)
     own[6].wait()
     W = d.R + 2 * N
-    r.xd[:, 0:W] = dot(r.inp[...], r.xp[...], 1, 1).astype(BF16)
-    xd_near = net.send(r.xd, r.xdn, ms, core)
-
-    def chips(src, near_copy, near, far):
+    bands = [pl.ds(0, T // 2), pl.ds(T // 2, T // 2)]
+    beside = lambda src, dst, band: net.send(src.at[band], dst.at[band], ms, core)
+    xd_near = []
+    for i, band in enumerate(bands):
+        lax.fori_loop(i * T // 128, (i + 1) * T // 128, conv, 0)
+        r.xd[band, 0:W] = dot(r.inp[band, :], r.xp[...], 1, 1).astype(BF16)
+        if i == 0:
+            xd_near.append(beside(r.xd, r.xdn, band))
+    xd_near.append(beside(r.xd, r.xdn, bands[1]))
+
+    def chips(src, near_copy, near, far, band):
         near_copy.wait()
-        src[...] = (src[...].astype(F32) + near[...].astype(F32)).astype(BF16)
-        return net.batch([(src, far.at[k - 1], *net.at(0, 2 * k)) for k in range(1, F // 2)], far)
-
-    def chips_total(src, batch, far):
-        batch.wait()
+        rows = src.at[band]
+        rows[...] = (rows[...].astype(F32) + near[band, :].astype(F32)).astype(BF16)
+        return net.batch(
+            [(rows, far.at[k - 1, band], *net.at(0, 2 * k)) for k in range(1, F // 2)],
+            far.at[:, band],
+        )
+
+    def chips_total(src, batches, far):
+        for c in batches:
+            c.wait()
         tot = src[:, 0:W].astype(F32)
         for k in range(F // 2 - 1):
             tot = tot + far[k, :, 0:W].astype(F32)
         return tot
 
-    xd_far = chips(r.xd, xd_near, r.xdn, r.xdr)
+    xd_far = [chips(r.xd, c, r.xdn, r.xdr, band) for c, band in zip(xd_near, bands)]
     relay_rows(r.cot, c_direct, c_beside)
     wg_near = w_relay(1, wg_far)
     perm = to_scan(d, 0)
@@ -803,25 +814,24 @@
         gating(j)
         if (j + 1) * LN == cut:
             sum_g = [gate_grads("a", slice(0, cut))]
-        if j == NB - 2:
-            backward(0)
-    late = list(range(1, NB))
+    level = S // 2
 
     sum_g.append(gate_grads("b", slice(cut, CL)))
-    for j in range(NB):
-        both_halves(put, "gow", j * LN, dot(r.gated[0:T, lane(j)], r.cot[...], 0, 0))
+    for c in range(0, CL, 256):
+        both_halves(put, "gow", c, dot(r.gated[0:T, c : c + 256], r.cot[...], 0, 0))
     r.gated[0:T, :] = dot(back0, r.gated[0:T, :]).astype(BF16)
     for c in range(0, D, 256):
         r.cot[:, c : c + 256] = dot(r.gated[0:T, :], r.ow[:, c : c + 256]).astype(BF16)
     outs = Rows(net, core, r.cot, r.hid, r.outr)
-    for i, j in enumerate(late):
+    for j in range(NB):
         backward(j)
-        if i == 0:
+        if j == 0:
             outs.cross()
             sum_o = sum_pair("gow", "o_out", False)
-        if j == NB - 2:
-            step(sum_g, S // 2)
-    step(sum_o, S // 4)
+        if j == 1:
+            step(sum_g, level)
+    step(sum_g, S - 2 - level)
+    step(sum_o, level)
     def finish(i, acc):
         rows = pl.ds(pl.multiple_of(i * 64, 64), 64)
         out = []
@@ -830,8 +840,9 @@
             z = r.dtpre[rows, lane(j)]
             gu = r.gsc[rows, lane(j)]
             gt = r.y_s[rows, lane(j)] * (1.0 / LOG2E) + gu * x
-            dt = jnp.maximum(z, 0.0) + jnp.log1p(jnp.exp(-jnp.abs(z)))
-            gz = gt * sigmoid(z)
+            e = jnp.exp(-jnp.abs(z))
+            dt = jnp.maximum(z, 0.0) + jnp.log1p(e)
+            gz = gt * (jnp.where(z >= 0.0, 1.0, e) / (1.0 + e))
             r.ggate[rows, lane(j)] = gz.astype(BF16)
             r.gsc[rows, lane(j)] = gu * dt + r.gy[rows, lane(j)] * r.cp[6:7, lane(j)]
             out.append(acc[j] + jnp.sum(gz.reshape(8, V, LN), axis=0))
@@ -840,23 +851,22 @@
     db = lax.fori_loop(0, T // 64, finish, tuple(jnp.zeros((V, LN), F32) for _ in range(NB)))
     for j in range(NB):
         r.rowsum[5:6, lane(j)] = jnp.sum(db[j], axis=0, keepdims=True)
-    r.gx[:, 0 : d.R] = dot(r.ggate[0:T, :], r.wdt[...], 1, 1).astype(BF16)
-    acc = jnp.zeros((T, 2 * N), F32)
-    for n in range(0, 2 * N, 4):
-        row = lax.div(lax.broadcasted_iota(jnp.int32, (4 * LN, 2 * N), 0), LN) + n
-        col = lax.broadcasted_iota(jnp.int32, (4 * LN, 2 * N), 1)
-        pick = jnp.where(row == col, 1.0, 0.0).astype(BF16)
-        acc = acc + dot(r.x_s[:, n * LN : (n + 4) * LN].astype(BF16), pick)
-    r.gx[:, d.R : W] = acc.astype(BF16)
-    gx_near = net.send(r.gx, r.gxn, ms, core)
-    gx_far = chips(r.gx, gx_near, r.gxn, r.gxr)
-
-    step(sum_g, S - 2 - S // 2)
-    step(sum_o, S // 2 - S // 4)
+    gx_near = []
+    for band in bands:
+        r.gx[band, 0 : d.R] = dot(r.ggate[band, :], r.wdt[...], 1, 1).astype(BF16)
+        acc = jnp.zeros((T // 2, 2 * N), F32)
+        for n in range(0, 2 * N, 4):
+            row = lax.div(lax.broadcasted_iota(jnp.int32, (4 * LN, 2 * N), 0), LN) + n
+            col = lax.broadcasted_iota(jnp.int32, (4 * LN, 2 * N), 1)
+            pick = jnp.where(row == col, 1.0, 0.0).astype(BF16)
+            acc = acc + dot(r.x_s[band, n * LN : (n + 4) * LN].astype(BF16), pick)
+        r.gx[band, d.R : W] = acc.astype(BF16)
+        gx_near.append(beside(r.gx, r.gxn, band))
+    gx_far = [chips(r.gx, c, r.gxn, r.gxr, band) for c, band in zip(gx_near, bands)]
     gwdt = dot(r.ggate[0:T, :], r.xd[:, 0 : d.R], 0, 0)
 
     gxd = chips_total(r.gx, gx_far, r.gxr).astype(BF16)
-    step(sum_o, S - 2 - S // 2)
+    step(sum_o, S - 2 - level)
     pad = HG * V
     r.gg[0:pad, :] = jnp.zeros((pad, CL), F32)
     r.gg[pad + T :, :] = jnp.zeros((pad, CL), F32)
@@ -905,9 +915,14 @@
 
     lax.fori_loop(0, d.TE // 32, gather_taps, 0)
     r.ggate[...] = dot(from_scan(d, HG), r.gated[...]).astype(BF16)
-    for c in range(0, D, LN):
-        both_halves(put_split, "giwx", c, dot(r.normed[:, c : c + LN], r.ggate[...], 0, 0))
-    sum_x = sum_pair("giwx", "o_wx", True)
+    sum_x, first = [], 0
+    for t in "ab":
+        part = getattr(r, "giwx" + t)
+        cols = slice(first, first + part.shape[-1])
+        first = cols.stop
+        for c in range(0, D, 256):
+            put_split(part, c, dot(r.normed[:, c : c + 256], r.ggate[:, cols], 0, 0))
+        sum_x.append(start_sum("giwx", "o_wx", t, True))
     r.y_s[0:CL, 0:LN] = r.rowsum[...].T
     r.y_s[0:CL, LN : LN + W] = dot(r.inp[...], gxd, 0, 0)
     r.y_s[0:CL, LN + W : 2 * LN] = jnp.zeros((CL, LN - W), F32)
@@ -1014,7 +1029,7 @@
 def semaphores(d):
     far = d.F // 2 - 1
     one = (d.F - 1) + 2 * (2 * far + 1) + d.F + 2 * (2 * far) + 2 + 2 * (6 * far) + 2 * (2 * far + 1) + d.F
-    one += 2 * 2 + 1 + d.NB + 1
+    one += 2 * 4 + 1 + d.NB + 1
     return one + 7 * d.S, one + 7 * (d.S - 1) + 17
 
 

time: 120 us -> 117 us (0.975)
  Pallas kernels: 119 us -> 116 us
    pallas_call x1, Pallas kernels: 115 us -> 112 us  [per_device(): pl.pallas_call(functools.partial(layer, d, names), out_shape=[jax.ShapeDt...]
where the time goes in v5:
time: 117 us
  Pallas kernels  116 us (99%)
    pallas_call x1, Pallas kernels, per_device(): pl.pallas_call(functools.partial(layer, d, names), out_shape=[jax.ShapeDt...  112 us
    pallas_call x1, Pallas kernels, kernel(): pl.pallas_call(body, out_shape=[jax.ShapeDtypeStruct(s, t) for s, t in ou...  4.09 us

profile of v5, /device:TPU:0, one launch (start us, length us, event | category | flops | bytes accessed | tf_op | source)
XLA Modules:
  0.0 117.0 jit_solution(9554065371680567349)
XLA Ops:
  0.6 112.1 %shard_map.220 = (bf16[3,128,1024]{2,1,0:T(8,128)(2,1)}, bf16[4,16,1024]{2,1,0:T(8,128)(2,1)}, bf16[3,128,1024]{2,1,0:T(8,128)(2,1)}, f32[1,1024]{1,0:T(1,128)},...) custom-call(bf16[128,1024]{1,0:T(8,128)(2,1)} %bitcast.12, ...), custom_call_target="tpu_custom_call" | custom-call | tf_op jit(solution)/shard_map/pallas_call | solution.py:1094
  112.8 4.1 %shard_map.221 = (bf16[1,128,1024]{2,1,0:T(8,128)(2,1)}, f32[1,128,1024]{2,1,0:T(8,128)}, f32[1,32]{1,0:T(1,128)}, f32[32,4096]{1,0:T(8,128)}, f32[4,64]{1,0:T(4...) custom-call(bf16[3,128,1024]{2,1,0:T(8,128)(2,1)} %get-tuple-element, ...), custom_call_target="tpu_custom_call" | custom-call | tf_op jit(solution)/shard_map/pallas_call | solution.py:46

commit v6 on v5

--- a/solution.py
+++ b/solution.py
@@ -946,11 +946,28 @@
     for s in range(S):
         r.gg8[s] = gtot[:, s * n : (s + 1) * n]
     gns = Rows(net, core, r.hid, r.m_s.at[0, :, pl.ds(0, D)], r.o_gn)
-    for k in range(F):
-        ps, pf = net.at(-1, k)
-        net.send(r.hid.at[pl.ds(T + pf * TAIL, TAIL)], r.o_gnh.at[mf], ps, pf)
+    halo_rows = lambda f: r.hid.at[pl.ds(T + f * TAIL, TAIL)]
+    halo_near = net.batch(
+        [
+            (halo_rows(lax.rem(core + 2 * k, F)), r.halo_n.at[k], ms, core)
+            for k in range(F // 2)
+        ],
+        r.halo_n,
+    )
+
+    def halo_cross():
+        halo_near.wait()
+        out = []
+        for k in range(F // 2):
+            f = lax.rem(mf + 2 * k, F)
+            here = halo_rows(f)
+            here[...] = (here[...].astype(F32) + r.halo_n[k].astype(F32)).astype(BF16)
+            out.append((here, r.o_gnh.at[k], lax.rem(ms + S - 1, S), f))
+        net.batch(out, r.o_gnh)
+
     step(sum_x, 2)
     gns.cross()
+    halo_cross()
     step([sum_s], 2)
 
     i, j = net.pair()
@@ -987,8 +1004,8 @@
             g = g + gn[k, rows, :].astype(F32)
             o = o + outr[k, rows, :].astype(F32)
         late = jnp.zeros((TAIL, D), F32)
-        for f in range(F):
-            late = late + gnh[f].astype(F32)
+        for k in range(gnh.shape[0]):
+            late = late + gnh[k].astype(F32)
         g = g + jnp.where(i == tok // 16 - 1, late, 0.0)
         inv = lax.rsqrt(jnp.mean(h * h, axis=-1, keepdims=True) + EPS)
         g2 = g * gain[...]
@@ -1028,7 +1045,7 @@
 
 def semaphores(d):
     far = d.F // 2 - 1
-    one = (d.F - 1) + 2 * (2 * far + 1) + d.F + 2 * (2 * far) + 2 + 2 * (6 * far) + 2 * (2 * far + 1) + d.F
+    one = (d.F - 1) + 2 * (2 * far + 1) + d.F + 2 * (2 * far) + 2 + 2 * (6 * far) + 2 * (2 * far + 1) + 2
     one += 2 * 4 + 1 + d.NB + 1
     return one + 7 * d.S, one + 7 * (d.S - 1) + 17
 
@@ -1054,7 +1071,7 @@
     half, most = CL // 2, CL // LN * 3 // 4 * LN or CL // 2
     two = lambda name, shape, t: {name + k: (shape, t) for k in "ab"}
     outs = dict(
-        o_gn=((F // 2 + 1, d.tok, D), BF16), o_gnh=((F, TAIL, D), BF16),
+        o_gn=((F // 2 + 1, d.tok, D), BF16), o_gnh=((F // 2, TAIL, D), BF16),
         outr=((F // 2 + 1, d.tok, D), BF16), gain=((1, D), F32),
         o_wxa=((2, F, DS // F, most), BF16), o_wxb=((2, F, DS // F, CL - most), BF16),
         **two("o_wg", (2, F, DS // F, half), BF16),
@@ -1077,7 +1094,7 @@
         start=((2, N * V, CL), F32), m_s=((NB, T, N * LN), BF16), y_s=((T, CL), F32),
         gsc=((T, CL), F32), x_s=((T, 2 * N * LN), F32 if small_t else BF16),
         gated=((d.TE, CL), BF16), ggate=((d.NAT, CL), BF16), gatn=((T, CL), BF16),
-        gx=((T, LN), BF16), gxn=((T, LN), BF16), gxr=((F // 2 - 1, T, LN), BF16), rowsum=((LN, CL), F32),
+        gx=((T, LN), BF16), gxn=((T, LN), BF16), gxr=((F // 2 - 1, T, LN), BF16), rowsum=((LN, CL), F32), halo_n=((F // 2, TAIL, D), BF16),
 
         small=((S, CS, W2), rt), small_n=((S - 2, CS, W2), rt),
         gg8=((S, 1, DS), F32),

time: 117 us -> 116 us (level); the launches traced: 117 us -> 115 us
  Pallas kernels: 116 us -> 114 us
    pallas_call x1, Pallas kernels: 112 us -> 110 us  [per_device(): pl.pallas_call(functools.partial(layer, d, names), out_shape=[jax.ShapeDt...]
where the time goes in v6:
time: 116 us; the launch traced here: 115 us
  Pallas kernels  114 us (98%)
    pallas_call x1, Pallas kernels, per_device(): pl.pallas_call(functools.partial(layer, d, names), out_shape=[jax.ShapeDt...  110 us
    pallas_call x1, Pallas kernels, kernel(): pl.pallas_call(body, out_shape=[jax.ShapeDtypeStruct(s, t) for s, t in ou...  4 us

profile of v6, /device:TPU:0, one launch (start us, length us, event | category | flops | bytes accessed | tf_op | source)
XLA Modules:
  0.0 114.7 jit_solution(7937272941432464962)
XLA Ops:
  0.6 109.9 %shard_map.220 = (bf16[3,128,1024]{2,1,0:T(8,128)(2,1)}, bf16[2,16,1024]{2,1,0:T(8,128)(2,1)}, bf16[3,128,1024]{2,1,0:T(8,128)(2,1)}, f32[1,1024]{1,0:T(1,128)},...) custom-call(bf16[128,1024]{1,0:T(8,128)(2,1)} %bitcast.12, ...), custom_call_target="tpu_custom_call" | custom-call | tf_op jit(solution)/shard_map/pallas_call | solution.py:1111
  110.6 4.0 %shard_map.221 = (bf16[1,128,1024]{2,1,0:T(8,128)(2,1)}, f32[1,128,1024]{2,1,0:T(8,128)}, f32[1,32]{1,0:T(1,128)}, f32[32,4096]{1,0:T(8,128)}, f32[4,64]{1,0:T(4...) custom-call(bf16[3,128,1024]{2,1,0:T(8,128)(2,1)} %get-tuple-element, ...), custom_call_target="tpu_custom_call" | custom-call | tf_op jit(solution)/shard_map/pallas_call | solution.py:46
